TPU v7x, 512 devices: a whole 4x4x16 slice. The times are simulated.
512 devices in a mesh: dp: 4 (over z_hi, core), row: 32 (over y, z_lo), chan: 4 (over x).
Axes of the slice: x: 4, y: 4, z: 16 (z_hi: 2, z_lo: 8; z = z_hi * 8 + z_lo), core: 2. Of those that a mesh axis runs over, the one named last changes fastest.
Arguments:
- pair: bfloat16 [1024, 256, 128], P(('dp', 'row', 'chan')), parts along dimension 0, may hold values from -256 to 256
- chain: int32 [1024], P('dp'), parts along dimension 0, may hold values from 0 to 4, never falling along the last dimension, each value on 1 to 85 neighbouring positions
- targets: int32 [1024, 256], P(('dp', 'row', 'chan')), parts along dimension 0, may hold values from 0 to 63
- pair_mask: int32 [1024, 256], P(('dp', 'row', 'chan')), parts along dimension 0, may hold values 0 or 1
- ln_in_gain: float32 [128], replicated, may hold values from 0.5 to 1.5
- ln_in_bias: float32 [128], replicated, may hold values from -3 to 3
- in_weight: bfloat16 [128, 512], replicated, may hold values from -0.5 to 0.5
- out_gate_weight: bfloat16 [128, 128], replicated, may hold values from -0.5 to 0.5
- ln_out_gain: float32 [128], replicated, may hold values from 0.5 to 1.5
- ln_out_bias: float32 [128], replicated, may hold values from -3 to 3
- out_weight: bfloat16 [128, 128], replicated, may hold values from -0.5 to 0.5
- dist_weight: bfloat16 [512, 64], P('dp'), parts along dimension 0, may hold values from -1 to 1
- dist_bias: float32 [64], replicated, may hold values from -4 to 4
Outputs:
- pair_out: bfloat16 [1024, 256, 128], P(('dp', 'row', 'chan')), parts along dimension 0
- grad_pair: float32 [1024, 256, 128], P(('dp', 'row', 'chan')), parts along dimension 0
- grad_weight: float32 [512, 64], P('dp'), parts along dimension 0
- loss: float32 [4], P('dp'), parts along dimension 0
There are 4 independent parts, one for each index of `dp`. A program takes and returns all parts, laid end to end along the dimension named above; an argument that names none is the same for every part. Nothing has to cross between parts.
Inputs may be any that keep to these rules, and one draw needn't show every extreme that they name: chain ids never fall along the tokens.
All inputs are finite; a program needn't handle non-finite values. No bound on the sum of `pair_mask` on one device may be relied on, other than what follows from the above.
Results may differ from a plain program's by a relative error of at most 0.007.
Values may be sent and summed in bfloat16 or wider, within the bound.
No kernel may reach another device: no remote copies, remote signals or barrier semaphores. Data moves between devices by JAX's collectives and lax.ppermute only.
A program may use at most 64 MiB of HBM per device.

v0:
```python
import jax
import jax.numpy as jnp
from jax import lax
from jax.sharding import PartitionSpec as P


def layer_norm(values, gain, bias, axis):
    center = jnp.mean(values, axis=axis, keepdims=True)
    spread = jnp.mean(jnp.square(values - center), axis=axis, keepdims=True)
    return (values - center) * lax.rsqrt(spread + 1e-05) * gain + bias


def on_device(
    pair,
    chain,
    targets,
    pair_mask,
    ln_in_gain,
    ln_in_bias,
    in_weight,
    out_gate_weight,
    ln_out_gain,
    ln_out_bias,
    out_weight,
    dist_weight,
    dist_bias,
):
    rows_dev = pair.shape[0]
    tokens = pair.shape[1]
    width = out_weight.shape[0]
    bins = dist_weight.shape[1]
    pair_full = pair.astype(jnp.float32)
    normed = layer_norm(pair_full, ln_in_gain, ln_in_bias, -1).astype(jnp.bfloat16)
    proj = jnp.einsum("ikc,cm->mik", normed, in_weight, preferred_element_type=jnp.float32)
    maskf = pair_mask.astype(jnp.float32)[None, :, :]
    projected = (proj[: 2 * width] * jax.nn.sigmoid(proj[2 * width :]) * maskf).astype(jnp.bfloat16)
    projected = projected.reshape(2, width, rows_dev, tokens)
    grouped = lax.all_to_all(projected, "chan", split_axis=1, concat_axis=2, tiled=True)
    a_rows = grouped[0]
    b_rows = grouped[1]
    products = jnp.einsum(
        "hik,hjk->hij",
        a_rows,
        lax.all_gather(b_rows, "row", axis=1, tiled=True),
        preferred_element_type=jnp.float32,
    )
    hidden_rows = lax.all_to_all(
        products.astype(jnp.bfloat16), "chan", split_axis=1, concat_axis=0, tiled=True
    ).astype(products.dtype)
    hidden_norm = layer_norm(
        hidden_rows, ln_out_gain[:, None, None], ln_out_bias[:, None, None], 0
    ).astype(jnp.bfloat16)
    gating = jax.nn.sigmoid(
        jnp.einsum("ikc,cd->ikd", normed, out_gate_weight, preferred_element_type=jnp.float32)
    )
    update = jnp.einsum("hik,hd->ikd", hidden_norm, out_weight, preferred_element_type=jnp.float32)
    updated = (pair_full + gating * update).astype(jnp.bfloat16)
    q_sent = jnp.einsum("ikc,cb->kib", updated, dist_weight, preferred_element_type=jnp.float32)
    q_back = lax.all_to_all(q_sent, ("row", "chan"), split_axis=0, concat_axis=1, tiled=True)
    logits = jnp.swapaxes(q_sent, 0, 1) + q_back + dist_bias
    log_probs = jax.nn.log_softmax(logits, axis=-1)
    onehot = (targets[:, :, None] == jnp.arange(bins, dtype=jnp.int32)[None, None, :]).astype(
        jnp.float32
    )
    offset = lax.axis_index(("row", "chan")) * rows_dev
    own_chain = lax.dynamic_slice_in_dim(chain, offset, rows_dev)
    weight = pair_mask.astype(jnp.float32) * (
        1.0 + (own_chain[:, None] != chain[None, :]).astype(jnp.float32)
    )
    partial_loss = jnp.sum(weight * -jnp.sum(onehot * log_probs, axis=-1))
    gradient = weight[:, :, None] * (jnp.exp(log_probs) - onehot)
    grad_back = lax.all_to_all(
        jnp.swapaxes(gradient, 0, 1).astype(jnp.bfloat16),
        ("row", "chan"),
        split_axis=0,
        concat_axis=1,
        tiled=True,
    ).astype(jnp.float32)
    grad_sym = gradient + grad_back
    grad_pair = jnp.einsum(
        "ikb,cb->ikc", grad_sym, dist_weight.astype(jnp.float32), precision=lax.Precision.HIGHEST
    )
    partial_weight = jnp.einsum(
        "ikc,ikb->cb", updated.astype(jnp.float32), grad_sym, precision=lax.Precision.HIGHEST
    )
    total_weight, total_loss = lax.psum((partial_weight, partial_loss), ("row", "chan"))
    return (updated, grad_pair, total_weight / tokens, (total_loss / (tokens * tokens)).reshape(1))


def solution(mesh):
    in_specs = (
        P(("dp", "row", "chan"), None, None),
        P("dp"),
        P(("dp", "row", "chan"), None),
        P(("dp", "row", "chan"), None),
        P(),
        P(),
        P(),
        P(),
        P(),
        P(),
        P(),
        P("dp", None),
        P(),
    )
    out_specs = (
        P(("dp", "row", "chan"), None, None),
        P(("dp", "row", "chan"), None, None),
        P("dp", None),
        P("dp"),
    )
    return jax.shard_map(
        on_device, mesh=mesh, in_specs=in_specs, out_specs=out_specs, check_vma=False
    )
```

profile of v0, /device:TPU:0, one launch (start us, length us, event | category | flops | bytes accessed | tf_op | source)
XLA Modules:
  0.0 1342.0 jit_solution(11085372587405195239)
XLA Ops:
  7.2 0.0 copy-start
  7.2 0.0 all-gather.2.cloned.1.call-start
  7.2 1.0 convert_reduce_fusion
  8.3 1.2 fusion.18
  9.4 0.7 convert_element_type.68
  10.1 0.0 copy-done
  10.1 1.3 convolution_bitcast_fusion
  11.4 0.2 fusion.15
  11.6 0.1 reshape.67
  11.7 0.0 copy-start.1
  11.7 0.0 copy-start.8
  11.7 0.0 copy-start.9
  11.7 0.0 copy-start.13
  11.7 0.5 copy.61
  12.2 9.1 all_to_all.51
  21.3 0.1 copy.64
  21.5 0.7 squeeze.7
  22.2 0.0 all-gather.2.cloned.1.call-update
  22.2 0.1 copy.63
  22.3 0.0 copy-start.5
  22.4 0.1 squeeze.6
  22.4 0.0 copy-start.3
  22.4 0.0 copy-start.7
  22.4 212.1 %all-gather.2.cloned.1.call-done = bf16[32,256,256]{2,1,0:T(8,128)(2,1)} async-done(((bf16[32,8,256]{2,1,0:T(8,128)(2,1)}), bf16[32,256,256]{2,1,0:T(8,128)(2,1)}) %all-gather.2.cloned.1.call-update) | async-done | bytes 4194320 | tf_op jit(solution)/shard_map/all_gather | solution.py:44
  234.5 3.4 convolution_convert_fusion
  237.9 0.0 copy-start.6
  237.9 0.7 copy.65
  238.6 4.5 all-to-all-start.1
  243.2 0.0 copy-done.1
  243.2 0.0 copy-done.8
  243.2 0.3 fusion.5
  243.5 5.7 all-to-all-done.1
  249.2 0.1 multiply_reduce_fusion
  249.4 0.1 fusion.25
  249.5 0.0 copy-done.5
  249.5 0.2 fusion.6
  249.7 0.0 copy-start.2
  249.8 0.2 fusion.41
  249.9 0.2 copy.68
  250.1 0.9 reshape.79
  251.0 10.7 all-to-all-start.2
  261.7 0.1 dynamic_slice.3
  261.8 14.8 %all-to-all-done.2 = f32[128,1,256]{2,1,0:T(1,128)S(1)} async-done(((f32[128,1,256]{2,1,0:T(1,128)}), f32[128,1,256]{2,1,0:T(1,128)S(1)}, u32[]{:S(2)}, u32[]{:S(2)}) %all-to-all-start.2) | async-done | bytes 131104 | tf_op jit(solution)/shard_map/all_to_all | solution.py:59
  276.6 0.5 broadcast.72
  277.1 1.0 reduce.2
  278.0 0.2 reshape.80
  278.2 0.2 copy.70
  278.5 0.1 copy.71
  278.6 0.0 copy-done.12
  278.6 0.1 fusion.7
  278.7 0.2 select_reduce_fusion
  278.9 0.7 multiply_reduce_fusion.1
  279.6 0.1 copy.72
  279.8 0.1 reshape.81
  279.9 22.4 %all_to_all.52 = bf16[128,2,128]{2,1,0:T(2,128)(2,1)S(1)} all-to-all(bf16[128,2,128]{2,1,0:T(2,128)(2,1)S(1)} %reshape.81), channel_id=1, replica_groups=mesh['dp'=4,'row'=32,'chan'=4] {'row','chan'}, dimensions={0} | all-to-all | bytes 131072 | tf_op jit(solution)/shard_map/all_to_all | solution.py:72
  302.3 0.1 reshape.82
  302.4 0.1 copy.73
  302.5 0.1 copy.74
  302.6 0.2 copy.75
  302.8 0.1 copy.76
  302.9 0.2 convolution_bitcast_fusion.1
  303.1 1.1 fusion.37
  304.2 1028.5 %all-reduce = (f32[128,64]{0,1:T(8,128)S(1)}, f32[]{:T(128)}) all-reduce(f32[128,64]{0,1:T(8,128)S(1)} %convolution_bitcast_fusion.1, f32[]{:T(128)} %get-tuple-element.6), channel_id=1, replica_groups=mesh['dp'=4,'row'=32,'chan'=4] {'row','chan'}, use_global_device_ids=true, to_apply=%region_6.7 | all-reduce | flops 8193 | bytes 65544 | tf_op jit(solution)/shard_map/psum | solution.py:86
  1332.7 0.6 broadcast_multiply_fusion
  (24 shorter events, 0.2 us)
Async XLA Ops:
  7.2 3.0 copy-start
  7.2 227.4 %all-gather.2.cloned.1.call-start = ((), (), s32[]{:S(2)}) async-start(), calls=%async_computation.4 | async-start | bytes 4325376 | tf_op jit(solution)/shard_map/all_gather | solution.py:44
  11.7 231.5 %copy-start.1 = (bf16[2,256,128]{2,1,0:T(8,128)(2,1)S(1)}, bf16[2,256,128]{2,1,0:T(8,128)(2,1)}, u32[]{:S(2)}) copy-start(bf16[2,256,128]{2,1,0:T(8,128)(2,1)} %param.13) | copy-start | bytes 393220
  11.7 231.5 %copy-start.8 = (f32[128]{0:T(128)S(1)}, f32[128]{0:T(128)}, u32[]{:S(2)}) copy-start(f32[128]{0:T(128)} %param.18) | copy-start | bytes 1540
  11.7 231.5 %copy-start.9 = (f32[128]{0:T(128)S(1)}, f32[128]{0:T(128)}, u32[]{:S(2)}) copy-start(f32[128]{0:T(128)} %param.17) | copy-start | bytes 1540
  11.7 231.5 %copy-start.13 = (bf16[128,128]{1,0:T(8,128)(2,1)S(1)}, bf16[128,128]{1,0:T(8,128)(2,1)}, u32[]{:S(2)}) copy-start(bf16[128,128]{1,0:T(8,128)(2,1)} %param.20) | copy-start | bytes 98308
  22.2 227.2 %copy-start.10 = (f32[128]{0:T(128)S(1)}, f32[128]{0:T(128)}, u32[]{:S(2)}) copy-start(f32[128]{0:T(128)} %param.22) | copy-start | bytes 1540
  22.2 227.2 %copy-start.11 = (f32[128]{0:T(128)S(1)}, f32[128]{0:T(128)}, u32[]{:S(2)}) copy-start(f32[128]{0:T(128)} %param.21) | copy-start | bytes 1540
  22.3 227.1 %copy-start.5 = (bf16[128,128]{1,0:T(8,128)(2,1)S(1)}, bf16[128,128]{1,0:T(8,128)(2,1)}, u32[]{:S(2)}) copy-start(bf16[128,128]{1,0:T(8,128)(2,1)} %param.23) | copy-start | bytes 98308
  22.4 227.3 %copy-start.3 = (bf16[128,64]{0,1:T(8,128)(2,1)S(1)}, bf16[128,64]{0,1:T(8,128)(2,1)}, u32[]{:S(2)}) copy-start(bf16[128,64]{0,1:T(8,128)(2,1)} %param.24) | copy-start | bytes 49156
  22.4 239.3 %copy-start.7 = (s32[256]{0:T(256)S(1)}, s32[256]{0:T(256)}, u32[]{:S(2)}) copy-start(s32[256]{0:T(256)} %param.14) | copy-start | bytes 3076
  237.9 40.7 %copy-start.12 = (f32[64]{0:T(128)S(1)}, f32[64]{0:T(128)}, u32[]{:S(2)}) copy-start(f32[64]{0:T(128)} %param.25) | copy-start | bytes 772
  237.9 40.8 %copy-start.4 = (s32[2,256]{1,0:T(2,128)S(1)}, s32[2,256]{1,0:T(2,128)}, u32[]{:S(2)}) copy-start(s32[2,256]{1,0:T(2,128)} %param.15) | copy-start | bytes 6148
  237.9 41.0 %copy-start.6 = (s32[2,256]{1,0:T(2,128)S(1)}, s32[2,256]{1,0:T(2,128)}, u32[]{:S(2)}) copy-start(s32[2,256]{1,0:T(2,128)} %param.16) | copy-start | bytes 6148
  238.6 10.6 all-to-all-start.1
  249.7 1084.3 %copy-start.2 = (bf16[2,256,128]{2,1,0:T(8,128)(2,1)}, bf16[2,256,128]{2,1,0:T(8,128)(2,1)S(1)}, u32[]{:S(2)}) copy-start(bf16[2,256,128]{2,1,0:T(8,128)(2,1)S(1)} %fusion.6) | copy-start | bytes 393220
  251.0 25.6 %all-to-all-start.2 = ((f32[128,1,256]{2,1,0:T(1,128)}), f32[128,1,256]{2,1,0:T(1,128)S(1)}, u32[]{:S(2)}, u32[]{:S(2)}) async-start(f32[128,1,256]{2,1,0:T(1,128)} %reshape.79), calls=%async_computation.2 | async-start | bytes 262144 | tf_op jit(solution)/shard_map/all_to_all | solution.py:59
Sparse Core Ops, SparseCore 0:
  22.3 212.1 all-gather.1
where the time goes:
time: 1340 us
  blocking collectives  1060 us (79%)
  waiting for transfers between devices  233 us (17%)
  between operations  16.2 us (1%)
  starting transfers between devices  15.2 us (1%)
    psum x1, blocking collectives, on_device(): lax.psum((partial_weight, partial_loss), ('row', 'chan'))  1030 us
    all_gather x1, waiting for transfers between devices, on_device(): lax.all_gather(b_rows, 'row', axis=1, tiled=True)  212 us
  transfers between devices with their start and end apart: 3, of which 3 were waited for; matrix products, arithmetic and copies ran while one was open for 0% of the time, Pallas kernels for 0%

commit v1 on v0

v1 whole, which is shorter than its diff:
```python
import jax
import jax.numpy as jnp
from jax import lax
from jax.sharding import Mesh
from jax.sharding import PartitionSpec as P

EVERY = ("zhi", "core", "y", "zlo", "x")
GROUP = ("y", "zlo", "x")
PLANE = ("y", "x")


def layer_norm(values, gain, bias, axis):
    center = jnp.mean(values, axis=axis, keepdims=True)
    spread = jnp.mean(jnp.square(values - center), axis=axis, keepdims=True)
    return (values - center) * lax.rsqrt(spread + 1e-05) * gain + bias


def group_sum(values, axes, peers):
    copies = jnp.broadcast_to(values[None], (peers,) + values.shape)
    return jnp.sum(lax.all_to_all(copies, axes, 0, 0, tiled=True), axis=0)


def on_device(
    pair,
    chain,
    targets,
    pair_mask,
    ln_in_gain,
    ln_in_bias,
    in_weight,
    out_gate_weight,
    ln_out_gain,
    ln_out_bias,
    out_weight,
    dist_weight,
    dist_bias,
):
    tokens = 256
    bf16, f32 = jnp.bfloat16, jnp.float32
    flat = pair.reshape(512, 128)
    normed = layer_norm(flat.astype(f32), ln_in_gain, ln_in_bias, -1).astype(bf16)
    proj = jnp.einsum("cm,tc->mt", in_weight, normed, preferred_element_type=f32)
    maskf = pair_mask.astype(f32).reshape(1, 512)
    projected = (proj[:256] * jax.nn.sigmoid(proj[256:]) * maskf).astype(bf16)
    pair_part = pair.reshape(2, 128, 2, 128).transpose(1, 2, 0, 3).reshape(128, 4, 128)
    marks = jnp.stack([targets, pair_mask]).reshape(2, 2, 128, 2).transpose(2, 0, 3, 1)
    marks = jnp.pad(marks.reshape(128, 1, 8).astype(bf16), ((0, 0), (0, 3), (0, 120)))
    send = jnp.concatenate(
        [projected[:128].reshape(128, 4, 128), projected[128:].reshape(128, 4, 128), pair_part, marks], axis=1
    )
    got = lax.all_to_all(send, GROUP, 0, 0, tiled=True)
    a = got[:, :4].reshape(256, 256)
    b = got[:, 4:8].reshape(256, 256)
    mixed = jnp.einsum("ik,jk->ij", a, b, preferred_element_type=f32).astype(bf16)
    mirrored = jnp.einsum("jk,ik->ji", b, a, preferred_element_type=f32).astype(bf16)
    send2 = jnp.concatenate(
        [mixed.reshape(128, 4, 128), mirrored.reshape(128, 4, 128)], axis=1
    )
    got2 = lax.all_to_all(send2, GROUP, 0, 0, tiled=True)
    pair_back = got[:, 8:12].reshape(128, 2, 2, 128).transpose(1, 0, 2, 3).reshape(512, 128)
    marks_back = got[:, 12, :8].reshape(128, 2, 2, 2).transpose(1, 2, 0, 3).reshape(2, 512)
    targets_back = marks_back[0].astype(jnp.int32)
    mask_back = marks_back[1].astype(f32)
    both = jnp.concatenate([flat, pair_back], axis=0).astype(f32)
    normed_back = layer_norm(pair_back.astype(f32), ln_in_gain, ln_in_bias, -1).astype(bf16)
    normed_both = jnp.concatenate([normed, normed_back], axis=0)
    gating = jax.nn.sigmoid(jnp.dot(normed_both, out_gate_weight, preferred_element_type=f32))
    hidden = got2.astype(f32)
    hidden_norm = layer_norm(
        hidden, ln_out_gain[:, None, None], ln_out_bias[:, None, None], 0
    ).astype(bf16)
    update = jnp.einsum(
        "ht,hd->td", hidden_norm.reshape(128, 1024), out_weight, preferred_element_type=f32
    )
    updated = (both + gating * update).astype(bf16)
    q = jnp.einsum("cb,tc->bt", dist_weight, updated, preferred_element_type=f32)
    logits = q[:, :512] + q[:, 512:] + dist_bias[:, None]
    log_probs = jax.nn.log_softmax(logits, axis=0)
    bins = jnp.arange(64, dtype=jnp.int32)[:, None]
    onehot = (targets.reshape(1, 512) == bins).astype(f32)
    onehot_back = (targets_back.reshape(1, 512) == bins).astype(f32)
    place = lax.axis_index(GROUP) * 2
    own_chain = lax.dynamic_slice_in_dim(chain, place, 2)
    factor = (1.0 + (own_chain[:, None] != chain[None, :]).astype(f32)).reshape(1, 512)
    weight = maskf * factor
    weight_back = mask_back.reshape(1, 512) * factor
    partial_loss = jnp.sum(weight * -jnp.sum(onehot * log_probs, axis=0, keepdims=True))
    probs = jnp.exp(log_probs)
    grad_sym = weight * (probs - onehot) + weight_back * (probs - onehot_back)
    own = updated[:512]
    grad_weight = jnp.einsum(
        "bt,tc->bc", grad_sym, own.astype(f32), precision=lax.Precision.HIGHEST
    )
    grad_pair = jnp.einsum(
        "bt,cb->tc", grad_sym, dist_weight.astype(f32), precision=lax.Precision.HIGHEST
    )
    loss_row = jnp.pad(jnp.broadcast_to(partial_loss, (1, 128)), ((0, 7), (0, 0)))
    total = jnp.concatenate([grad_weight, loss_row], axis=0)
    total = group_sum(total, PLANE, 16)
    total = group_sum(total, "zlo", 8)
    return (
        own.reshape(2, 256, 128),
        grad_pair.reshape(2, 256, 128),
        jnp.swapaxes(total[:64], 0, 1) / tokens,
        (total[64, :1] / (tokens * tokens)).reshape(1),
    )


def solution(mesh):
    fine = Mesh(mesh.devices.reshape(2, 2, 4, 8, 4), EVERY)
    part = ("zhi", "core")
    in_specs = (
        P(EVERY, None, None),
        P(part),
        P(EVERY, None),
        P(EVERY, None),
        P(),
        P(),
        P(),
        P(),
        P(),
        P(),
        P(),
        P(part, None),
        P(),
    )
    out_specs = (
        P(EVERY, None, None),
        P(EVERY, None, None),
        P(part, None),
        P(part),
    )
    return jax.shard_map(
        on_device, mesh=fine, in_specs=in_specs, out_specs=out_specs, check_vma=False
    )
```

time: 1340 us -> 134 us (0.10)
  the two profiles are of different devices: /device:TPU:0 before, /device:TPU:32 now
where the time goes in v1:
time: 134 us; the launch traced here: 133 us
  waiting for transfers between devices  60.6 us (45%)
  starting transfers between devices  34.4 us (26%)
  blocking collectives  14.1 us (11%)
  local copies, waits for them, and re-layouts  10.6 us (8%)
  other arithmetic  7.49 us (6%)
  matrix products  2.83 us (2%)
  between operations  2.8 us (2%)
    all_to_all x1, waiting for transfers between devices, on_device(): got = lax.all_to_all(send, GROUP, 0, 0, tiled=True)  28.9 us
    all_to_all x1, starting transfers between devices, on_device(): got = lax.all_to_all(send, GROUP, 0, 0, tiled=True)  19.1 us
    all_to_all x1, waiting for transfers between devices, on_device(): got2 = lax.all_to_all(send2, GROUP, 0, 0, tiled=True)  17.4 us
    all_to_all x1, waiting for transfers between devices, group_sum(): return jnp.sum(lax.all_to_all(copies, axes, 0, 0, tiled=True), axis=0)  14.3 us
    all_to_all x1, blocking collectives, group_sum(): return jnp.sum(lax.all_to_all(copies, axes, 0, 0, tiled=True), axis=0)  14.1 us
    all_to_all x1, starting transfers between devices, on_device(): got2 = lax.all_to_all(send2, GROUP, 0, 0, tiled=True)  9.04 us
    all_to_all x1, starting transfers between devices, group_sum(): return jnp.sum(lax.all_to_all(copies, axes, 0, 0, tiled=True), axis=0)  6.32 us
    unnamed x32, local copies, waits for them, and re-layouts  5.29 us
  transfers between devices with their start and end apart: 3, of which 3 were waited for; matrix products, arithmetic and copies ran while one was open for 3% of the time, Pallas kernels for 0%

profile of v1, /device:TPU:32, one launch (start us, length us, event | category | flops | bytes accessed | tf_op | source)
XLA Modules:
  0.0 132.8 jit_solution(12256385586263793782)
XLA Ops:
  0.7 0.7 convert.10
  1.4 1.0 convert_reduce_fusion.2
  2.4 0.2 fusion.20
  2.7 0.7 copy-done.5
  3.4 0.2 stack.9
  3.6 0.1 copy.41
  3.7 0.2 stack.10
  3.9 0.1 copy.42
  4.0 0.1 copy.40
  4.1 0.6 copy-done.6
  4.8 0.0 copy-done.7
  4.8 0.2 add_convert_fusion.1
  5.0 0.3 convolution_bitcast_fusion
  5.3 0.2 fusion.18
  5.5 1.2 copy.44
  6.7 19.1 %all-to-all-start = ((bf16[128,16,128]{2,1,0:T(8,128)(2,1)}), bf16[128,16,128]{2,1,0:T(8,128)(2,1)S(1)}, u32[]{:S(2)}, u32[]{:S(2)}) async-start(bf16[128,16,128]{2,1,0:T(8,128)(2,1)} %copy.44), calls=%async_computation | async-start | bytes 1048576 | tf_op jit(solution)/shard_map/all_to_all | solution.py:51
  25.8 0.7 copy-done.4
  26.5 0.7 copy-done.8
  27.2 0.1 dynamic_slice.3
  27.2 28.9 %all-to-all-done = bf16[128,16,128]{2,1,0:T(8,128)(2,1)S(1)} async-done(((bf16[128,16,128]{2,1,0:T(8,128)(2,1)}), bf16[128,16,128]{2,1,0:T(8,128)(2,1)S(1)}, u32[]{:S(2)}, u32[]{:S(2)}) %all-to-all-start) | async-done | bytes 524320 | tf_op jit(solution)/shard_map/all_to_all | solution.py:51
  56.2 0.1 fusion.42
  56.3 0.1 reshape.241
  56.4 0.1 reshape.242
  56.5 0.2 convolution_convert_fusion
  56.7 0.2 convolution_convert_fusion.1
  57.0 0.3 convert_reduce_fusion.1
  57.3 0.1 copy.45
  57.4 0.1 slice.72
  57.5 0.1 copy.49
  57.6 0.2 copy.47
  57.7 0.1 reshape.248
  58.0 0.8 pad_maximum_fusion
  58.8 9.0 %all-to-all-start.1 = ((bf16[128,8,128]{2,1,0:T(8,128)(2,1)}), bf16[128,8,128]{2,1,0:T(8,128)(2,1)S(1)}, u32[]{:S(2)}, u32[]{:S(2)}) async-start(bf16[128,8,128]{2,1,0:T(8,128)(2,1)} %pad_maximum_fusion), calls=%async_computation.1 | async-start | bytes 524288 | tf_op jit(solution)/shard_map/all_to_all | solution.py:59
  67.8 0.1 copy.48
  68.0 0.1 reshape.249
  68.1 0.1 div.46
  68.3 0.6 fusion.22
  69.0 0.1 rsqrt.33
  69.1 0.2 add_convert_fusion
  69.3 0.5 copy-done.12
  69.9 0.3 fusion.2
  70.2 17.4 %all-to-all-done.1 = bf16[128,8,128]{2,1,0:T(8,128)(2,1)S(1)} async-done(((bf16[128,8,128]{2,1,0:T(8,128)(2,1)}), bf16[128,8,128]{2,1,0:T(8,128)(2,1)S(1)}, u32[]{:S(2)}, u32[]{:S(2)}) %all-to-all-start.1) | async-done | bytes 262176 | tf_op jit(solution)/shard_map/all_to_all | solution.py:59
  87.5 0.1 convert_reduce_fusion
  87.7 0.1 fusion.8
  87.8 0.6 copy-done.10
  88.5 0.3 fusion.11
  88.8 0.4 copy-done.3
  89.2 0.3 fusion.4
  89.5 0.5 copy-done.2
  90.0 0.2 convolution_bitcast_fusion.1
  90.2 0.4 copy-done.9
  90.6 0.1 fusion.40
  90.8 0.7 fusion.36
  91.5 0.7 compare_select_fusion
  92.2 0.3 fusion.29
  92.5 0.1 pad_maximum_fusion.1
  92.6 14.1 %all_to_all.20 = f32[16,72,128]{2,1,0:T(8,128)S(1)} all-to-all(f32[16,72,128]{2,1,0:T(8,128)S(1)} %broadcast_in_dim.9), channel_id=1, replica_groups=mesh['zhi'=2,'core'=2,'y'=4,'zlo'=8,'x'=4] {'y','x'}, dimensions={0} | all-to-all | bytes 1179648 | tf_op jit(solution)/shard_map/all_to_all | solution.py:20
  106.8 0.7 broadcast_in_dim.10
  107.5 6.3 %all-to-all-start.3 = ((f32[8,72,128]{2,1,0:T(8,128)}), f32[8,72,128]{2,1,0:T(8,128)S(1)}, u32[]{:S(2)}, u32[]{:S(2)}) async-start(f32[8,72,128]{2,1,0:T(8,128)} %broadcast_in_dim.10), calls=%async_computation.3 | async-start | bytes 589824 | tf_op jit(solution)/shard_map/all_to_all | solution.py:20
  113.8 0.7 slice.69
  114.5 1.1 fusion.30
  115.6 14.3 %all-to-all-done.3 = f32[8,72,128]{2,1,0:T(8,128)S(1)} async-done(((f32[8,72,128]{2,1,0:T(8,128)}), f32[8,72,128]{2,1,0:T(8,128)S(1)}, u32[]{:S(2)}, u32[]{:S(2)}) %all-to-all-start.3) | async-done | bytes 294944 | tf_op jit(solution)/shard_map/all_to_all | solution.py:20
  129.9 0.5 slice.76
  130.4 0.6 fusion.31
  (44 shorter events, 0.5 us)
Async XLA Ops:
  0.6 4.4 %copy-start = (bf16[128,512]{1,0:T(8,128)(2,1)S(1)}, bf16[128,512]{1,0:T(8,128)(2,1)}, u32[]{:S(2)}) copy-start(bf16[128,512]{1,0:T(8,128)(2,1)} %param.19) | copy-start | bytes 393220
  0.6 1.8 %copy-start.1 = (bf16[2,256,128]{2,1,0:T(8,128)(2,1)S(1)}, bf16[2,256,128]{2,1,0:T(8,128)(2,1)}, u32[]{:S(2)}) copy-start(bf16[2,256,128]{2,1,0:T(8,128)(2,1)} %param.13) | copy-start | bytes 393220
  2.7 0.7 copy-start.5
  4.1 0.7 copy-start.6
  4.1 0.7 copy-start.7
  6.7 49.5 %all-to-all-start = ((bf16[128,16,128]{2,1,0:T(8,128)(2,1)}), bf16[128,16,128]{2,1,0:T(8,128)(2,1)S(1)}, u32[]{:S(2)}, u32[]{:S(2)}) async-start(bf16[128,16,128]{2,1,0:T(8,128)(2,1)} %copy.44), calls=%async_computation | async-start | bytes 1048576 | tf_op jit(solution)/shard_map/all_to_all | solution.py:51
  25.8 0.7 copy-start.4
  26.5 0.7 copy-start.8
  58.8 28.7 %all-to-all-start.1 = ((bf16[128,8,128]{2,1,0:T(8,128)(2,1)}), bf16[128,8,128]{2,1,0:T(8,128)(2,1)S(1)}, u32[]{:S(2)}, u32[]{:S(2)}) async-start(bf16[128,8,128]{2,1,0:T(8,128)(2,1)} %pad_maximum_fusion), calls=%async_computation.1 | async-start | bytes 524288 | tf_op jit(solution)/shard_map/all_to_all | solution.py:59
  69.1 0.8 copy-start.12
  87.8 0.7 copy-start.10
  87.8 0.7 copy-start.11
  88.5 0.8 copy-start.3
  89.2 0.7 copy-start.2
  90.0 0.7 copy-start.9
  107.5 22.4 %all-to-all-start.3 = ((f32[8,72,128]{2,1,0:T(8,128)}), f32[8,72,128]{2,1,0:T(8,128)S(1)}, u32[]{:S(2)}, u32[]{:S(2)}) async-start(f32[8,72,128]{2,1,0:T(8,128)} %broadcast_in_dim.10), calls=%async_computation.3 | async-start | bytes 589824 | tf_op jit(solution)/shard_map/all_to_all | solution.py:20

commit v2 on v1

v2 whole, which is shorter than its diff:
```python
import jax
import jax.numpy as jnp
from jax import lax
from jax.experimental import pallas as pl
from jax.experimental.pallas import tpu as pltpu
from jax.sharding import Mesh
from jax.sharding import PartitionSpec as P

EVERY = ("zhi", "core", "y", "zlo", "x")
GROUP = ("y", "zlo", "x")
PLANE = ("y", "x")
BF16, F32 = jnp.bfloat16, jnp.float32
TN = (((0,), (0,)), ((), ()))
NT = (((1,), (1,)), ((), ()))
NN = (((1,), (0,)), ((), ()))
TT = (((0,), (1,)), ((), ()))


def dot(left, right, dims):
    return lax.dot_general(left, right, dims, preferred_element_type=F32)


def norm_lanes(values, gain, bias):
    center = jnp.mean(values, axis=1, keepdims=True)
    spread = jnp.mean(jnp.square(values - center), axis=1, keepdims=True)
    return (values - center) * lax.rsqrt(spread + 1e-05) * gain + bias


def picker(parity):
    rows = lax.broadcasted_iota(jnp.int32, (128, 256), 0)
    columns = lax.broadcasted_iota(jnp.int32, (128, 256), 1)
    return (columns == 2 * rows + parity).astype(F32).astype(BF16)


def pack_kernel(pair, targets, mask, gain, bias, in_weight, send, flat, marks, rows):
    flat[...] = pair[...].astype(F32)
    maskf = mask[...].astype(F32)
    for r in range(2):
        normed = norm_lanes(flat[r * 256 : (r + 1) * 256, :], gain[...], bias[...]).astype(BF16)
        proj = dot(in_weight[...], normed, TT)
        projected = proj[:256] * jax.nn.sigmoid(proj[256:]) * maskf[r : r + 1]
        for side in range(2):
            for half in range(2):
                rows[pl.ds(side * 4 + r * 2 + half, 128, stride=16), :] = projected[
                    side * 128 : (side + 1) * 128, half * 128 : (half + 1) * 128
                ]
    marks[...] = jnp.zeros_like(marks)
    for ir in range(2):
        marks[ir, 4 * ir : 4 * ir + 2, :] = targets[...].astype(F32)
        marks[ir, 4 * ir + 2 : 4 * ir + 4, :] = maskf
        for jr in range(2):
            rows[pl.ds(8 + ir * 2 + jr, 128, stride=16), :] = flat[
                pl.ds(jr * 256 + ir, 128, stride=2), :
            ]
    rows[pl.ds(12, 128, stride=16), :] = dot(picker(0), marks[0].astype(BF16), NT) + dot(
        picker(1), marks[1].astype(BF16), NT
    )
    for row in range(13, 16):
        rows[pl.ds(row, 128, stride=16), :] = jnp.zeros((128, 128), F32)
    send[...] = rows[...].astype(BF16)


def triangle_kernel(got, send, rows, products):
    rows[...] = got[...].astype(F32)
    sides = []
    for side in range(2):
        for r in range(2):
            halves = [rows[pl.ds(side * 4 + r * 2 + half, 128, stride=16), :] for half in range(2)]
            sides.append(jnp.concatenate(halves, axis=1).astype(BF16))
    for r in range(2):
        for jr in range(2):
            products[pl.ds(r * 2 + jr, 128, stride=8), :] = dot(sides[r], sides[2 + jr], NT)
            products[pl.ds(4 + r * 2 + jr, 128, stride=8), :] = dot(sides[2 + r], sides[jr], NT)
    send[...] = products[...].astype(BF16)


def gate_kernel(
    pair, got, targets, mask, factor, gain, bias, gate_weight, base, gate, marks, flat, rows, own
):
    flat[...] = pair[...].astype(F32)
    rows[...] = got[...].astype(F32)
    for r in range(2):
        for jr in range(2):
            block = r * 2 + jr
            base[block * 128 : (block + 1) * 128, :] = flat[pl.ds(r * 256 + jr, 128, stride=2), :]
            base[(4 + block) * 128 : (5 + block) * 128, :] = rows[
                pl.ds(8 + block, 128, stride=16), :
            ]
    normed = norm_lanes(base[...], gain[...], bias[...]).astype(BF16)
    gate[...] = jax.nn.sigmoid(dot(normed, gate_weight[...], NN))
    own[...] = jnp.zeros_like(own)
    own[0:2, :] = targets[...].astype(F32)
    own[2:4, :] = mask[...].astype(F32)
    own[4:6, :] = factor[...]
    back = jnp.transpose(rows[pl.ds(12, 128, stride=16), :])
    for jr in range(2):
        picked = dot(own[...].astype(BF16), picker(jr), NT)
        for r in range(2):
            block = r * 2 + jr
            weight = picked[4 + r : 5 + r]
            at = r * 4 + jr
            marks[block : block + 1, :] = picked[2 + r : 3 + r] * weight
            marks[4 + block : 5 + block, :] = back[at + 2 : at + 3] * weight
            marks[8 + block : 9 + block, :] = picked[r : r + 1]
            marks[12 + block : 13 + block, :] = back[at : at + 1]


def head_kernel(
    got, base, gate, marks, gain, bias, out_weight, dist_weight, dist_bias, updated, grad, total, hidden
):
    values = got[...].astype(F32).reshape(128, 8, 128)
    hidden[...] = got[...].astype(F32)
    center = jnp.mean(values, axis=0)
    spread = jnp.mean(jnp.square(values - center[None]), axis=0)
    scale = lax.rsqrt(spread + 1e-05)
    q = []
    kept = []
    for block in range(8):
        here = hidden[pl.ds(block, 128, stride=8), :]
        normed = (here - center[block : block + 1]) * scale[block : block + 1]
        normed = (normed * gain[...] + bias[...]).astype(BF16)
        update = dot(normed, out_weight[...], TN)
        at = pl.ds(block * 128, 128)
        sums = (base[at, :] + gate[at, :] * update).astype(BF16)
        q.append(dot(dist_weight[...], sums, TT))
        if block < 4:
            kept.append(sums)
            updated[at, :] = sums
    bins = lax.broadcasted_iota(jnp.int32, (64, 128), 0).astype(F32)
    losses = jnp.zeros((1, 128), F32)
    weights = jnp.zeros((64, 128), F32)
    for block in range(4):
        logits = q[block] + q[4 + block] + dist_bias[...]
        shifted = logits - jnp.max(logits, axis=0, keepdims=True)
        powers = jnp.exp(shifted)
        norms = jnp.sum(powers, axis=0, keepdims=True)
        log_probs = shifted - jnp.log(norms)
        probs = powers / norms
        row = lambda at: marks[at + block : at + block + 1, :]
        onehot = (bins == row(8)).astype(F32)
        onehot_back = (bins == row(12)).astype(F32)
        losses = losses - row(0) * jnp.sum(onehot * log_probs, axis=0, keepdims=True)
        slope = row(0) * (probs - onehot) + row(4) * (probs - onehot_back)
        grad[block * 64 : (block + 1) * 64, :] = slope
        high = slope.astype(BF16)
        low = (slope - high.astype(F32)).astype(BF16)
        weights = weights + dot(high, kept[block], NN) + dot(low, kept[block], NN)
    loss = jnp.broadcast_to(jnp.sum(losses, axis=1, keepdims=True), (8, 128))
    for peer in range(16):
        total[peer * 72 : peer * 72 + 64, :] = weights
        total[peer * 72 + 64 : peer * 72 + 72, :] = loss


def output_kernel(updated, grad, dist_weight, pair_out, grad_pair, rows):
    for r in range(2):
        for jr in range(2):
            block = r * 2 + jr
            at = pl.ds(r * 256 + jr, 128, stride=2)
            rows[at, :] = updated[block * 128 : (block + 1) * 128, :].astype(F32)
            slope = grad[block * 64 : (block + 1) * 64, :]
            high = slope.astype(BF16)
            rest = slope - high.astype(F32)
            middle = rest.astype(BF16)
            grad_pair[at, :] = dot(high, dist_weight[...], TT) + dot(middle, dist_weight[...], TT)
    pair_out[...] = rows[...].astype(BF16)


def run(kernel, outs, scratch, args, flops=10_000_000):
    shapes = [jax.ShapeDtypeStruct(s, d) for s, d in outs]
    moved = sum(x.size * x.dtype.itemsize for x in args)
    return pl.pallas_call(
        kernel,
        out_shape=shapes,
        scratch_shapes=[pltpu.VMEM(s, d) for s, d in scratch],
        compiler_params=pltpu.CompilerParams(vmem_limit_bytes=24 * 1024 * 1024),
        cost_estimate=pl.CostEstimate(flops=flops, bytes_accessed=moved, transcendentals=0),
    )(*args)


def pack(pair, targets, mask, gain, bias, in_weight):
    scratch = [((512, 128), F32), ((2, 128, 256), F32), ((2048, 128), F32)]
    return run(pack_kernel, [((2048, 128), BF16)], scratch, (pair, targets, mask, gain, bias, in_weight))[0]


def triangle(got):
    scratch = [((2048, 128), F32), ((1024, 128), F32)]
    return run(triangle_kernel, [((1024, 128), BF16)], scratch, (got,))[0]


def gates(pair, got, targets, mask, factor, gain, bias, gate_weight):
    outs = [((1024, 128), F32), ((1024, 128), F32), ((16, 128), F32)]
    scratch = [((512, 128), F32), ((2048, 128), F32), ((16, 256), F32)]
    return run(gate_kernel, outs, scratch, (pair, got, targets, mask, factor, gain, bias, gate_weight))


def head(*args):
    outs = [((512, 128), BF16), ((256, 128), F32), ((1152, 128), F32)]
    return run(head_kernel, outs, [((1024, 128), F32)], args)


def outputs(updated, grad, dist_weight):
    outs = [((512, 128), BF16), ((512, 128), F32)]
    return run(output_kernel, outs, [((512, 128), F32)], (updated, grad, dist_weight))


def exchange(values, axes):
    return lax.all_to_all(values, axes, 0, 0, tiled=True)


def on_device(
    pair,
    chain,
    targets,
    pair_mask,
    ln_in_gain,
    ln_in_bias,
    in_weight,
    out_gate_weight,
    ln_out_gain,
    ln_out_bias,
    out_weight,
    dist_weight,
    dist_bias,
):
    tokens = 256
    flat = pair.reshape(512, 128)
    gain, bias = ln_in_gain.reshape(1, 128), ln_in_bias.reshape(1, 128)
    place = lax.axis_index(GROUP) * 2
    own_chain = lax.dynamic_slice_in_dim(chain, place, 2)
    factor = 1.0 + (own_chain[:, None] != chain[None, :]).astype(F32)

    send = pack(flat, targets, pair_mask, gain, bias, in_weight)
    got = exchange(send.reshape(128, 16, 128), GROUP).reshape(2048, 128)
    products = triangle(got)
    base, gate, marks = gates(flat, got, targets, pair_mask, factor, gain, bias, out_gate_weight)
    hidden = exchange(products.reshape(128, 8, 128), GROUP).reshape(1024, 128)
    updated, grad, total = head(
        hidden,
        base,
        gate,
        marks,
        ln_out_gain.reshape(128, 1),
        ln_out_bias.reshape(128, 1),
        out_weight,
        dist_weight,
        dist_bias.reshape(64, 1),
    )
    total = jnp.sum(exchange(total.reshape(16, 72, 128), PLANE), axis=0)
    pair_out, grad_pair = outputs(updated, grad, dist_weight)
    total = exchange(jnp.broadcast_to(total[None], (8, 72, 128)), "zlo")
    total = jnp.sum(total, axis=0)
    return (
        pair_out.reshape(2, 256, 128),
        grad_pair.reshape(2, 256, 128),
        jnp.swapaxes(total[:64], 0, 1) / tokens,
        (total[64, :1] / (tokens * tokens)).reshape(1),
    )


def solution(mesh):
    fine = Mesh(mesh.devices.reshape(2, 2, 4, 8, 4), EVERY)
    part = ("zhi", "core")
    in_specs = (
        P(EVERY, None, None),
        P(part),
        P(EVERY, None),
        P(EVERY, None),
        P(),
        P(),
        P(),
        P(),
        P(),
        P(),
        P(),
        P(part, None),
        P(),
    )
    out_specs = (
        P(EVERY, None, None),
        P(EVERY, None, None),
        P(part, None),
        P(part),
    )
    return jax.shard_map(
        on_device, mesh=fine, in_specs=in_specs, out_specs=out_specs, check_vma=False
    )
```

time: 134 us -> 126 us (0.940)
  blocking collectives: 14.1 us -> 63.4 us
  waiting for transfers between devices: 60.6 us -> 32.1 us
  starting transfers between devices: 34.4 us -> 15.5 us
  other arithmetic: 7.49 us -> 0.75 us
  Pallas kernels: 0 us -> 5.23 us
  local copies, waits for them, and re-layouts: 10.6 us -> 5.57 us
  matrix products: 2.83 us -> 0 us
    all_to_all x1 -> x2, blocking collectives: 14.1 us -> 63.4 us  [exchange(): return lax.all_to_all(values, axes, 0, 0, tiled=True)]
    all_to_all x3 -> x2, waiting for transfers between devices: 60.6 us -> 32.1 us  [exchange(): return lax.all_to_all(values, axes, 0, 0, tiled=True)]
    all_to_all x3 -> x2, starting transfers between devices: 34.4 us -> 15.5 us  [exchange(): return lax.all_to_all(values, axes, 0, 0, tiled=True)]
    pallas_call x0 -> x5, Pallas kernels: none -> 5.23 us  [run(): pl.pallas_call(kernel, out_shape=shapes, scratch_shapes=[pltpu.VMEM(s, d)...]
    reduce_sum x11 -> x2, other arithmetic: 3.34 us -> 0.06 us  [the longest x1 0.04 us: on_device(): total = jnp.sum(exchange(total.reshape(16, 72, 128), PLANE), axis=0)]
    dot_general x8 -> x0, matrix products: 2.83 us -> none  [the longest x1 1.11 us: on_device(): jnp.einsum('bt,cb->tc', grad_sym, dist_weight.astype(f32), precision=lax....]
    concatenate x4 -> x0, other arithmetic: 1.68 us -> none  [the longest x1 0.84 us: on_device(): jnp.concatenate([mixed.reshape(128, 4, 128), mirrored.reshape(128, 4, 128...]
    unnamed x32 -> x29, local copies, waits for them, and re-layouts: 5.29 us -> 3.94 us
  transfers between devices with their start and end apart: 3 -> 2, of which waited for: 3 -> 2; matrix products, arithmetic and copies ran while one was open for 3% -> 0% of each run, Pallas kernels for 0% -> 1%
where the time goes in v2:
time: 126 us; the launch traced here: 125 us
  blocking collectives  63.4 us (50%)
  waiting for transfers between devices  32.1 us (25%)
  starting transfers between devices  15.5 us (12%)
  local copies, waits for them, and re-layouts  5.57 us (4%)
  Pallas kernels  5.23 us (4%)
  between operations  2.54 us (2%)
    all_to_all x2, blocking collectives, exchange(): return lax.all_to_all(values, axes, 0, 0, tiled=True)  63.4 us
    all_to_all x2, waiting for transfers between devices, exchange(): return lax.all_to_all(values, axes, 0, 0, tiled=True)  32.1 us
    all_to_all x2, starting transfers between devices, exchange(): return lax.all_to_all(values, axes, 0, 0, tiled=True)  15.5 us
    pallas_call x5, Pallas kernels, run(): pl.pallas_call(kernel, out_shape=shapes, scratch_shapes=[pltpu.VMEM(s, d)...  5.23 us
    unnamed x29, local copies, waits for them, and re-layouts  3.94 us
  transfers between devices with their start and end apart: 2, of which 2 were waited for; matrix products, arithmetic and copies ran while one was open for 0% of the time, Pallas kernels for 1%

profile of v2, /device:TPU:32, one launch (start us, length us, event | category | flops | bytes accessed | tf_op | source)
XLA Modules:
  0.0 125.1 jit_solution(13501113013645069756)
XLA Ops:
  0.6 0.0 copy-start.6
  0.6 0.0 copy-start.5
  0.7 0.0 copy-start.7
  0.7 0.0 copy-start.8
  0.7 0.6 copy-done.6
  1.3 0.0 copy-done.5
  1.3 0.0 copy-done.7
  1.3 0.0 copy-done.8
  1.3 0.0 copy-start
  1.3 0.9 copy-done
  2.2 0.0 copy-start.2
  2.2 0.9 copy-done.2
  3.1 0.8 shard_map.156
  3.9 49.3 %all_to_all.20 = bf16[128,16,128]{2,1,0:T(8,128)(2,1)S(1)} all-to-all(bf16[128,16,128]{2,1,0:T(8,128)(2,1)S(1)} %bitcast.18), channel_id=1, replica_groups=mesh['zhi'=2,'core'=2,'y'=4,'zlo'=8,'x'=4] {'y','zlo','x'}, dimensions={0} | all-to-all | bytes 1048576 | tf_op jit(solution)/shard_map/all_to_all | solution.py:207
  53.2 1.2 shard_map.157
  54.4 0.0 copy-start.9
  54.4 0.0 copy-start.11
  54.4 0.0 copy-start.12
  54.4 9.2 %all-to-all-start.1 = ((bf16[128,8,128]{2,1,0:T(8,128)(2,1)}), bf16[128,8,128]{2,1,0:T(8,128)(2,1)S(1)}, u32[]{:S(2)}, u32[]{:S(2)}) async-start(bf16[128,8,128]{2,1,0:T(8,128)(2,1)} %bitcast.5), calls=%async_computation.1 | async-start | bytes 524288 | tf_op jit(solution)/shard_map/all_to_all | solution.py:207
  63.5 0.0 copy-start.1
  63.6 0.0 copy-done.9
  63.6 0.1 copy.24.dist_weight
  63.7 0.0 copy-done.11
  63.7 0.1 copy.25.dist_bias
  63.8 0.0 copy-done.12
  63.8 0.1 copy.22.gain
  63.9 0.0 copy-start.13
  63.9 0.7 copy-done.13
  64.6 0.0 copy-start.3
  64.6 0.1 copy.23.bias
  64.7 0.0 copy-start.10
  64.7 0.7 copy-done.10
  65.4 0.1 dynamic_slice.3
  65.4 0.1 fusion.1.factor
  65.5 0.0 copy-done.1
  65.5 0.0 copy-done.3
  65.5 0.0 copy-start.4
  65.5 0.6 shard_map.158
  66.1 17.1 %all-to-all-done.1 = bf16[128,8,128]{2,1,0:T(8,128)(2,1)S(1)} async-done(((bf16[128,8,128]{2,1,0:T(8,128)(2,1)}), bf16[128,8,128]{2,1,0:T(8,128)(2,1)S(1)}, u32[]{:S(2)}, u32[]{:S(2)}) %all-to-all-start.1) | async-done | bytes 262176 | tf_op jit(solution)/shard_map/all_to_all | solution.py:207
  83.2 0.0 copy-done.4
  83.2 1.7 %shard_map.159 = (bf16[512,128]{1,0:T(8,128)(2,1)S(1)}, f32[256,128]{1,0:T(8,128)S(1)}, f32[1152,128]{1,0:T(8,128)S(1)}) custom-call(bf16[1024,128]{1,0:T(8,128)(2,1)S(1)} %bitcast.19, f32[1024,128]{1,0:T(8,128)S(1)} %get-tuple-element.12.base, f32[1024,128]{1,0:T(8,128)S(1)} %get-tuple-element.13.gate, f32[16,128]{1,0:T(8,128)S(1)} %get-tuple-element.14.marks, ...), custom_call_target="tpu_custom_call" | custom-call | flops 10000000 | bytes 1369344 | tf_op jit(solution)/shard_map/pallas_call | solution.py:171
  84.9 14.1 %all_to_all.21 = f32[16,72,128]{2,1,0:T(8,128)S(1)} all-to-all(f32[16,72,128]{2,1,0:T(8,128)S(1)} %bitcast.20), channel_id=1, replica_groups=mesh['zhi'=2,'core'=2,'y'=4,'zlo'=8,'x'=4] {'y','x'}, dimensions={0} | all-to-all | bytes 1179648 | tf_op jit(solution)/shard_map/all_to_all | solution.py:207
  99.1 0.7 broadcast_in_dim.2
  99.8 6.3 %all-to-all-start.3 = ((f32[8,72,128]{2,1,0:T(8,128)}), f32[8,72,128]{2,1,0:T(8,128)S(1)}, u32[]{:S(2)}, u32[]{:S(2)}) async-start(f32[8,72,128]{2,1,0:T(8,128)} %broadcast_in_dim.2), calls=%async_computation.3 | async-start | bytes 589824 | tf_op jit(solution)/shard_map/all_to_all | solution.py:207
  106.1 1.0 shard_map.160
  107.2 15.0 %all-to-all-done.3 = f32[8,72,128]{2,1,0:T(8,128)S(1)} async-done(((f32[8,72,128]{2,1,0:T(8,128)}), f32[8,72,128]{2,1,0:T(8,128)S(1)}, u32[]{:S(2)}, u32[]{:S(2)}) %all-to-all-start.3) | async-done | bytes 294944 | tf_op jit(solution)/shard_map/all_to_all | solution.py:207
  122.2 0.5 slice.9
  122.7 0.6 fusion
  (2 shorter events, 0.1 us)
Async XLA Ops:
  0.6 0.7 copy-start.6
  0.6 0.7 copy-start.5
  0.7 0.7 copy-start.7
  0.7 0.7 copy-start.8
  1.3 0.9 copy-start
  2.2 0.9 copy-start.2
  54.4 9.2 %copy-start.9 = (bf16[128,64]{0,1:T(8,128)(2,1)S(1)}, bf16[128,64]{0,1:T(8,128)(2,1)}, u32[]{:S(2)}) copy-start(bf16[128,64]{0,1:T(8,128)(2,1)} %param.24) | copy-start | bytes 49156
  54.4 9.3 %copy-start.11 = (f32[64]{0:T(128)S(1)}, f32[64]{0:T(128)}, u32[]{:S(2)}) copy-start(f32[64]{0:T(128)} %param.25) | copy-start | bytes 772
  54.4 9.4 %copy-start.12 = (f32[128]{0:T(128)S(1)}, f32[128]{0:T(128)}, u32[]{:S(2)}) copy-start(f32[128]{0:T(128)} %param.21) | copy-start | bytes 1540
  54.4 28.9 %all-to-all-start.1 = ((bf16[128,8,128]{2,1,0:T(8,128)(2,1)}), bf16[128,8,128]{2,1,0:T(8,128)(2,1)S(1)}, u32[]{:S(2)}, u32[]{:S(2)}) async-start(bf16[128,8,128]{2,1,0:T(8,128)(2,1)} %bitcast.5), calls=%async_computation.1 | async-start | bytes 524288 | tf_op jit(solution)/shard_map/all_to_all | solution.py:207
  63.5 2.0 %copy-start.1 = (bf16[2,256,128]{2,1,0:T(8,128)(2,1)S(1)}, bf16[2,256,128]{2,1,0:T(8,128)(2,1)}, u32[]{:S(2)}) copy-start(bf16[2,256,128]{2,1,0:T(8,128)(2,1)} %param.13) | copy-start | bytes 393220
  63.9 0.7 copy-start.13
  64.6 0.9 copy-start.3
  64.7 0.7 copy-start.10
  65.5 17.7 %copy-start.4 = (bf16[128,128]{1,0:T(8,128)(2,1)S(1)}, bf16[128,128]{1,0:T(8,128)(2,1)}, u32[]{:S(2)}) copy-start(bf16[128,128]{1,0:T(8,128)(2,1)} %out_weight.1) | copy-start | bytes 98308
  99.8 22.4 %all-to-all-start.3 = ((f32[8,72,128]{2,1,0:T(8,128)}), f32[8,72,128]{2,1,0:T(8,128)S(1)}, u32[]{:S(2)}, u32[]{:S(2)}) async-start(f32[8,72,128]{2,1,0:T(8,128)} %broadcast_in_dim.2), calls=%async_computation.3 | async-start | bytes 589824 | tf_op jit(solution)/shard_map/all_to_all | solution.py:207

commit v3 on v2

v3 whole, which is shorter than its diff:
```python
import jax
import jax.numpy as jnp
from jax import lax
from jax.experimental import pallas as pl
from jax.experimental.pallas import tpu as pltpu
from jax.sharding import Mesh
from jax.sharding import PartitionSpec as P

EVERY = ("zhi", "core", "y", "zlo", "x")
GROUP = ("y", "zlo", "x")
PLANE = ("y", "x")
BF16, F32 = jnp.bfloat16, jnp.float32
TN = (((0,), (0,)), ((), ()))
NT = (((1,), (1,)), ((), ()))
NN = (((1,), (0,)), ((), ()))
TT = (((0,), (1,)), ((), ()))


def dot(left, right, dims):
    return lax.dot_general(left, right, dims, preferred_element_type=F32)


def norm_lanes(values, gain, bias):
    center = jnp.mean(values, axis=1, keepdims=True)
    spread = jnp.mean(jnp.square(values - center), axis=1, keepdims=True)
    return (values - center) * lax.rsqrt(spread + 1e-05) * gain + bias


def picker(parity):
    rows = lax.broadcasted_iota(jnp.int32, (128, 256), 0)
    columns = lax.broadcasted_iota(jnp.int32, (128, 256), 1)
    return (columns == 2 * rows + parity).astype(F32).astype(BF16)


def pack_kernel(
    pair_far, targets_far, mask_far, gain_far, bias_far, weight_far, send,
    pair, targets, mask, gain, bias, in_weight, flat, marks, rows, sems,
):
    far = (targets_far, mask_far, pair_far, gain_far, bias_far, weight_far)
    near = (targets, mask, pair, gain, bias, in_weight)
    copies = [pltpu.make_async_copy(far[n], near[n], sems.at[n]) for n in range(6)]
    for copy in copies:
        copy.start()
    copies[0].wait()
    copies[1].wait()
    maskf = mask[...].astype(F32)
    marks[...] = jnp.zeros_like(marks)
    for ir in range(2):
        marks[ir, 4 * ir : 4 * ir + 2, :] = targets[...].astype(F32)
        marks[ir, 4 * ir + 2 : 4 * ir + 4, :] = maskf
    rows[pl.ds(12, 128, stride=14), :] = dot(picker(0), marks[0].astype(BF16), NT) + dot(
        picker(1), marks[1].astype(BF16), NT
    )
    rows[pl.ds(13, 128, stride=14), :] = jnp.zeros((128, 128), F32)
    copies[2].wait()
    flat[...] = pair[...].astype(F32)
    for ir in range(2):
        for jr in range(2):
            rows[pl.ds(8 + ir * 2 + jr, 128, stride=14), :] = flat[
                pl.ds(jr * 256 + ir, 128, stride=2), :
            ]
    for copy in copies[3:]:
        copy.wait()
    for r in range(2):
        normed = norm_lanes(flat[r * 256 : (r + 1) * 256, :], gain[...], bias[...]).astype(BF16)
        proj = dot(in_weight[...], normed, TT)
        projected = proj[:256] * jax.nn.sigmoid(proj[256:]) * maskf[r : r + 1]
        for side in range(2):
            for half in range(2):
                rows[pl.ds(side * 4 + r * 2 + half, 128, stride=14), :] = projected[
                    side * 128 : (side + 1) * 128, half * 128 : (half + 1) * 128
                ]
    send[...] = rows[...].astype(BF16)


def triangle_kernel(got, send, rows, products):
    rows[...] = got[...].astype(F32)
    sides = []
    for side in range(2):
        for r in range(2):
            halves = [rows[pl.ds(side * 4 + r * 2 + half, 128, stride=14), :] for half in range(2)]
            sides.append(jnp.concatenate(halves, axis=1).astype(BF16))
    for r in range(2):
        for jr in range(2):
            products[pl.ds(r * 2 + jr, 128, stride=8), :] = dot(sides[r], sides[2 + jr], NT)
            products[pl.ds(4 + r * 2 + jr, 128, stride=8), :] = dot(sides[2 + r], sides[jr], NT)
    send[...] = products[...].astype(BF16)


def gate_kernel(
    pair, got, targets, mask, chain, place, gain, bias, gate_weight, base, gate, marks, flat, rows, own
):
    flat[...] = pair[...].astype(F32)
    rows[...] = got[...].astype(F32)
    for r in range(2):
        for jr in range(2):
            block = r * 2 + jr
            base[block * 128 : (block + 1) * 128, :] = flat[pl.ds(r * 256 + jr, 128, stride=2), :]
            base[(4 + block) * 128 : (5 + block) * 128, :] = rows[
                pl.ds(8 + block, 128, stride=14), :
            ]
    normed = norm_lanes(base[...], gain[...], bias[...]).astype(BF16)
    gate[...] = jax.nn.sigmoid(dot(normed, gate_weight[...], NN))
    own[...] = jnp.zeros_like(own)
    own[0:2, :] = targets[...].astype(F32)
    own[2:4, :] = mask[...].astype(F32)
    columns = lax.broadcasted_iota(jnp.int32, (1, 256), 1)
    for r in range(2):
        here = jnp.sum(jnp.where(columns == place[0] + r, chain[...], 0), axis=1, keepdims=True)
        own[4 + r : 5 + r, :] = 1.0 + (chain[...] != here).astype(F32)
    back = jnp.transpose(rows[pl.ds(12, 128, stride=14), :])
    for jr in range(2):
        picked = dot(own[...].astype(BF16), picker(jr), NT)
        for r in range(2):
            block = r * 2 + jr
            weight = picked[4 + r : 5 + r]
            at = r * 4 + jr
            marks[block : block + 1, :] = picked[2 + r : 3 + r] * weight
            marks[4 + block : 5 + block, :] = back[at + 2 : at + 3] * weight
            marks[8 + block : 9 + block, :] = picked[r : r + 1]
            marks[12 + block : 13 + block, :] = back[at : at + 1]


def spread_sums(weights, loss, peers):
    row = lax.broadcasted_iota(jnp.int32, (8, 128), 0)
    high = loss.astype(BF16).astype(F32)
    terms = jnp.where(row == 0, high, jnp.where(row == 1, loss - high, 0.0))
    return jnp.concatenate([weights, terms] * peers, axis=0).astype(BF16)


def add_sums(got, peers):
    sums = jnp.sum(got[...].astype(F32).reshape(peers, 72, 128), axis=0)
    return sums[:64], sums[64:65, 0:1] + sums[65:66, 0:1]


def middle_kernel(got, send):
    weights, loss = add_sums(got, 16)
    send[...] = spread_sums(weights, loss, 8)


def last_kernel(got, grad_weight, loss):
    weights, total = add_sums(got, 8)
    grad_weight[...] = weights * (1.0 / 256)
    loss[0] = total[0, 0] * (1.0 / 65536)


def head_kernel(
    got, base, gate, marks, gain, bias, out_weight, dist_weight, dist_bias, updated, grad, total, hidden
):
    values = got[...].astype(F32).reshape(128, 8, 128)
    hidden[...] = got[...].astype(F32)
    gain = jnp.transpose(jnp.broadcast_to(gain[...], (8, 128)))[:, :1]
    bias = jnp.transpose(jnp.broadcast_to(bias[...], (8, 128)))[:, :1]
    dist_bias = jnp.transpose(jnp.broadcast_to(dist_bias[...], (8, 64)))[:, :1]
    center = jnp.mean(values, axis=0)
    spread = jnp.mean(jnp.square(values - center[None]), axis=0)
    scale = lax.rsqrt(spread + 1e-05)
    q = []
    kept = []
    for block in range(8):
        here = hidden[pl.ds(block, 128, stride=8), :]
        normed = (here - center[block : block + 1]) * scale[block : block + 1]
        normed = (normed * gain + bias).astype(BF16)
        update = dot(normed, out_weight[...], TN)
        at = pl.ds(block * 128, 128)
        sums = (base[at, :] + gate[at, :] * update).astype(BF16)
        q.append(dot(dist_weight[...], sums, NT))
        if block < 4:
            kept.append(sums)
            updated[at, :] = sums
    bins = lax.broadcasted_iota(jnp.int32, (64, 128), 0).astype(F32)
    losses = jnp.zeros((1, 128), F32)
    weights = jnp.zeros((64, 128), F32)
    for block in range(4):
        logits = q[block] + q[4 + block] + dist_bias
        shifted = logits - jnp.max(logits, axis=0, keepdims=True)
        powers = jnp.exp(shifted)
        norms = jnp.sum(powers, axis=0, keepdims=True)
        log_probs = shifted - jnp.log(norms)
        probs = powers / norms
        row = lambda at: marks[at + block : at + block + 1, :]
        onehot = (bins == row(8)).astype(F32)
        onehot_back = (bins == row(12)).astype(F32)
        losses = losses - row(0) * jnp.sum(onehot * log_probs, axis=0, keepdims=True)
        slope = row(0) * (probs - onehot) + row(4) * (probs - onehot_back)
        grad[block * 64 : (block + 1) * 64, :] = slope
        high = slope.astype(BF16)
        low = (slope - high.astype(F32)).astype(BF16)
        weights = weights + dot(high, kept[block], NN) + dot(low, kept[block], NN)
    total[...] = spread_sums(weights, jnp.sum(losses, axis=1, keepdims=True), 16)


def output_kernel(updated, grad, dist_weight, pair_out, grad_pair, rows):
    for r in range(2):
        for jr in range(2):
            block = r * 2 + jr
            at = pl.ds(r * 256 + jr, 128, stride=2)
            rows[at, :] = updated[block * 128 : (block + 1) * 128, :].astype(F32)
            slope = grad[block * 64 : (block + 1) * 64, :]
            high = slope.astype(BF16)
            rest = slope - high.astype(F32)
            middle = rest.astype(BF16)
            grad_pair[at, :] = dot(high, dist_weight[...], TN) + dot(middle, dist_weight[...], TN)
    pair_out[...] = rows[...].astype(BF16)


def run(kernel, outs, scratch, args, room=24, **specs):
    shapes = [jax.ShapeDtypeStruct(s, d) for s, d in outs]
    moved = sum(x.size * x.dtype.itemsize for x in args)
    scratch = [pltpu.VMEM(*s) if isinstance(s, tuple) else s for s in scratch]
    return pl.pallas_call(
        kernel,
        out_shape=shapes,
        scratch_shapes=scratch,
        compiler_params=pltpu.CompilerParams(vmem_limit_bytes=room * 1024 * 1024),
        cost_estimate=pl.CostEstimate(flops=10_000_000, bytes_accessed=moved, transcendentals=0),
        **specs,
    )(*args)


VMEM, FAR = pl.BlockSpec(memory_space=pltpu.VMEM), pl.BlockSpec(memory_space=pl.ANY)
SMEM = pl.BlockSpec(memory_space=pltpu.SMEM)


def pack(pair, targets, mask, gain, bias, in_weight):
    scratch = [
        ((512, 128), BF16),
        ((2, 256), jnp.int32),
        ((2, 256), jnp.int32),
        ((1, 128), F32),
        ((1, 128), F32),
        ((128, 512), BF16),
        ((512, 128), F32),
        ((2, 128, 256), F32),
        ((1792, 128), F32),
        pltpu.SemaphoreType.DMA((6,)),
    ]
    args = (pair, targets, mask, gain, bias, in_weight)
    return run(pack_kernel, [((1792, 128), BF16)], scratch, args, 60, in_specs=[FAR] * 6)[0]


def triangle(got):
    scratch = [((1792, 128), F32), ((1024, 128), F32)]
    return run(triangle_kernel, [((1024, 128), BF16)], scratch, (got,))[0]


def gates(*args):
    outs = [((1024, 128), F32), ((1024, 128), F32), ((16, 128), F32)]
    scratch = [((512, 128), F32), ((1792, 128), F32), ((16, 256), F32)]
    return run(gate_kernel, outs, scratch, args, in_specs=[VMEM] * 5 + [SMEM] + [VMEM] * 3)


def head(*args):
    outs = [((512, 128), BF16), ((256, 128), F32), ((1152, 128), BF16)]
    return run(head_kernel, outs, [((1024, 128), F32)], args)


def outputs(updated, grad, dist_weight):
    outs = [((512, 128), BF16), ((512, 128), F32)]
    return run(output_kernel, outs, [((512, 128), F32)], (updated, grad, dist_weight))


def middle(got):
    return run(middle_kernel, [((576, 128), BF16)], [], (got,))[0]


def last(got):
    outs = [((64, 128), F32), ((1,), F32)]
    return run(last_kernel, outs, [], (got,), out_specs=[VMEM, SMEM])


def exchange(values, axes):
    return lax.all_to_all(values, axes, 0, 0, tiled=True)


def on_device(
    pair,
    chain,
    targets,
    pair_mask,
    ln_in_gain,
    ln_in_bias,
    in_weight,
    out_gate_weight,
    ln_out_gain,
    ln_out_bias,
    out_weight,
    dist_weight,
    dist_bias,
):
    flat = pair.reshape(512, 128)
    gain, bias = ln_in_gain.reshape(1, 128), ln_in_bias.reshape(1, 128)
    place = (lax.axis_index(GROUP) * 2).reshape(1)
    dist_weight = jnp.swapaxes(dist_weight, 0, 1)

    send = pack(flat, targets, pair_mask, gain, bias, in_weight)
    got = exchange(send.reshape(128, 7, 2, 128), GROUP).reshape(1792, 128)
    products = triangle(got)
    base, gate, marks = gates(
        flat, got, targets, pair_mask, chain.reshape(1, 256), place, gain, bias, out_gate_weight
    )
    hidden = exchange(products.reshape(128, 8, 128), GROUP).reshape(1024, 128)
    updated, grad, total = head(
        hidden,
        base,
        gate,
        marks,
        ln_out_gain.reshape(1, 128),
        ln_out_bias.reshape(1, 128),
        out_weight,
        dist_weight,
        dist_bias.reshape(1, 64),
    )
    total = middle(exchange(total.reshape(16, 72, 128), PLANE).reshape(1152, 128))
    pair_out, grad_pair = outputs(updated, grad, dist_weight)
    grad_weight, loss = last(exchange(total.reshape(8, 72, 128), "zlo").reshape(576, 128))
    return (
        pair_out.reshape(2, 256, 128),
        grad_pair.reshape(2, 256, 128),
        jnp.swapaxes(grad_weight, 0, 1),
        loss,
    )


def solution(mesh):
    fine = Mesh(mesh.devices.reshape(2, 2, 4, 8, 4), EVERY)
    part = ("zhi", "core")
    in_specs = (
        P(EVERY, None, None),
        P(part),
        P(EVERY, None),
        P(EVERY, None),
        P(),
        P(),
        P(),
        P(),
        P(),
        P(),
        P(),
        P(part, None),
        P(),
    )
    out_specs = (
        P(EVERY, None, None),
        P(EVERY, None, None),
        P(part, None),
        P(part),
    )
    return jax.shard_map(
        on_device, mesh=fine, in_specs=in_specs, out_specs=out_specs, check_vma=False
    )
```

time: 126 us -> 112 us (0.89)
  the two profiles are of different devices: /device:TPU:32 before, /device:TPU:2 now
where the time goes in v3:
time: 112 us
  blocking collectives  59.8 us (53%)
  waiting for transfers between devices  29.6 us (26%)
  starting transfers between devices  12.3 us (11%)
  Pallas kernels  8.12 us (7%)
  local copies, waits for them, and re-layouts  1.33 us (1%)
    all_to_all x2, blocking collectives, exchange(): return lax.all_to_all(values, axes, 0, 0, tiled=True)  59.8 us
    all_to_all x2, waiting for transfers between devices, exchange(): return lax.all_to_all(values, axes, 0, 0, tiled=True)  29.6 us
    all_to_all x2, starting transfers between devices, exchange(): return lax.all_to_all(values, axes, 0, 0, tiled=True)  12.3 us
    pallas_call x7, Pallas kernels, run(): pl.pallas_call(kernel, out_shape=shapes, scratch_shapes=scratch, compiler...  8.12 us
  transfers between devices with their start and end apart: 2, of which 2 were waited for; matrix products, arithmetic and copies ran while one was open for 0% of the time, Pallas kernels for 1%

profile of v3, /device:TPU:2, one launch (start us, length us, event | category | flops | bytes accessed | tf_op | source)
XLA Modules:
  0.0 111.8 jit_solution(7262319672838249789)
XLA Ops:
  0.6 2.4 %shard_map.156 = bf16[1792,128]{1,0:T(8,128)(2,1)} custom-call(bf16[512,128]{1,0:T(8,128)(2,1)} %bitcast.25, s32[2,256]{1,0:T(2,128)} %targets.1, s32[2,256]{1,0:T(2,128)} %mask.1, f32[1,128]{1,0:T(1,128)} %bitcast.30, f32[1,128]{1,0:T(1,128)} %bitcast.32, bf16[128,512]{1,0:T(8,128)(2,1)} %weight_far.1), custom_call_target="tpu_custom_call" | custom-call | flops 10000000 | bytes 267264 | tf_op jit(solution)/shard_map/pallas_call | solution.py:211
  3.0 48.1 %all_to_all.20 = bf16[128,7,2,128]{3,2,1,0:T(2,128)(2,1)S(1)} all-to-all(bf16[128,7,2,128]{3,2,1,0:T(2,128)(2,1)} %bitcast.38), channel_id=1, replica_groups=mesh['zhi'=2,'core'=2,'y'=4,'zlo'=8,'x'=4] {'y','zlo','x'}, dimensions={0} | all-to-all | bytes 917504 | tf_op jit(solution)/shard_map/all_to_all | solution.py:273
  51.1 1.1 shard_map.157
  52.2 0.0 copy-start
  52.2 0.0 copy-start.2
  52.2 0.0 copy-start.8
  52.2 8.3 %all-to-all-start.1 = ((bf16[128,8,128]{2,1,0:T(8,128)(2,1)}), bf16[128,8,128]{2,1,0:T(8,128)(2,1)S(1)}, u32[]{:S(2)}, u32[]{:S(2)}) async-start(bf16[128,8,128]{2,1,0:T(8,128)(2,1)} %bitcast.5), calls=%async_computation.1 | async-start | bytes 524288 | tf_op jit(solution)/shard_map/all_to_all | solution.py:273
  60.5 0.0 copy-start.5
  60.5 0.0 copy-start.4
  60.5 0.0 copy-start.6
  60.5 0.0 copy-start.7
  60.5 0.0 copy-done
  60.5 0.0 copy-done.2
  60.5 0.0 copy-done.8
  60.5 0.6 copy-done.5
  61.1 0.0 copy-done.4
  61.2 0.0 copy-done.6
  61.2 0.0 copy-done.7
  61.2 0.0 copy-start.1
  61.2 0.0 copy-start.3
  61.2 0.6 shard_map.158
  61.7 18.9 %all-to-all-done.1 = bf16[128,8,128]{2,1,0:T(8,128)(2,1)S(1)} async-done(((bf16[128,8,128]{2,1,0:T(8,128)(2,1)}), bf16[128,8,128]{2,1,0:T(8,128)(2,1)S(1)}, u32[]{:S(2)}, u32[]{:S(2)}) %all-to-all-start.1) | async-done | bytes 262176 | tf_op jit(solution)/shard_map/all_to_all | solution.py:273
  80.6 0.0 copy-start.9
  80.6 0.0 copy-start.10
  80.6 0.0 copy-start.11
  80.6 0.0 copy-done.1
  80.7 0.0 copy-done.3
  80.7 0.6 copy-done.9
  81.3 0.0 copy-done.10
  81.3 0.0 copy-done.11
  81.3 1.7 %shard_map.159 = (bf16[512,128]{1,0:T(8,128)(2,1)S(1)}, f32[256,128]{1,0:T(8,128)S(1)}, bf16[1152,128]{1,0:T(8,128)(2,1)S(1)}) custom-call(bf16[1024,128]{1,0:T(8,128)(2,1)S(1)} %bitcast.23, f32[1024,128]{1,0:T(8,128)S(1)} %get-tuple-element.14.base, f32[1024,128]{1,0:T(8,128)S(1)} %get-tuple-element.15.gate, f32[16,128]{1,0:T(8,128)S(1)} %get-tuple-element.16.marks, ...), custom_call_target="tpu_custom_call" | custom-call | flops 10000000 | bytes 1369344 | tf_op jit(solution)/shard_map/pallas_call | solution.py:211
  83.0 11.8 %all_to_all.21 = bf16[16,72,128]{2,1,0:T(8,128)(2,1)S(1)} all-to-all(bf16[16,72,128]{2,1,0:T(8,128)(2,1)S(1)} %bitcast.27), channel_id=1, replica_groups=mesh['zhi'=2,'core'=2,'y'=4,'zlo'=8,'x'=4] {'y','x'}, dimensions={0} | all-to-all | bytes 589824 | tf_op jit(solution)/shard_map/all_to_all | solution.py:273
  94.8 0.8 shard_map.161
  95.5 4.0 %all-to-all-start.3 = ((bf16[8,72,128]{2,1,0:T(8,128)(2,1)}), bf16[8,72,128]{2,1,0:T(8,128)(2,1)S(1)}, u32[]{:S(2)}, u32[]{:S(2)}) async-start(bf16[8,72,128]{2,1,0:T(8,128)(2,1)} %bitcast.17), calls=%async_computation.3 | async-start | bytes 294912 | tf_op jit(solution)/shard_map/all_to_all | solution.py:273
  99.6 1.0 shard_map.160
  100.5 10.7 %all-to-all-done.3 = bf16[8,72,128]{2,1,0:T(8,128)(2,1)S(1)} async-done(((bf16[8,72,128]{2,1,0:T(8,128)(2,1)}), bf16[8,72,128]{2,1,0:T(8,128)(2,1)S(1)}, u32[]{:S(2)}, u32[]{:S(2)}) %all-to-all-start.3) | async-done | bytes 147488 | tf_op jit(solution)/shard_map/all_to_all | solution.py:273
  111.2 0.6 shard_map.162
Async XLA Ops:
  52.2 8.3 %copy-start = (bf16[2,256,128]{2,1,0:T(8,128)(2,1)S(1)}, bf16[2,256,128]{2,1,0:T(8,128)(2,1)}, u32[]{:S(2)}) copy-start(bf16[2,256,128]{2,1,0:T(8,128)(2,1)} %param.13) | copy-start | bytes 393220
  52.2 8.3 %copy-start.2 = (bf16[128,128]{1,0:T(8,128)(2,1)S(1)}, bf16[128,128]{1,0:T(8,128)(2,1)}, u32[]{:S(2)}) copy-start(bf16[128,128]{1,0:T(8,128)(2,1)} %gate_weight.1) | copy-start | bytes 98308
  52.2 8.4 %copy-start.8 = (s32[256]{0:T(256)S(1)}, s32[256]{0:T(256)}, u32[]{:S(2)}) copy-start(s32[256]{0:T(256)} %param.14) | copy-start | bytes 3076
  52.2 28.5 %all-to-all-start.1 = ((bf16[128,8,128]{2,1,0:T(8,128)(2,1)}), bf16[128,8,128]{2,1,0:T(8,128)(2,1)S(1)}, u32[]{:S(2)}, u32[]{:S(2)}) async-start(bf16[128,8,128]{2,1,0:T(8,128)(2,1)} %bitcast.5), calls=%async_computation.1 | async-start | bytes 524288 | tf_op jit(solution)/shard_map/all_to_all | solution.py:273
  60.5 0.7 copy-start.5
  60.5 0.7 copy-start.4
  60.5 0.7 copy-start.6
  60.5 0.7 copy-start.7
  61.2 19.5 %copy-start.1 = (bf16[128,64]{0,1:T(8,128)(2,1)S(1)}, bf16[128,64]{0,1:T(8,128)(2,1)}, u32[]{:S(2)}) copy-start(bf16[128,64]{0,1:T(8,128)(2,1)} %param.24) | copy-start | bytes 49156
  61.2 19.5 %copy-start.3 = (bf16[128,128]{1,0:T(8,128)(2,1)S(1)}, bf16[128,128]{1,0:T(8,128)(2,1)}, u32[]{:S(2)}) copy-start(bf16[128,128]{1,0:T(8,128)(2,1)} %out_weight.1) | copy-start | bytes 98308
  80.6 0.7 copy-start.9
  80.6 0.7 copy-start.10
  80.6 0.7 copy-start.11
  95.5 15.7 %all-to-all-start.3 = ((bf16[8,72,128]{2,1,0:T(8,128)(2,1)}), bf16[8,72,128]{2,1,0:T(8,128)(2,1)S(1)}, u32[]{:S(2)}, u32[]{:S(2)}) async-start(bf16[8,72,128]{2,1,0:T(8,128)(2,1)} %bitcast.17), calls=%async_computation.3 | async-start | bytes 294912 | tf_op jit(solution)/shard_map/all_to_all | solution.py:273

commit v4 on v3

v4 whole, which is shorter than its diff:
```python
import jax
import jax.numpy as jnp
from jax import lax
from jax.experimental import pallas as pl
from jax.experimental.pallas import tpu as pltpu
from jax.sharding import Mesh
from jax.sharding import PartitionSpec as P

EVERY = ("zhi", "core", "y", "zlo", "x")
GROUP = ("y", "zlo", "x")
PLANE = ("y", "x")
BF16, F32 = jnp.bfloat16, jnp.float32
TN = (((0,), (0,)), ((), ()))
NT = (((1,), (1,)), ((), ()))
NN = (((1,), (0,)), ((), ()))
TT = (((0,), (1,)), ((), ()))


def dot(left, right, dims):
    return lax.dot_general(left, right, dims, preferred_element_type=F32)


def norm_lanes(values, gain, bias):
    center = jnp.mean(values, axis=1, keepdims=True)
    spread = jnp.mean(jnp.square(values - center), axis=1, keepdims=True)
    return (values - center) * lax.rsqrt(spread + 1e-05) * gain + bias


def picker(parity):
    rows = lax.broadcasted_iota(jnp.int32, (128, 256), 0)
    columns = lax.broadcasted_iota(jnp.int32, (128, 256), 1)
    return (columns == 2 * rows + parity).astype(F32).astype(BF16)


def pack_kernel(
    place, pair_far, targets_far, mask_far, gain_far, bias_far, weight_far, send,
    pair, targets, mask, gain, bias, in_weight, flat, marks, rows, sems,
):
    far = (targets_far, mask_far, pair_far, gain_far, bias_far, weight_far)
    near = (targets, mask, pair, gain, bias, in_weight)
    copies = [pltpu.make_async_copy(far[n], near[n], sems.at[n]) for n in range(6)]
    for copy in copies:
        copy.start()
    copies[0].wait()
    copies[1].wait()
    lower = lax.broadcasted_iota(jnp.int32, (128, 128), 0) * 2 <= place[0]
    maskf = mask[...].astype(F32)
    targetsf = targets[...].astype(F32)
    marks[...] = jnp.zeros_like(marks)
    for form, row, jr in ((0, 0, 0), (1, 2, 0), (2, 0, 0), (2, 2, 1)):
        marks[form, row : row + 1, :] = targetsf[jr : jr + 1]
        marks[form, row + 1 : row + 2, :] = maskf[jr : jr + 1]
    rows[pl.ds(10, 128, stride=12), :] = jnp.where(
        lower,
        dot(picker(0), marks[0].astype(BF16), NT) + dot(picker(1), marks[1].astype(BF16), NT),
        dot(picker(1), marks[2].astype(BF16), NT),
    )
    rows[pl.ds(11, 128, stride=12), :] = jnp.zeros((128, 128), F32)
    copies[2].wait()
    flat[...] = pair[...].astype(F32)
    first, second, third = (
        flat[pl.ds(jr * 256 + ir, 128, stride=2), :] for ir, jr in ((0, 0), (1, 0), (1, 1))
    )
    rows[pl.ds(8, 128, stride=12), :] = jnp.where(lower, first, second)
    rows[pl.ds(9, 128, stride=12), :] = jnp.where(lower, second, third)
    for copy in copies[3:]:
        copy.wait()
    for r in range(2):
        normed = norm_lanes(flat[r * 256 : (r + 1) * 256, :], gain[...], bias[...]).astype(BF16)
        proj = dot(in_weight[...], normed, TT)
        projected = proj[:256] * jax.nn.sigmoid(proj[256:]) * maskf[r : r + 1]
        for side in range(2):
            for half in range(2):
                rows[pl.ds(side * 4 + r * 2 + half, 128, stride=12), :] = projected[
                    side * 128 : (side + 1) * 128, half * 128 : (half + 1) * 128
                ]
    send[...] = rows[...].astype(BF16)


def triangle_kernel(got, send, rows, products):
    rows[...] = got[...].astype(F32)
    sides = []
    for side in range(2):
        for r in range(2):
            halves = [rows[pl.ds(side * 4 + r * 2 + half, 128, stride=12), :] for half in range(2)]
            sides.append(jnp.concatenate(halves, axis=1).astype(BF16))
    for r in range(2):
        for jr in range(2):
            products[pl.ds(r * 2 + jr, 128, stride=6), :] = dot(sides[r], sides[2 + jr], NT)
    first, second, third = (
        dot(sides[2 + r], sides[jr], NT) for r, jr in ((0, 0), (1, 0), (1, 1))
    )
    higher = lax.broadcasted_iota(jnp.int32, (128, 128), 1) >= lax.broadcasted_iota(
        jnp.int32, (128, 128), 0
    )
    products[pl.ds(4, 128, stride=6), :] = jnp.where(higher, first, second)
    products[pl.ds(5, 128, stride=6), :] = jnp.where(higher, second, third)
    send[...] = products[...].astype(BF16)


def gate_kernel(
    pair, got, targets, mask, chain, place, gain, bias, gate_weight, out_gain, out_bias, dist_bias,
    base, gate, marks, flat, rows, own,
):
    marks[...] = jnp.zeros((24, 128), F32)
    marks[16:17, :] = out_gain[...]
    marks[17:18, :] = out_bias[...]
    marks[18:19, :64] = dist_bias[...]
    flat[...] = pair[...].astype(F32)
    rows[...] = got[...].astype(F32)
    for block in range(4):
        base[block * 128 : (block + 1) * 128, :] = flat[
            pl.ds(block // 2 * 256 + block % 2, 128, stride=2), :
        ]
    base[512:640, :] = rows[pl.ds(8, 128, stride=12), :]
    base[640:768, :] = rows[pl.ds(9, 128, stride=12), :]
    normed = norm_lanes(base[...], gain[...], bias[...]).astype(BF16)
    gate[...] = jax.nn.sigmoid(dot(normed, gate_weight[...], NN))
    own[...] = jnp.zeros_like(own)
    own[0:2, :] = targets[...].astype(F32)
    own[2:4, :] = mask[...].astype(F32)
    columns = lax.broadcasted_iota(jnp.int32, (1, 256), 1)
    for r in range(2):
        here = jnp.sum(jnp.where(columns == place[0] + r, chain[...], 0), axis=1, keepdims=True)
        own[4 + r : 5 + r, :] = 1.0 + (chain[...] != here).astype(F32)
    even, odd = (dot(own[...].astype(BF16), picker(jr), NT) for jr in range(2))
    back = jnp.transpose(rows[pl.ds(10, 128, stride=12), :])
    lanes = lax.broadcasted_iota(jnp.int32, (1, 128), 1) * 2
    higher, same = lanes >= place[0], lanes == place[0]
    target, valid, factor = (
        (
            jnp.where(higher, even[at : at + 1], even[at + 1 : at + 2]),
            jnp.where(higher, even[at + 1 : at + 2], odd[at + 1 : at + 2]),
            odd[at + 1 : at + 2],
        )
        for at in (0, 2, 4)
    )
    for group in range(2):
        marks[group : group + 1, :] = valid[group] * factor[group]
        marks[3 + group : 4 + group, :] = back[2 * group + 1 : 2 * group + 2] * factor[group]
        marks[9 + group : 10 + group, :] = back[2 * group : 2 * group + 1]
    alone = jnp.where(same, valid[2] * factor[2], 0.0)
    marks[2:3, :] = alone
    marks[5:6, :] = alone
    for group in range(3):
        marks[6 + group : 7 + group, :] = target[group]
    marks[11:12, :] = target[2]
    marks[12:13, :] = jnp.where(same, 0.0, back[1:2] * factor[0])


def message(weights, loss, others):
    row = lax.broadcasted_iota(jnp.int32, (8, 128), 0)
    high = loss.astype(BF16).astype(F32)
    terms = jnp.where(row == 0, high, jnp.where(row == 1, loss - high, 0.0))
    pieces = [piece for other in others for piece in (weights, terms, other)]
    return jnp.concatenate(pieces, axis=0).astype(BF16)


def add_sums(values, peers):
    sums = jnp.sum(values.reshape(peers, values.shape[0] // peers, 128), axis=0)
    return sums[:64], sums[64:65, 0:1] + sums[65:66, 0:1]


def head_kernel(
    got, base, gate, marks, place, out_weight, dist_weight, updated, grad, total, hidden, slopes
):
    hidden[...] = got[...].astype(F32)
    columns = jnp.transpose(marks[16:24, :])
    gain, bias, dist_bias = columns[:, 0:1], columns[:, 1:2], columns[:64, 2:3]
    q = []
    kept = []
    for block in range(6):
        here = hidden[pl.ds(block, 128, stride=6), :]
        center = jnp.mean(here, axis=0, keepdims=True)
        spread = jnp.mean(jnp.square(here - center), axis=0, keepdims=True)
        normed = (here - center) * lax.rsqrt(spread + 1e-05)
        normed = (normed * gain + bias).astype(BF16)
        update = dot(normed, out_weight[...], TN)
        at = pl.ds(block * 128, 128)
        sums = (base[at, :] + gate[at, :] * update).astype(BF16)
        q.append(dot(dist_weight[...], sums, NT))
        kept.append(sums)
        if block < 4:
            updated[at, :] = sums
    lanes = lax.broadcasted_iota(jnp.int32, (64, 128), 1) * 2
    higher = lanes >= place[0]
    pairs = (
        jnp.where(higher, q[0], q[2]) + q[4],
        jnp.where(higher, q[2], q[3]) + q[5],
        q[3] + q[3],
    )
    bins = lax.broadcasted_iota(jnp.int32, (64, 128), 0).astype(F32)
    row = lambda at: marks[at : at + 1, :]
    losses = jnp.zeros((1, 128), F32)
    slope = []
    for group in range(3):
        logits = pairs[group] + dist_bias
        shifted = logits - jnp.max(logits, axis=0, keepdims=True)
        powers = jnp.exp(shifted)
        norms = jnp.sum(powers, axis=0, keepdims=True)
        log_probs = shifted - jnp.log(norms)
        probs = powers / norms
        onehot = (bins == row(6 + group)).astype(F32)
        onehot_back = (bins == row(9 + group)).astype(F32)
        losses = losses - row(group) * jnp.sum(onehot * log_probs, axis=0, keepdims=True)
        if group < 2:
            counted = row(12) if group == 0 else row(4)
            losses = losses - counted * jnp.sum(onehot_back * log_probs, axis=0, keepdims=True)
        slope.append(row(group) * (probs - onehot) + row(3 + group) * (probs - onehot_back))
    blocks = (
        (0, jnp.where(higher, slope[0], 0.0)),
        (2, jnp.where(higher, slope[1], slope[0])),
        (3, jnp.where(higher, 0.0, slope[1]) + slope[2]),
        (4, jnp.where(lanes == place[0], 0.0, slope[0])),
        (5, slope[1]),
    )
    weights = jnp.zeros((64, 128), F32)
    for block, values in blocks:
        high = values.astype(BF16)
        low = (values - high.astype(F32)).astype(BF16)
        weights = weights + dot(high, kept[block], NN) + dot(low, kept[block], NN)
    for n in range(3):
        grad[n * 64 : (n + 1) * 64, :] = blocks[n][1]
    slopes[...] = jnp.transpose(jnp.concatenate(slope[:2], axis=0))
    others = [slopes[pl.ds(y * 32 + x, 8, stride=4), :] for y in range(4) for x in range(4)]
    total[...] = message(weights, jnp.sum(losses, axis=1, keepdims=True), others)


def middle_kernel(got, send, values):
    values[...] = got[...].astype(F32)
    weights, loss = add_sums(values[...], 16)
    send[...] = message(weights, loss, [values[pl.ds(72 + z, 16, stride=80), :] for z in range(8)])


def output_kernel(updated, grad, dist_weight, pair_out, part, rows):
    for block in range(4):
        rows[pl.ds(block // 2 * 256 + block % 2, 128, stride=2), :] = updated[
            block * 128 : (block + 1) * 128, :
        ].astype(F32)
    pair_out[...] = rows[...].astype(BF16)
    part[128:256, :] = jnp.zeros((128, 128), F32)
    for n, block in enumerate((0, 2, 3)):
        slope = grad[n * 64 : (n + 1) * 64, :]
        high = slope.astype(BF16)
        low = (slope - high.astype(F32)).astype(BF16)
        part[block * 128 : (block + 1) * 128, :] = dot(high, dist_weight[...], TN) + dot(
            low, dist_weight[...], TN
        )


def last_kernel(got, part, place, dist_weight, grad_weight, loss, grad_pair, values, slopes):
    values[...] = got[...].astype(F32)
    for z in range(8):
        for y in range(4):
            at = z * 88 + 72 + y * 4
            slopes[y * 32 + z * 4 : y * 32 + z * 4 + 4, :] = values[at : at + 4, :]
    there = slopes[...].astype(BF16)
    none = jnp.zeros((64, 128), BF16)
    first = dot(there, jnp.concatenate([dist_weight[...], none], axis=0), NN)
    second = dot(there, jnp.concatenate([none, dist_weight[...]], axis=0), NN)
    device = lax.broadcasted_iota(jnp.int32, (128, 128), 0) * 2
    added = (
        jnp.where(device < place[0], first, 0.0),
        jnp.where(device <= place[0], second, first),
        None,
        jnp.where(device > place[0], second, 0.0),
    )
    for block in range(4):
        sums = part[block * 128 : (block + 1) * 128, :]
        grad_pair[pl.ds(block // 2 * 256 + block % 2, 128, stride=2), :] = (
            sums if added[block] is None else sums + added[block]
        )
    weights, total = add_sums(values[...], 8)
    grad_weight[...] = weights * (1.0 / 256)
    loss[0] = total[0, 0] * (1.0 / 65536)


def run(kernel, outs, scratch, args, room=24, **specs):
    shapes = [jax.ShapeDtypeStruct(s, d) for s, d in outs]
    moved = sum(x.size * x.dtype.itemsize for x in args)
    scratch = [pltpu.VMEM(*s) if isinstance(s, tuple) else s for s in scratch]
    return pl.pallas_call(
        kernel,
        out_shape=shapes,
        scratch_shapes=scratch,
        compiler_params=pltpu.CompilerParams(vmem_limit_bytes=room * 1024 * 1024),
        cost_estimate=pl.CostEstimate(flops=10_000_000, bytes_accessed=moved, transcendentals=0),
        **specs,
    )(*args)


VMEM, FAR = pl.BlockSpec(memory_space=pltpu.VMEM), pl.BlockSpec(memory_space=pl.ANY)
SMEM = pl.BlockSpec(memory_space=pltpu.SMEM)


def pack(*args):
    scratch = [
        ((512, 128), BF16),
        ((2, 256), jnp.int32),
        ((2, 256), jnp.int32),
        ((1, 128), F32),
        ((1, 128), F32),
        ((128, 512), BF16),
        ((512, 128), F32),
        ((3, 128, 256), F32),
        ((1536, 128), F32),
        pltpu.SemaphoreType.DMA((6,)),
    ]
    specs = [SMEM] + [FAR] * 6
    return run(pack_kernel, [((1536, 128), BF16)], scratch, args, 60, in_specs=specs)[0]


def triangle(got):
    scratch = [((1536, 128), F32), ((768, 128), F32)]
    return run(triangle_kernel, [((768, 128), BF16)], scratch, (got,))[0]


def gates(*args):
    outs = [((768, 128), F32), ((768, 128), F32), ((24, 128), F32)]
    scratch = [((512, 128), F32), ((1536, 128), F32), ((16, 256), F32)]
    return run(gate_kernel, outs, scratch, args, in_specs=[VMEM] * 5 + [SMEM] + [VMEM] * 6)


def head(*args):
    outs = [((512, 128), BF16), ((192, 128), F32), ((1280, 128), BF16)]
    scratch = [((768, 128), F32), ((128, 128), F32)]
    return run(head_kernel, outs, scratch, args, in_specs=[VMEM] * 4 + [SMEM] + [VMEM] * 2)


def middle(got):
    return run(middle_kernel, [((704, 128), BF16)], [((1280, 128), F32)], (got,))[0]


def outputs(updated, grad, dist_weight):
    outs = [((512, 128), BF16), ((512, 128), F32)]
    return run(output_kernel, outs, [((512, 128), F32)], (updated, grad, dist_weight))


def last(*args):
    outs = [((64, 128), F32), ((1,), F32), ((512, 128), F32)]
    scratch = [((704, 128), F32), ((128, 128), F32)]
    specs = {"in_specs": [VMEM, VMEM, SMEM, VMEM], "out_specs": [VMEM, SMEM, VMEM]}
    return run(last_kernel, outs, scratch, args, **specs)


def exchange(values, axes):
    return lax.all_to_all(values, axes, 0, 0, tiled=True)


def on_device(
    pair,
    chain,
    targets,
    pair_mask,
    ln_in_gain,
    ln_in_bias,
    in_weight,
    out_gate_weight,
    ln_out_gain,
    ln_out_bias,
    out_weight,
    dist_weight,
    dist_bias,
):
    flat = pair.reshape(512, 128)
    gain, bias = ln_in_gain.reshape(1, 128), ln_in_bias.reshape(1, 128)
    place = (lax.axis_index(GROUP) * 2).reshape(1)
    dist_weight = jnp.swapaxes(dist_weight, 0, 1)

    send = pack(place, flat, targets, pair_mask, gain, bias, in_weight)
    got = exchange(send.reshape(128, 6, 2, 128), GROUP).reshape(1536, 128)
    products = triangle(got)
    base, gate, marks = gates(
        flat, got, targets, pair_mask, chain.reshape(1, 256), place, gain, bias, out_gate_weight,
        ln_out_gain.reshape(1, 128), ln_out_bias.reshape(1, 128), dist_bias.reshape(1, 64),
    )
    hidden = exchange(products.reshape(128, 3, 2, 128), GROUP).reshape(768, 128)
    updated, grad, total = head(hidden, base, gate, marks, place, out_weight, dist_weight)
    total = middle(exchange(total.reshape(16, 80, 128), PLANE).reshape(1280, 128))
    pair_out, part = outputs(updated, grad, dist_weight)
    total = exchange(total.reshape(8, 88, 128), "zlo").reshape(704, 128)
    grad_weight, loss, grad_pair = last(total, part, place, dist_weight)
    return (
        pair_out.reshape(2, 256, 128),
        grad_pair.reshape(2, 256, 128),
        jnp.swapaxes(grad_weight, 0, 1),
        loss,
    )


def solution(mesh):
    fine = Mesh(mesh.devices.reshape(2, 2, 4, 8, 4), EVERY)
    part = ("zhi", "core")
    in_specs = (
        P(EVERY, None, None),
        P(part),
        P(EVERY, None),
        P(EVERY, None),
        P(),
        P(),
        P(),
        P(),
        P(),
        P(),
        P(),
        P(part, None),
        P(),
    )
    out_specs = (
        P(EVERY, None, None),
        P(EVERY, None, None),
        P(part, None),
        P(part),
    )
    return jax.shard_map(
        on_device, mesh=fine, in_specs=in_specs, out_specs=out_specs, check_vma=False
    )
```

time: 112 us -> 107 us (0.955)
  the two profiles are of different devices: /device:TPU:2 before, /device:TPU:32 now
where the time goes in v4:
time: 107 us; the launch traced here: 106 us
  blocking collectives  56.8 us (53%)
  waiting for transfers between devices  26.3 us (25%)
  starting transfers between devices  14.1 us (13%)
  Pallas kernels  7.75 us (7%)
    all_to_all x2, blocking collectives, exchange(): return lax.all_to_all(values, axes, 0, 0, tiled=True)  56.8 us
    all_to_all x2, waiting for transfers between devices, exchange(): return lax.all_to_all(values, axes, 0, 0, tiled=True)  26.3 us
    all_to_all x2, starting transfers between devices, exchange(): return lax.all_to_all(values, axes, 0, 0, tiled=True)  14.1 us
    pallas_call x7, Pallas kernels, run(): pl.pallas_call(kernel, out_shape=shapes, scratch_shapes=scratch, compiler...  7.75 us
  transfers between devices with their start and end apart: 2, of which 2 were waited for; matrix products, arithmetic and copies ran while one was open for 0% of the time, Pallas kernels for 1%

profile of v4, /device:TPU:32, one launch (start us, length us, event | category | flops | bytes accessed | tf_op | source)
XLA Modules:
  0.0 106.4 jit_solution(2098498341934632762)
XLA Ops:
  0.6 2.4 %shard_map.156 = bf16[1536,128]{1,0:T(8,128)(2,1)} custom-call(s32[1]{0:T(128)} %bitcast.place, bf16[512,128]{1,0:T(8,128)(2,1)} %bitcast.25, s32[2,256]{1,0:T(2,128)} %targets.1, s32[2,256]{1,0:T(2,128)} %mask.1, f32[1,128]{1,0:T(1,128)} %bitcast.31, f32[1,128]{1,0:T(1,128)} %bitcast.33, bf16[128,512]{1,0:T(8,128)(2,1)} %weight_far.1), custom_call_target="tpu_custom_call" | custom-call | flops 10000000 | bytes 267268 | tf_op jit(solution)/shard_map/pallas_call | solution.py:282
  3.0 44.4 %all_to_all.20 = bf16[128,6,2,128]{3,2,1,0:T(2,128)(2,1)S(1)} all-to-all(bf16[128,6,2,128]{3,2,1,0:T(2,128)(2,1)} %bitcast.39), channel_id=1, replica_groups=mesh['zhi'=2,'core'=2,'y'=4,'zlo'=8,'x'=4] {'y','zlo','x'}, dimensions={0} | all-to-all | bytes 786432 | tf_op jit(solution)/shard_map/all_to_all | solution.py:347
  47.4 1.0 shard_map.157
  48.4 0.0 copy-start
  48.4 0.0 copy-start.2
  48.4 0.0 copy-start.8
  48.4 0.0 copy-start.10
  48.4 0.0 copy-start.11
  48.5 8.8 %all-to-all-start.1 = ((bf16[128,3,2,128]{3,2,1,0:T(2,128)(2,1)}), bf16[128,3,2,128]{3,2,1,0:T(2,128)(2,1)S(1)}, u32[]{:S(2)}, u32[]{:S(2)}) async-start(bf16[128,3,2,128]{3,2,1,0:T(2,128)(2,1)} %bitcast.6), calls=%async_computation.1 | async-start | bytes 393216 | tf_op jit(solution)/shard_map/all_to_all | solution.py:347
  57.3 0.0 copy-start.5
  57.3 0.0 copy-start.4
  57.3 0.0 copy-start.6
  57.3 0.0 copy-start.7
  57.3 0.0 copy-start.9
  57.3 0.0 copy-done
  57.3 0.0 copy-done.2
  57.4 0.0 copy-done.8
  57.4 0.0 copy-done.10
  57.4 0.0 copy-done.11
  57.4 0.6 copy-done.5
  58.0 0.0 copy-done.4
  58.0 0.0 copy-done.6
  58.0 0.0 copy-done.7
  58.0 0.0 copy-done.9
  58.0 0.0 copy-start.1
  58.0 0.0 copy-start.3
  58.0 0.5 shard_map.158
  58.5 16.0 %all-to-all-done.1 = bf16[128,3,2,128]{3,2,1,0:T(2,128)(2,1)S(1)} async-done(((bf16[128,3,2,128]{3,2,1,0:T(2,128)(2,1)}), bf16[128,3,2,128]{3,2,1,0:T(2,128)(2,1)S(1)}, u32[]{:S(2)}, u32[]{:S(2)}) %all-to-all-start.1) | async-done | bytes 196640 | tf_op jit(solution)/shard_map/all_to_all | solution.py:347
  74.5 0.0 copy-done.1
  74.5 0.0 copy-done.3
  74.5 1.4 %shard_map.159 = (bf16[512,128]{1,0:T(8,128)(2,1)S(1)}, f32[192,128]{1,0:T(8,128)S(1)}, bf16[1280,128]{1,0:T(8,128)(2,1)S(1)}) custom-call(bf16[768,128]{1,0:T(8,128)(2,1)S(1)} %bitcast.23, f32[768,128]{1,0:T(8,128)S(1)} %get-tuple-element.15.base, f32[768,128]{1,0:T(8,128)S(1)} %get-tuple-element.16.gate, f32[24,128]{1,0:T(8,128)S(1)} %get-tuple-element.17.marks, ...), custom_call_target="tpu_custom_call" | custom-call | flops 10000000 | bytes 1044484 | tf_op jit(solution)/shard_map/pallas_call | solution.py:282
  75.9 12.4 %all_to_all.21 = bf16[16,80,128]{2,1,0:T(8,128)(2,1)S(1)} all-to-all(bf16[16,80,128]{2,1,0:T(8,128)(2,1)S(1)} %bitcast.27), channel_id=1, replica_groups=mesh['zhi'=2,'core'=2,'y'=4,'zlo'=8,'x'=4] {'y','x'}, dimensions={0} | all-to-all | bytes 655360 | tf_op jit(solution)/shard_map/all_to_all | solution.py:347
  88.3 0.8 shard_map.161
  89.1 5.3 %all-to-all-start.3 = ((bf16[8,88,128]{2,1,0:T(8,128)(2,1)}), bf16[8,88,128]{2,1,0:T(8,128)(2,1)S(1)}, u32[]{:S(2)}, u32[]{:S(2)}) async-start(bf16[8,88,128]{2,1,0:T(8,128)(2,1)} %bitcast.16), calls=%async_computation.3 | async-start | bytes 360448 | tf_op jit(solution)/shard_map/all_to_all | solution.py:347
  94.4 0.8 shard_map.160
  95.2 10.3 %all-to-all-done.3 = bf16[8,88,128]{2,1,0:T(8,128)(2,1)S(1)} async-done(((bf16[8,88,128]{2,1,0:T(8,128)(2,1)}), bf16[8,88,128]{2,1,0:T(8,128)(2,1)S(1)}, u32[]{:S(2)}, u32[]{:S(2)}) %all-to-all-start.3) | async-done | bytes 180256 | tf_op jit(solution)/shard_map/all_to_all | solution.py:347
  105.5 0.9 shard_map.162
Async XLA Ops:
  48.4 8.9 %copy-start = (bf16[2,256,128]{2,1,0:T(8,128)(2,1)S(1)}, bf16[2,256,128]{2,1,0:T(8,128)(2,1)}, u32[]{:S(2)}) copy-start(bf16[2,256,128]{2,1,0:T(8,128)(2,1)} %param.13) | copy-start | bytes 393220
  48.4 8.9 %copy-start.2 = (bf16[128,128]{1,0:T(8,128)(2,1)S(1)}, bf16[128,128]{1,0:T(8,128)(2,1)}, u32[]{:S(2)}) copy-start(bf16[128,128]{1,0:T(8,128)(2,1)} %gate_weight.1) | copy-start | bytes 98308
  48.4 8.9 %copy-start.8 = (s32[256]{0:T(256)S(1)}, s32[256]{0:T(256)}, u32[]{:S(2)}) copy-start(s32[256]{0:T(256)} %param.14) | copy-start | bytes 3076
  48.4 8.9 %copy-start.10 = (f32[128]{0:T(128)S(1)}, f32[128]{0:T(128)}, u32[]{:S(2)}) copy-start(f32[128]{0:T(128)} %param.22) | copy-start | bytes 1540
  48.4 8.9 %copy-start.11 = (f32[64]{0:T(128)S(1)}, f32[64]{0:T(128)}, u32[]{:S(2)}) copy-start(f32[64]{0:T(128)} %param.25) | copy-start | bytes 772
  48.5 26.0 %all-to-all-start.1 = ((bf16[128,3,2,128]{3,2,1,0:T(2,128)(2,1)}), bf16[128,3,2,128]{3,2,1,0:T(2,128)(2,1)S(1)}, u32[]{:S(2)}, u32[]{:S(2)}) async-start(bf16[128,3,2,128]{3,2,1,0:T(2,128)(2,1)} %bitcast.6), calls=%async_computation.1 | async-start | bytes 393216 | tf_op jit(solution)/shard_map/all_to_all | solution.py:347
  57.3 0.7 copy-start.5
  57.3 0.7 copy-start.4
  57.3 0.7 copy-start.6
  57.3 0.7 copy-start.7
  57.3 0.7 copy-start.9
  58.0 16.5 %copy-start.1 = (bf16[128,64]{0,1:T(8,128)(2,1)S(1)}, bf16[128,64]{0,1:T(8,128)(2,1)}, u32[]{:S(2)}) copy-start(bf16[128,64]{0,1:T(8,128)(2,1)} %param.24) | copy-start | bytes 49156
  58.0 16.5 %copy-start.3 = (bf16[128,128]{1,0:T(8,128)(2,1)S(1)}, bf16[128,128]{1,0:T(8,128)(2,1)}, u32[]{:S(2)}) copy-start(bf16[128,128]{1,0:T(8,128)(2,1)} %out_weight.1) | copy-start | bytes 98308
  89.1 16.4 %all-to-all-start.3 = ((bf16[8,88,128]{2,1,0:T(8,128)(2,1)}), bf16[8,88,128]{2,1,0:T(8,128)(2,1)S(1)}, u32[]{:S(2)}, u32[]{:S(2)}) async-start(bf16[8,88,128]{2,1,0:T(8,128)(2,1)} %bitcast.16), calls=%async_computation.3 | async-start | bytes 360448 | tf_op jit(solution)/shard_map/all_to_all | solution.py:347

commit v5 on v4

--- a/solution.py
+++ b/solution.py
@@ -33,36 +33,33 @@
 
 
 def pack_kernel(
-    place, pair_far, targets_far, mask_far, gain_far, bias_far, weight_far, send,
-    pair, targets, mask, gain, bias, in_weight, flat, marks, rows, sems,
+    place, pair_far, targets_far, mask_far, gain_far, bias_far, weight_far, send, labels,
+    pair, targets, mask, gain, bias, in_weight, flat, rows, sems,
 ):
     far = (targets_far, mask_far, pair_far, gain_far, bias_far, weight_far)
     near = (targets, mask, pair, gain, bias, in_weight)
     copies = [pltpu.make_async_copy(far[n], near[n], sems.at[n]) for n in range(6)]
     for copy in copies:
         copy.start()
+    lower = lax.broadcasted_iota(jnp.int32, (128, 128), 0) * 2 <= place[0]
+    even, odd = picker(0), picker(1)
     copies[0].wait()
     copies[1].wait()
-    lower = lax.broadcasted_iota(jnp.int32, (128, 128), 0) * 2 <= place[0]
     maskf = mask[...].astype(F32)
-    targetsf = targets[...].astype(F32)
-    marks[...] = jnp.zeros_like(marks)
-    for form, row, jr in ((0, 0, 0), (1, 2, 0), (2, 0, 0), (2, 2, 1)):
-        marks[form, row : row + 1, :] = targetsf[jr : jr + 1]
-        marks[form, row + 1 : row + 2, :] = maskf[jr : jr + 1]
-    rows[pl.ds(10, 128, stride=12), :] = jnp.where(
-        lower,
-        dot(picker(0), marks[0].astype(BF16), NT) + dot(picker(1), marks[1].astype(BF16), NT),
-        dot(picker(1), marks[2].astype(BF16), NT),
-    )
-    rows[pl.ds(11, 128, stride=12), :] = jnp.zeros((128, 128), F32)
+    label = jnp.where(mask[...] > 0, targets[...].astype(F32), 64.0)
+    first, second, third = (
+        dot(picked, jnp.broadcast_to(label[jr : jr + 1], (128, 256)).astype(BF16), NT)
+        for picked, jr in ((even, 0), (odd, 0), (odd, 1))
+    )
+    labels[0:128, :] = jnp.where(lower, first, second)
+    labels[128:256, :] = jnp.where(lower, second, third)
     copies[2].wait()
     flat[...] = pair[...].astype(F32)
     first, second, third = (
         flat[pl.ds(jr * 256 + ir, 128, stride=2), :] for ir, jr in ((0, 0), (1, 0), (1, 1))
     )
-    rows[pl.ds(8, 128, stride=12), :] = jnp.where(lower, first, second)
-    rows[pl.ds(9, 128, stride=12), :] = jnp.where(lower, second, third)
+    rows[pl.ds(8, 128, stride=10), :] = jnp.where(lower, first, second)
+    rows[pl.ds(9, 128, stride=10), :] = jnp.where(lower, second, third)
     for copy in copies[3:]:
         copy.wait()
     for r in range(2):
@@ -71,18 +68,18 @@
         projected = proj[:256] * jax.nn.sigmoid(proj[256:]) * maskf[r : r + 1]
         for side in range(2):
             for half in range(2):
-                rows[pl.ds(side * 4 + r * 2 + half, 128, stride=12), :] = projected[
+                rows[pl.ds(side * 4 + r * 2 + half, 128, stride=10), :] = projected[
                     side * 128 : (side + 1) * 128, half * 128 : (half + 1) * 128
                 ]
     send[...] = rows[...].astype(BF16)
 
 
-def triangle_kernel(got, send, rows, products):
+def triangle_kernel(got, labels, send, rows, products):
     rows[...] = got[...].astype(F32)
     sides = []
     for side in range(2):
         for r in range(2):
-            halves = [rows[pl.ds(side * 4 + r * 2 + half, 128, stride=12), :] for half in range(2)]
+            halves = [rows[pl.ds(side * 4 + r * 2 + half, 128, stride=10), :] for half in range(2)]
             sides.append(jnp.concatenate(halves, axis=1).astype(BF16))
     for r in range(2):
         for jr in range(2):
@@ -90,11 +87,14 @@
     first, second, third = (
         dot(sides[2 + r], sides[jr], NT) for r, jr in ((0, 0), (1, 0), (1, 1))
     )
-    higher = lax.broadcasted_iota(jnp.int32, (128, 128), 1) >= lax.broadcasted_iota(
-        jnp.int32, (128, 128), 0
-    )
-    products[pl.ds(4, 128, stride=6), :] = jnp.where(higher, first, second)
-    products[pl.ds(5, 128, stride=6), :] = jnp.where(higher, second, third)
+    lane = lax.broadcasted_iota(jnp.int32, (128, 128), 1)
+    device = lax.broadcasted_iota(jnp.int32, (128, 128), 0)
+    products[pl.ds(4, 128, stride=6), :] = jnp.where(
+        lane == device, labels[0:128, :], jnp.where(lane > device, first, second)
+    )
+    products[pl.ds(5, 128, stride=6), :] = jnp.where(
+        lane == device, labels[128:256, :], jnp.where(lane > device, second, third)
+    )
     send[...] = products[...].astype(BF16)
 
 
@@ -112,8 +112,8 @@
         base[block * 128 : (block + 1) * 128, :] = flat[
             pl.ds(block // 2 * 256 + block % 2, 128, stride=2), :
         ]
-    base[512:640, :] = rows[pl.ds(8, 128, stride=12), :]
-    base[640:768, :] = rows[pl.ds(9, 128, stride=12), :]
+    base[512:640, :] = rows[pl.ds(8, 128, stride=10), :]
+    base[640:768, :] = rows[pl.ds(9, 128, stride=10), :]
     normed = norm_lanes(base[...], gain[...], bias[...]).astype(BF16)
     gate[...] = jax.nn.sigmoid(dot(normed, gate_weight[...], NN))
     own[...] = jnp.zeros_like(own)
@@ -124,7 +124,6 @@
         here = jnp.sum(jnp.where(columns == place[0] + r, chain[...], 0), axis=1, keepdims=True)
         own[4 + r : 5 + r, :] = 1.0 + (chain[...] != here).astype(F32)
     even, odd = (dot(own[...].astype(BF16), picker(jr), NT) for jr in range(2))
-    back = jnp.transpose(rows[pl.ds(10, 128, stride=12), :])
     lanes = lax.broadcasted_iota(jnp.int32, (1, 128), 1) * 2
     higher, same = lanes >= place[0], lanes == place[0]
     target, valid, factor = (
@@ -137,15 +136,12 @@
     )
     for group in range(2):
         marks[group : group + 1, :] = valid[group] * factor[group]
-        marks[3 + group : 4 + group, :] = back[2 * group + 1 : 2 * group + 2] * factor[group]
-        marks[9 + group : 10 + group, :] = back[2 * group : 2 * group + 1]
+        marks[3 + group : 4 + group, :] = factor[group]
     alone = jnp.where(same, valid[2] * factor[2], 0.0)
     marks[2:3, :] = alone
     marks[5:6, :] = alone
     for group in range(3):
         marks[6 + group : 7 + group, :] = target[group]
-    marks[11:12, :] = target[2]
-    marks[12:13, :] = jnp.where(same, 0.0, back[1:2] * factor[0])
 
 
 def message(weights, loss, others):
@@ -169,8 +165,14 @@
     gain, bias, dist_bias = columns[:, 0:1], columns[:, 1:2], columns[:64, 2:3]
     q = []
     kept = []
+    lanes = lax.broadcasted_iota(jnp.int32, (128, 128), 1) * 2
+    chosen = (lanes[:16] == place[0]).astype(F32).astype(BF16)
+    heres = [hidden[pl.ds(block, 128, stride=6), :] for block in range(6)]
+    labels = [dot(chosen, heres[4 + group].astype(BF16), NT)[0:1] for group in range(2)]
+    for group in range(2):
+        heres[4 + group] = jnp.where(lanes == place[0], heres[group], heres[4 + group])
     for block in range(6):
-        here = hidden[pl.ds(block, 128, stride=6), :]
+        here = heres[block]
         center = jnp.mean(here, axis=0, keepdims=True)
         spread = jnp.mean(jnp.square(here - center), axis=0, keepdims=True)
         normed = (here - center) * lax.rsqrt(spread + 1e-05)
@@ -182,7 +184,7 @@
         kept.append(sums)
         if block < 4:
             updated[at, :] = sums
-    lanes = lax.broadcasted_iota(jnp.int32, (64, 128), 1) * 2
+    lanes = lanes[:64]
     higher = lanes >= place[0]
     pairs = (
         jnp.where(higher, q[0], q[2]) + q[4],
@@ -191,6 +193,10 @@
     )
     bins = lax.broadcasted_iota(jnp.int32, (64, 128), 0).astype(F32)
     row = lambda at: marks[at : at + 1, :]
+    mirrored = [jnp.where(labels[group] < 63.5, row(3 + group), 0.0) for group in range(2)]
+    counted = [jnp.where(lanes[:1] == place[0], 0.0, mirrored[0]), mirrored[1]]
+    mirrored.append(row(5))
+    labels.append(row(8))
     losses = jnp.zeros((1, 128), F32)
     slope = []
     for group in range(3):
@@ -201,12 +207,11 @@
         log_probs = shifted - jnp.log(norms)
         probs = powers / norms
         onehot = (bins == row(6 + group)).astype(F32)
-        onehot_back = (bins == row(9 + group)).astype(F32)
+        onehot_back = (bins == labels[group]).astype(F32)
         losses = losses - row(group) * jnp.sum(onehot * log_probs, axis=0, keepdims=True)
         if group < 2:
-            counted = row(12) if group == 0 else row(4)
-            losses = losses - counted * jnp.sum(onehot_back * log_probs, axis=0, keepdims=True)
-        slope.append(row(group) * (probs - onehot) + row(3 + group) * (probs - onehot_back))
+            losses = losses - counted[group] * jnp.sum(onehot_back * log_probs, axis=0, keepdims=True)
+        slope.append(row(group) * (probs - onehot) + mirrored[group] * (probs - onehot_back))
     blocks = (
         (0, jnp.where(higher, slope[0], 0.0)),
         (2, jnp.where(higher, slope[1], slope[0])),
@@ -226,10 +231,11 @@
     total[...] = message(weights, jnp.sum(losses, axis=1, keepdims=True), others)
 
 
-def middle_kernel(got, send, values):
-    values[...] = got[...].astype(F32)
-    weights, loss = add_sums(values[...], 16)
-    send[...] = message(weights, loss, [values[pl.ds(72 + z, 16, stride=80), :] for z in range(8)])
+def middle_kernel(got, send, slopes):
+    values = got[...].astype(F32)
+    slopes[...] = values.reshape(16, 80, 128)[:, 72:80].reshape(128, 128)
+    weights, loss = add_sums(values, 16)
+    send[...] = message(weights, loss, [slopes[pl.ds(z, 16, stride=8), :] for z in range(8)])
 
 
 def output_kernel(updated, grad, dist_weight, pair_out, part, rows):
@@ -248,12 +254,12 @@
         )
 
 
-def last_kernel(got, part, place, dist_weight, grad_weight, loss, grad_pair, values, slopes):
-    values[...] = got[...].astype(F32)
+def last_kernel(got, part, place, dist_weight, grad_weight, loss, grad_pair, slopes):
+    values = got[...].astype(F32)
     for z in range(8):
         for y in range(4):
             at = z * 88 + 72 + y * 4
-            slopes[y * 32 + z * 4 : y * 32 + z * 4 + 4, :] = values[at : at + 4, :]
+            slopes[y * 32 + z * 4 : y * 32 + z * 4 + 4, :] = values[at : at + 4]
     there = slopes[...].astype(BF16)
     none = jnp.zeros((64, 128), BF16)
     first = dot(there, jnp.concatenate([dist_weight[...], none], axis=0), NN)
@@ -270,12 +276,12 @@
         grad_pair[pl.ds(block // 2 * 256 + block % 2, 128, stride=2), :] = (
             sums if added[block] is None else sums + added[block]
         )
-    weights, total = add_sums(values[...], 8)
+    weights, total = add_sums(values, 8)
     grad_weight[...] = weights * (1.0 / 256)
     loss[0] = total[0, 0] * (1.0 / 65536)
 
 
-def run(kernel, outs, scratch, args, room=24, **specs):
+def run(kernel, outs, scratch, args, **specs):
     shapes = [jax.ShapeDtypeStruct(s, d) for s, d in outs]
     moved = sum(x.size * x.dtype.itemsize for x in args)
     scratch = [pltpu.VMEM(*s) if isinstance(s, tuple) else s for s in scratch]
@@ -283,7 +289,7 @@
         kernel,
         out_shape=shapes,
         scratch_shapes=scratch,
-        compiler_params=pltpu.CompilerParams(vmem_limit_bytes=room * 1024 * 1024),
+        compiler_params=pltpu.CompilerParams(vmem_limit_bytes=24 * 1024 * 1024),
         cost_estimate=pl.CostEstimate(flops=10_000_000, bytes_accessed=moved, transcendentals=0),
         **specs,
     )(*args)
@@ -293,7 +299,7 @@
 SMEM = pl.BlockSpec(memory_space=pltpu.SMEM)
 
 
-def pack(*args):
+def pack(place, *args):
     scratch = [
         ((512, 128), BF16),
         ((2, 256), jnp.int32),
@@ -302,22 +308,22 @@
         ((1, 128), F32),
         ((128, 512), BF16),
         ((512, 128), F32),
-        ((3, 128, 256), F32),
-        ((1536, 128), F32),
+        ((1280, 128), F32),
         pltpu.SemaphoreType.DMA((6,)),
     ]
-    specs = [SMEM] + [FAR] * 6
-    return run(pack_kernel, [((1536, 128), BF16)], scratch, args, 60, in_specs=specs)[0]
-
-
-def triangle(got):
-    scratch = [((1536, 128), F32), ((768, 128), F32)]
-    return run(triangle_kernel, [((768, 128), BF16)], scratch, (got,))[0]
+    outs = [((1280, 128), BF16), ((256, 128), F32)]
+    args = [pltpu.with_memory_space_constraint(arg, pltpu.HBM) for arg in args]
+    return run(pack_kernel, outs, scratch, (place, *args), in_specs=[SMEM] + [FAR] * 6)
+
+
+def triangle(got, labels):
+    scratch = [((1280, 128), F32), ((768, 128), F32)]
+    return run(triangle_kernel, [((768, 128), BF16)], scratch, (got, labels))[0]
 
 
 def gates(*args):
     outs = [((768, 128), F32), ((768, 128), F32), ((24, 128), F32)]
-    scratch = [((512, 128), F32), ((1536, 128), F32), ((16, 256), F32)]
+    scratch = [((512, 128), F32), ((1280, 128), F32), ((16, 256), F32)]
     return run(gate_kernel, outs, scratch, args, in_specs=[VMEM] * 5 + [SMEM] + [VMEM] * 6)
 
 
@@ -328,7 +334,7 @@
 
 
 def middle(got):
-    return run(middle_kernel, [((704, 128), BF16)], [((1280, 128), F32)], (got,))[0]
+    return run(middle_kernel, [((704, 128), BF16)], [((128, 128), F32)], (got,))[0]
 
 
 def outputs(updated, grad, dist_weight):
@@ -338,7 +344,7 @@
 
 def last(*args):
     outs = [((64, 128), F32), ((1,), F32), ((512, 128), F32)]
-    scratch = [((704, 128), F32), ((128, 128), F32)]
+    scratch = [((128, 128), F32)]
     specs = {"in_specs": [VMEM, VMEM, SMEM, VMEM], "out_specs": [VMEM, SMEM, VMEM]}
     return run(last_kernel, outs, scratch, args, **specs)
 
@@ -367,9 +373,9 @@
     place = (lax.axis_index(GROUP) * 2).reshape(1)
     dist_weight = jnp.swapaxes(dist_weight, 0, 1)
 
-    send = pack(place, flat, targets, pair_mask, gain, bias, in_weight)
-    got = exchange(send.reshape(128, 6, 2, 128), GROUP).reshape(1536, 128)
-    products = triangle(got)
+    send, labels = pack(place, flat, targets, pair_mask, gain, bias, in_weight)
+    got = exchange(send.reshape(128, 5, 2, 128), GROUP).reshape(1280, 128)
+    products = triangle(got, labels)
     base, gate, marks = gates(
         flat, got, targets, pair_mask, chain.reshape(1, 256), place, gain, bias, out_gate_weight,
         ln_out_gain.reshape(1, 128), ln_out_bias.reshape(1, 128), dist_bias.reshape(1, 64),

time: 107 us -> 103 us (0.963)
  blocking collectives: 56.8 us -> 54.1 us
    all_to_all x2, blocking collectives: 56.8 us -> 54.1 us  [exchange(): return lax.all_to_all(values, axes, 0, 0, tiled=True)]
where the time goes in v5:
time: 103 us
  blocking collectives  54.1 us (53%)
  waiting for transfers between devices  26.3 us (26%)
  starting transfers between devices  13.9 us (13%)
  Pallas kernels  6.85 us (7%)
    all_to_all x2, blocking collectives, exchange(): return lax.all_to_all(values, axes, 0, 0, tiled=True)  54.1 us
    all_to_all x2, waiting for transfers between devices, exchange(): return lax.all_to_all(values, axes, 0, 0, tiled=True)  26.3 us
    all_to_all x2, starting transfers between devices, exchange(): return lax.all_to_all(values, axes, 0, 0, tiled=True)  13.9 us
    pallas_call x7, Pallas kernels, run(): pl.pallas_call(kernel, out_shape=shapes, scratch_shapes=scratch, compiler...  6.85 us
  transfers between devices with their start and end apart: 2, of which 2 were waited for; matrix products, arithmetic and copies ran while one was open for 0% of the time, Pallas kernels for 1%

profile of v5, /device:TPU:32, one launch (start us, length us, event | category | flops | bytes accessed | tf_op | source)
XLA Modules:
  0.0 102.6 jit_solution(4819721726617637452)
XLA Ops:
  0.6 1.6 %shard_map.156 = (bf16[1280,128]{1,0:T(8,128)(2,1)S(1)}, f32[256,128]{1,0:T(8,128)S(1)}) custom-call(s32[1]{0:T(128)} %bitcast.place, bf16[512,128]{1,0:T(8,128)(2,1)} %bitcast.25, s32[2,256]{1,0:T(2,128)} %targets.1, s32[2,256]{1,0:T(2,128)} %mask.1, f32[1,128]{1,0:T(1,128)} %bitcast.32, f32[1,128]{1,0:T(1,128)} %bitcast.34, bf16[128,512]{1,0:T(8,128)(2,1)} %weight_far.1), custom_call_target="tpu_custom_call" | custom-call | flops 10000000 | bytes 267268 | tf_op jit(solution)/shard_map/pallas_call | solution.py:288
  2.3 41.6 %all_to_all.20 = bf16[128,5,2,128]{3,2,1,0:T(2,128)(2,1)S(1)} all-to-all(bf16[128,5,2,128]{3,2,1,0:T(2,128)(2,1)S(1)} %bitcast.28), channel_id=1, replica_groups=mesh['zhi'=2,'core'=2,'y'=4,'zlo'=8,'x'=4] {'y','zlo','x'}, dimensions={0} | all-to-all | bytes 655360 | tf_op jit(solution)/shard_map/all_to_all | solution.py:353
  43.9 1.0 shard_map.157
  44.9 0.0 copy-start
  44.9 0.0 copy-start.2
  44.9 0.0 copy-start.8
  44.9 0.0 copy-start.10
  44.9 0.0 copy-start.11
  45.0 8.6 %all-to-all-start.1 = ((bf16[128,3,2,128]{3,2,1,0:T(2,128)(2,1)}), bf16[128,3,2,128]{3,2,1,0:T(2,128)(2,1)S(1)}, u32[]{:S(2)}, u32[]{:S(2)}) async-start(bf16[128,3,2,128]{3,2,1,0:T(2,128)(2,1)} %bitcast.6), calls=%async_computation.1 | async-start | bytes 393216 | tf_op jit(solution)/shard_map/all_to_all | solution.py:353
  53.6 0.0 copy-start.5
  53.6 0.0 copy-start.4
  53.6 0.0 copy-start.6
  53.6 0.0 copy-start.7
  53.6 0.0 copy-start.9
  53.7 0.0 copy-done
  53.7 0.0 copy-done.2
  53.7 0.0 copy-done.8
  53.7 0.0 copy-done.10
  53.7 0.0 copy-done.11
  53.7 0.6 copy-done.5
  54.3 0.0 copy-done.4
  54.3 0.0 copy-done.6
  54.3 0.0 copy-done.7
  54.3 0.0 copy-done.9
  54.3 0.0 copy-start.1
  54.3 0.0 copy-start.3
  54.3 0.5 shard_map.158
  54.8 16.0 %all-to-all-done.1 = bf16[128,3,2,128]{3,2,1,0:T(2,128)(2,1)S(1)} async-done(((bf16[128,3,2,128]{3,2,1,0:T(2,128)(2,1)}), bf16[128,3,2,128]{3,2,1,0:T(2,128)(2,1)S(1)}, u32[]{:S(2)}, u32[]{:S(2)}) %all-to-all-start.1) | async-done | bytes 196640 | tf_op jit(solution)/shard_map/all_to_all | solution.py:353
  70.8 0.0 copy-done.1
  70.8 0.0 copy-done.3
  70.8 1.3 %shard_map.159 = (bf16[512,128]{1,0:T(8,128)(2,1)S(1)}, f32[192,128]{1,0:T(8,128)S(1)}, bf16[1280,128]{1,0:T(8,128)(2,1)S(1)}) custom-call(bf16[768,128]{1,0:T(8,128)(2,1)S(1)} %bitcast.23, f32[768,128]{1,0:T(8,128)S(1)} %get-tuple-element.19.base, f32[768,128]{1,0:T(8,128)S(1)} %get-tuple-element.20.gate, f32[24,128]{1,0:T(8,128)S(1)} %get-tuple-element.21.marks, ...), custom_call_target="tpu_custom_call" | custom-call | flops 10000000 | bytes 1044484 | tf_op jit(solution)/shard_map/pallas_call | solution.py:288
  72.1 12.4 %all_to_all.21 = bf16[16,80,128]{2,1,0:T(8,128)(2,1)S(1)} all-to-all(bf16[16,80,128]{2,1,0:T(8,128)(2,1)S(1)} %bitcast.27), channel_id=1, replica_groups=mesh['zhi'=2,'core'=2,'y'=4,'zlo'=8,'x'=4] {'y','x'}, dimensions={0} | all-to-all | bytes 655360 | tf_op jit(solution)/shard_map/all_to_all | solution.py:353
  84.5 0.8 shard_map.161
  85.3 5.3 %all-to-all-start.3 = ((bf16[8,88,128]{2,1,0:T(8,128)(2,1)}), bf16[8,88,128]{2,1,0:T(8,128)(2,1)S(1)}, u32[]{:S(2)}, u32[]{:S(2)}) async-start(bf16[8,88,128]{2,1,0:T(8,128)(2,1)} %bitcast.16), calls=%async_computation.3 | async-start | bytes 360448 | tf_op jit(solution)/shard_map/all_to_all | solution.py:353
  90.6 0.8 shard_map.160
  91.4 10.3 %all-to-all-done.3 = bf16[8,88,128]{2,1,0:T(8,128)(2,1)S(1)} async-done(((bf16[8,88,128]{2,1,0:T(8,128)(2,1)}), bf16[8,88,128]{2,1,0:T(8,128)(2,1)S(1)}, u32[]{:S(2)}, u32[]{:S(2)}) %all-to-all-start.3) | async-done | bytes 180256 | tf_op jit(solution)/shard_map/all_to_all | solution.py:353
  101.7 0.9 shard_map.162
Async XLA Ops:
  44.9 8.7 %copy-start = (bf16[2,256,128]{2,1,0:T(8,128)(2,1)S(1)}, bf16[2,256,128]{2,1,0:T(8,128)(2,1)}, u32[]{:S(2)}) copy-start(bf16[2,256,128]{2,1,0:T(8,128)(2,1)} %param.13) | copy-start | bytes 393220
  44.9 8.7 %copy-start.2 = (bf16[128,128]{1,0:T(8,128)(2,1)S(1)}, bf16[128,128]{1,0:T(8,128)(2,1)}, u32[]{:S(2)}) copy-start(bf16[128,128]{1,0:T(8,128)(2,1)} %gate_weight.1) | copy-start | bytes 98308
  44.9 8.7 %copy-start.8 = (s32[256]{0:T(256)S(1)}, s32[256]{0:T(256)}, u32[]{:S(2)}) copy-start(s32[256]{0:T(256)} %param.14) | copy-start | bytes 3076
  44.9 8.8 %copy-start.10 = (f32[128]{0:T(128)S(1)}, f32[128]{0:T(128)}, u32[]{:S(2)}) copy-start(f32[128]{0:T(128)} %param.22) | copy-start | bytes 1540
  44.9 8.8 %copy-start.11 = (f32[64]{0:T(128)S(1)}, f32[64]{0:T(128)}, u32[]{:S(2)}) copy-start(f32[64]{0:T(128)} %param.25) | copy-start | bytes 772
  45.0 25.9 %all-to-all-start.1 = ((bf16[128,3,2,128]{3,2,1,0:T(2,128)(2,1)}), bf16[128,3,2,128]{3,2,1,0:T(2,128)(2,1)S(1)}, u32[]{:S(2)}, u32[]{:S(2)}) async-start(bf16[128,3,2,128]{3,2,1,0:T(2,128)(2,1)} %bitcast.6), calls=%async_computation.1 | async-start | bytes 393216 | tf_op jit(solution)/shard_map/all_to_all | solution.py:353
  53.6 0.7 copy-start.5
  53.6 0.7 copy-start.4
  53.6 0.7 copy-start.6
  53.6 0.7 copy-start.7
  53.6 0.7 copy-start.9
  54.3 16.5 %copy-start.1 = (bf16[128,64]{0,1:T(8,128)(2,1)S(1)}, bf16[128,64]{0,1:T(8,128)(2,1)}, u32[]{:S(2)}) copy-start(bf16[128,64]{0,1:T(8,128)(2,1)} %param.24) | copy-start | bytes 49156
  54.3 16.5 %copy-start.3 = (bf16[128,128]{1,0:T(8,128)(2,1)S(1)}, bf16[128,128]{1,0:T(8,128)(2,1)}, u32[]{:S(2)}) copy-start(bf16[128,128]{1,0:T(8,128)(2,1)} %out_weight.1) | copy-start | bytes 98308
  85.3 16.4 %all-to-all-start.3 = ((bf16[8,88,128]{2,1,0:T(8,128)(2,1)}), bf16[8,88,128]{2,1,0:T(8,128)(2,1)S(1)}, u32[]{:S(2)}, u32[]{:S(2)}) async-start(bf16[8,88,128]{2,1,0:T(8,128)(2,1)} %bitcast.16), calls=%async_computation.3 | async-start | bytes 360448 | tf_op jit(solution)/shard_map/all_to_all | solution.py:353

commit v6 on v5

--- a/solution.py
+++ b/solution.py
@@ -145,16 +145,18 @@
 
 
 def message(weights, loss, others):
-    row = lax.broadcasted_iota(jnp.int32, (8, 128), 0)
+    row = lax.broadcasted_iota(jnp.int32, (64, 128), 0)
+    lane = lax.broadcasted_iota(jnp.int32, (1, 128), 1)
     high = loss.astype(BF16).astype(F32)
-    terms = jnp.where(row == 0, high, jnp.where(row == 1, loss - high, 0.0))
-    pieces = [piece for other in others for piece in (weights, terms, other)]
+    terms = jnp.where(lane == 0, high, jnp.where(lane == 1, loss - high, 0.0))
+    sums = jnp.where(row == 63, terms, weights)
+    pieces = [piece for other in others for piece in (sums, other)]
     return jnp.concatenate(pieces, axis=0).astype(BF16)
 
 
 def add_sums(values, peers):
-    sums = jnp.sum(values.reshape(peers, values.shape[0] // peers, 128), axis=0)
-    return sums[:64], sums[64:65, 0:1] + sums[65:66, 0:1]
+    sums = jnp.sum(values.reshape(peers, values.shape[0] // peers, 128)[:, :64], axis=0)
+    return sums, sums[63:64, 0:1] + sums[63:64, 1:2]
 
 
 def head_kernel(
@@ -233,7 +235,7 @@
 
 def middle_kernel(got, send, slopes):
     values = got[...].astype(F32)
-    slopes[...] = values.reshape(16, 80, 128)[:, 72:80].reshape(128, 128)
+    slopes[...] = values.reshape(16, 72, 128)[:, 64:72].reshape(128, 128)
     weights, loss = add_sums(values, 16)
     send[...] = message(weights, loss, [slopes[pl.ds(z, 16, stride=8), :] for z in range(8)])
 
@@ -258,7 +260,7 @@
     values = got[...].astype(F32)
     for z in range(8):
         for y in range(4):
-            at = z * 88 + 72 + y * 4
+            at = z * 80 + 64 + y * 4
             slopes[y * 32 + z * 4 : y * 32 + z * 4 + 4, :] = values[at : at + 4]
     there = slopes[...].astype(BF16)
     none = jnp.zeros((64, 128), BF16)
@@ -277,7 +279,10 @@
             sums if added[block] is None else sums + added[block]
         )
     weights, total = add_sums(values, 8)
-    grad_weight[...] = weights * (1.0 / 256)
+    row = lax.broadcasted_iota(jnp.int32, (64, 128), 0)
+    weights = jnp.where(row == 63, 0.0, weights)
+    rest = jnp.sum(weights, axis=0, keepdims=True)
+    grad_weight[...] = jnp.where(row == 63, -rest, weights) * (1.0 / 256)
     loss[0] = total[0, 0] * (1.0 / 65536)
 
 
@@ -328,13 +333,13 @@
 
 
 def head(*args):
-    outs = [((512, 128), BF16), ((192, 128), F32), ((1280, 128), BF16)]
+    outs = [((512, 128), BF16), ((192, 128), F32), ((1152, 128), BF16)]
     scratch = [((768, 128), F32), ((128, 128), F32)]
     return run(head_kernel, outs, scratch, args, in_specs=[VMEM] * 4 + [SMEM] + [VMEM] * 2)
 
 
 def middle(got):
-    return run(middle_kernel, [((704, 128), BF16)], [((128, 128), F32)], (got,))[0]
+    return run(middle_kernel, [((640, 128), BF16)], [((128, 128), F32)], (got,))[0]
 
 
 def outputs(updated, grad, dist_weight):
@@ -382,9 +387,9 @@
     )
     hidden = exchange(products.reshape(128, 3, 2, 128), GROUP).reshape(768, 128)
     updated, grad, total = head(hidden, base, gate, marks, place, out_weight, dist_weight)
-    total = middle(exchange(total.reshape(16, 80, 128), PLANE).reshape(1280, 128))
+    total = middle(exchange(total.reshape(16, 72, 128), PLANE).reshape(1152, 128))
     pair_out, part = outputs(updated, grad, dist_weight)
-    total = exchange(total.reshape(8, 88, 128), "zlo").reshape(704, 128)
+    total = exchange(total.reshape(8, 80, 128), "zlo").reshape(640, 128)
     grad_weight, loss, grad_pair = last(total, part, place, dist_weight)
     return (
         pair_out.reshape(2, 256, 128),

time: 103 us -> 102 us (level)
  the two profiles are of different devices: /device:TPU:32 before, /device:TPU:2 now
where the time goes in v6:
time: 102 us
  blocking collectives  54.4 us (53%)
  waiting for transfers between devices  27.4 us (27%)
  starting transfers between devices  12 us (12%)
  Pallas kernels  6.91 us (7%)
    all_to_all x2, blocking collectives, exchange(): return lax.all_to_all(values, axes, 0, 0, tiled=True)  54.4 us
    all_to_all x2, waiting for transfers between devices, exchange(): return lax.all_to_all(values, axes, 0, 0, tiled=True)  27.4 us
    all_to_all x2, starting transfers between devices, exchange(): return lax.all_to_all(values, axes, 0, 0, tiled=True)  12 us
    pallas_call x7, Pallas kernels, run(): pl.pallas_call(kernel, out_shape=shapes, scratch_shapes=scratch, compiler...  6.91 us
  transfers between devices with their start and end apart: 2, of which 2 were waited for; matrix products, arithmetic and copies ran while one was open for 0% of the time, Pallas kernels for 1%

profile of v6, /device:TPU:2, one launch (start us, length us, event | category | flops | bytes accessed | tf_op | source)
XLA Modules:
  0.0 102.1 jit_solution(14927011912692203937)
XLA Ops:
  0.6 1.6 %shard_map.156 = (bf16[1280,128]{1,0:T(8,128)(2,1)S(1)}, f32[256,128]{1,0:T(8,128)S(1)}) custom-call(s32[1]{0:T(128)} %bitcast.place, bf16[512,128]{1,0:T(8,128)(2,1)} %bitcast.25, s32[2,256]{1,0:T(2,128)} %targets.1, s32[2,256]{1,0:T(2,128)} %mask.1, f32[1,128]{1,0:T(1,128)} %bitcast.32, f32[1,128]{1,0:T(1,128)} %bitcast.34, bf16[128,512]{1,0:T(8,128)(2,1)} %weight_far.1), custom_call_target="tpu_custom_call" | custom-call | flops 10000000 | bytes 267268 | tf_op jit(solution)/shard_map/pallas_call | solution.py:293
  2.3 42.6 %all_to_all.20 = bf16[128,5,2,128]{3,2,1,0:T(2,128)(2,1)S(1)} all-to-all(bf16[128,5,2,128]{3,2,1,0:T(2,128)(2,1)S(1)} %bitcast.27), channel_id=1, replica_groups=mesh['zhi'=2,'core'=2,'y'=4,'zlo'=8,'x'=4] {'y','zlo','x'}, dimensions={0} | all-to-all | bytes 655360 | tf_op jit(solution)/shard_map/all_to_all | solution.py:358
  44.9 1.0 shard_map.157
  45.9 0.0 copy-start
  45.9 0.0 copy-start.2
  45.9 0.0 copy-start.8
  45.9 0.0 copy-start.10
  45.9 0.0 copy-start.11
  45.9 8.1 %all-to-all-start.1 = ((bf16[128,3,2,128]{3,2,1,0:T(2,128)(2,1)}), bf16[128,3,2,128]{3,2,1,0:T(2,128)(2,1)S(1)}, u32[]{:S(2)}, u32[]{:S(2)}) async-start(bf16[128,3,2,128]{3,2,1,0:T(2,128)(2,1)} %bitcast.6), calls=%async_computation.1 | async-start | bytes 393216 | tf_op jit(solution)/shard_map/all_to_all | solution.py:358
  54.0 0.0 copy-start.5
  54.0 0.0 copy-start.4
  54.0 0.0 copy-start.6
  54.1 0.0 copy-start.7
  54.1 0.0 copy-start.9
  54.1 0.0 copy-done
  54.1 0.0 copy-done.2
  54.1 0.0 copy-done.8
  54.1 0.0 copy-done.10
  54.1 0.0 copy-done.11
  54.1 0.6 copy-done.5
  54.7 0.0 copy-done.4
  54.7 0.0 copy-done.6
  54.7 0.0 copy-done.7
  54.7 0.0 copy-done.9
  54.7 0.0 copy-start.1
  54.7 0.0 copy-start.3
  54.7 0.5 shard_map.158
  55.2 16.3 %all-to-all-done.1 = bf16[128,3,2,128]{3,2,1,0:T(2,128)(2,1)S(1)} async-done(((bf16[128,3,2,128]{3,2,1,0:T(2,128)(2,1)}), bf16[128,3,2,128]{3,2,1,0:T(2,128)(2,1)S(1)}, u32[]{:S(2)}, u32[]{:S(2)}) %all-to-all-start.1) | async-done | bytes 196640 | tf_op jit(solution)/shard_map/all_to_all | solution.py:358
  71.6 0.0 copy-done.1
  71.6 0.0 copy-done.3
  71.6 1.3 %shard_map.159 = (bf16[512,128]{1,0:T(8,128)(2,1)S(1)}, f32[192,128]{1,0:T(8,128)S(1)}, bf16[1152,128]{1,0:T(8,128)(2,1)S(1)}) custom-call(bf16[768,128]{1,0:T(8,128)(2,1)S(1)} %bitcast.23, f32[768,128]{1,0:T(8,128)S(1)} %get-tuple-element.19.base, f32[768,128]{1,0:T(8,128)S(1)} %get-tuple-element.20.gate, f32[24,128]{1,0:T(8,128)S(1)} %get-tuple-element.21.marks, ...), custom_call_target="tpu_custom_call" | custom-call | flops 10000000 | bytes 1044484 | tf_op jit(solution)/shard_map/pallas_call | solution.py:293
  72.9 11.8 %all_to_all.21 = bf16[16,72,128]{2,1,0:T(8,128)(2,1)S(1)} all-to-all(bf16[16,72,128]{2,1,0:T(8,128)(2,1)S(1)} %bitcast.28), channel_id=1, replica_groups=mesh['zhi'=2,'core'=2,'y'=4,'zlo'=8,'x'=4] {'y','x'}, dimensions={0} | all-to-all | bytes 589824 | tf_op jit(solution)/shard_map/all_to_all | solution.py:358
  84.7 0.8 shard_map.161
  85.5 3.9 %all-to-all-start.3 = ((bf16[8,80,128]{2,1,0:T(8,128)(2,1)}), bf16[8,80,128]{2,1,0:T(8,128)(2,1)S(1)}, u32[]{:S(2)}, u32[]{:S(2)}) async-start(bf16[8,80,128]{2,1,0:T(8,128)(2,1)} %bitcast.16), calls=%async_computation.3 | async-start | bytes 327680 | tf_op jit(solution)/shard_map/all_to_all | solution.py:358
  89.4 0.8 shard_map.160
  90.2 11.0 %all-to-all-done.3 = bf16[8,80,128]{2,1,0:T(8,128)(2,1)S(1)} async-done(((bf16[8,80,128]{2,1,0:T(8,128)(2,1)}), bf16[8,80,128]{2,1,0:T(8,128)(2,1)S(1)}, u32[]{:S(2)}, u32[]{:S(2)}) %all-to-all-start.3) | async-done | bytes 163872 | tf_op jit(solution)/shard_map/all_to_all | solution.py:358
  101.2 0.9 shard_map.162
Async XLA Ops:
  45.9 8.2 %copy-start = (bf16[2,256,128]{2,1,0:T(8,128)(2,1)S(1)}, bf16[2,256,128]{2,1,0:T(8,128)(2,1)}, u32[]{:S(2)}) copy-start(bf16[2,256,128]{2,1,0:T(8,128)(2,1)} %param.13) | copy-start | bytes 393220
  45.9 8.2 %copy-start.2 = (bf16[128,128]{1,0:T(8,128)(2,1)S(1)}, bf16[128,128]{1,0:T(8,128)(2,1)}, u32[]{:S(2)}) copy-start(bf16[128,128]{1,0:T(8,128)(2,1)} %gate_weight.1) | copy-start | bytes 98308
  45.9 8.2 %copy-start.8 = (s32[256]{0:T(256)S(1)}, s32[256]{0:T(256)}, u32[]{:S(2)}) copy-start(s32[256]{0:T(256)} %param.14) | copy-start | bytes 3076
  45.9 8.2 %copy-start.10 = (f32[128]{0:T(128)S(1)}, f32[128]{0:T(128)}, u32[]{:S(2)}) copy-start(f32[128]{0:T(128)} %param.22) | copy-start | bytes 1540
  45.9 8.2 %copy-start.11 = (f32[64]{0:T(128)S(1)}, f32[64]{0:T(128)}, u32[]{:S(2)}) copy-start(f32[64]{0:T(128)} %param.25) | copy-start | bytes 772
  45.9 25.7 %all-to-all-start.1 = ((bf16[128,3,2,128]{3,2,1,0:T(2,128)(2,1)}), bf16[128,3,2,128]{3,2,1,0:T(2,128)(2,1)S(1)}, u32[]{:S(2)}, u32[]{:S(2)}) async-start(bf16[128,3,2,128]{3,2,1,0:T(2,128)(2,1)} %bitcast.6), calls=%async_computation.1 | async-start | bytes 393216 | tf_op jit(solution)/shard_map/all_to_all | solution.py:358
  54.0 0.7 copy-start.5
  54.0 0.7 copy-start.4
  54.0 0.7 copy-start.6
  54.1 0.7 copy-start.7
  54.1 0.7 copy-start.9
  54.7 16.8 %copy-start.1 = (bf16[128,64]{0,1:T(8,128)(2,1)S(1)}, bf16[128,64]{0,1:T(8,128)(2,1)}, u32[]{:S(2)}) copy-start(bf16[128,64]{0,1:T(8,128)(2,1)} %param.24) | copy-start | bytes 49156
  54.7 16.8 %copy-start.3 = (bf16[128,128]{1,0:T(8,128)(2,1)S(1)}, bf16[128,128]{1,0:T(8,128)(2,1)}, u32[]{:S(2)}) copy-start(bf16[128,128]{1,0:T(8,128)(2,1)} %out_weight.1) | copy-start | bytes 98308
  85.5 15.7 %all-to-all-start.3 = ((bf16[8,80,128]{2,1,0:T(8,128)(2,1)}), bf16[8,80,128]{2,1,0:T(8,128)(2,1)S(1)}, u32[]{:S(2)}, u32[]{:S(2)}) async-start(bf16[8,80,128]{2,1,0:T(8,128)(2,1)} %bitcast.16), calls=%async_computation.3 | async-start | bytes 327680 | tf_op jit(solution)/shard_map/all_to_all | solution.py:358

commit v7 on v5

v7 whole, which is shorter than its diff:
```python
import jax
import jax.numpy as jnp
from jax import lax
from jax.experimental import pallas as pl
from jax.experimental.pallas import tpu as pltpu
from jax.sharding import Mesh
from jax.sharding import PartitionSpec as P

EVERY = ("zhi", "core", "y", "zlo", "x")
GROUP = ("y", "zlo", "x")
PLANE = ("y", "x")
BF16, F32 = jnp.bfloat16, jnp.float32
TN = (((0,), (0,)), ((), ()))
NT = (((1,), (1,)), ((), ()))
NN = (((1,), (0,)), ((), ()))
TT = (((0,), (1,)), ((), ()))


def dot(left, right, dims):
    return lax.dot_general(left, right, dims, preferred_element_type=F32)


def norm_lanes(values, gain, bias):
    center = jnp.mean(values, axis=1, keepdims=True)
    spread = jnp.mean(jnp.square(values - center), axis=1, keepdims=True)
    return (values - center) * lax.rsqrt(spread + 1e-05) * gain + bias


def picker(parity):
    rows = lax.broadcasted_iota(jnp.int32, (128, 256), 0)
    columns = lax.broadcasted_iota(jnp.int32, (128, 256), 1)
    return (columns == 2 * rows + parity).astype(F32).astype(BF16)


def pack_kernel(place, *refs):
    far, (send, labels, base, gate, marks, heavy) = refs[:13], refs[13:19]
    near, (flat, rows, own, sems) = refs[19:32], refs[32:]
    targets, mask, chain, pair, gain, bias, out_gain, out_bias, dist_bias = near[:9]
    in_weight, gate_weight, out_weight, dist_weight = near[9:]
    copies = [pltpu.make_async_copy(far[n], near[n], sems.at[n]) for n in range(13)]
    for copy in copies:
        copy.start()
    lower = lax.broadcasted_iota(jnp.int32, (128, 128), 0) * 2 <= place[0]
    pickers = picker(0), picker(1)
    for copy in copies[:3]:
        copy.wait()
    maskf = mask[...].astype(F32)
    label = jnp.where(mask[...] > 0, targets[...].astype(F32), 64.0)
    first, second, third = (
        dot(pickers[ir], jnp.broadcast_to(label[jr : jr + 1], (128, 256)).astype(BF16), NT)
        for ir, jr in ((0, 0), (1, 0), (1, 1))
    )
    labels[0:128, :] = jnp.where(lower, first, second)
    labels[128:256, :] = jnp.where(lower, second, third)
    own[...] = jnp.zeros_like(own)
    own[0:2, :] = targets[...].astype(F32)
    own[2:4, :] = maskf
    columns = lax.broadcasted_iota(jnp.int32, (1, 256), 1)
    for r in range(2):
        here = jnp.sum(jnp.where(columns == place[0] + r, chain[...], 0), axis=1, keepdims=True)
        own[4 + r : 5 + r, :] = 1.0 + (chain[...] != here).astype(F32)
    even, odd = (dot(own[...].astype(BF16), pickers[jr], NT) for jr in range(2))
    lanes = lax.broadcasted_iota(jnp.int32, (1, 128), 1) * 2
    higher, same = lanes >= place[0], lanes == place[0]
    target, valid, factor = (
        (
            jnp.where(higher, even[at : at + 1], even[at + 1 : at + 2]),
            jnp.where(higher, even[at + 1 : at + 2], odd[at + 1 : at + 2]),
            odd[at + 1 : at + 2],
        )
        for at in (0, 2, 4)
    )
    alone = jnp.where(same, valid[2] * factor[2], 0.0)
    marks[...] = jnp.zeros((24, 128), F32)
    for group in range(2):
        marks[group : group + 1, :] = valid[group] * factor[group]
        marks[3 + group : 4 + group, :] = factor[group]
    marks[2:3, :] = alone
    marks[5:6, :] = alone
    for group in range(3):
        marks[6 + group : 7 + group, :] = target[group]
    copies[3].wait()
    flat[...] = pair[...].astype(F32)
    for block in range(4):
        base[block * 128 : (block + 1) * 128, :] = flat[
            pl.ds(block // 2 * 256 + block % 2, 128, stride=2), :
        ]
    first, second, third = (
        flat[pl.ds(jr * 256 + ir, 128, stride=2), :] for ir, jr in ((0, 0), (1, 0), (1, 1))
    )
    rows[pl.ds(8, 128, stride=10), :] = jnp.where(lower, first, second)
    rows[pl.ds(9, 128, stride=10), :] = jnp.where(lower, second, third)
    for copy in copies[4:]:
        copy.wait()
    marks[16:17, :] = out_gain[...]
    marks[17:18, :] = out_bias[...]
    marks[18:19, :64] = dist_bias[...]
    marks[19:20, :] = gain[...]
    marks[20:21, :] = bias[...]
    heavy[0:128, :] = gate_weight[...]
    heavy[128:256, :] = out_weight[...]
    heavy[256:320, :] = dist_weight[...]
    normed = norm_lanes(flat[...], gain[...], bias[...]).astype(BF16)
    proj = dot(in_weight[...], normed, TT)
    for n in range(4):
        r, half = n // 2, n % 2
        at = slice(n * 128, (n + 1) * 128)
        here = jax.nn.sigmoid(proj[256:, at]) * maskf[r : r + 1, half * 128 : (half + 1) * 128]
        here = proj[:256, at] * here
        for side in range(2):
            rows[pl.ds(side * 4 + n, 128, stride=10), :] = here[side * 128 : (side + 1) * 128]
    send[...] = rows[...].astype(BF16)
    flat[...] = jax.nn.sigmoid(dot(normed, gate_weight[...], NN))
    for block in range(4):
        gate[block * 128 : (block + 1) * 128, :] = flat[
            pl.ds(block // 2 * 256 + block % 2, 128, stride=2), :
        ]


def triangle_kernel(got, labels, marks, heavy, send, base, gate, rows, products):
    rows[...] = got[...].astype(F32)
    sides = []
    for side in range(2):
        halves = []
        for half in range(2):
            parts = [
                rows[pl.ds(side * 4 + r * 2 + half, 128, stride=10), :].astype(BF16)
                for r in range(2)
            ]
            halves.append(jnp.concatenate(parts, axis=0))
        sides.append(jnp.concatenate(halves, axis=1))
    mixed = dot(sides[0], sides[1], NT)
    mirrored = dot(sides[1], sides[0], NT)
    for r in range(2):
        for jr in range(2):
            products[pl.ds(r * 2 + jr, 128, stride=6), :] = mixed[
                r * 128 : (r + 1) * 128, jr * 128 : (jr + 1) * 128
            ]
    first, second, third = mirrored[:128, :128], mirrored[128:, :128], mirrored[128:, 128:]
    lane = lax.broadcasted_iota(jnp.int32, (128, 128), 1)
    device = lax.broadcasted_iota(jnp.int32, (128, 128), 0)
    products[pl.ds(4, 128, stride=6), :] = jnp.where(
        lane == device, labels[0:128, :], jnp.where(lane > device, first, second)
    )
    products[pl.ds(5, 128, stride=6), :] = jnp.where(
        lane == device, labels[128:256, :], jnp.where(lane > device, second, third)
    )
    send[...] = products[...].astype(BF16)
    base[0:128, :] = rows[pl.ds(8, 128, stride=10), :]
    base[128:256, :] = rows[pl.ds(9, 128, stride=10), :]
    normed = norm_lanes(base[...], marks[19:20, :], marks[20:21, :]).astype(BF16)
    gate[...] = jax.nn.sigmoid(dot(normed, heavy[0:128, :], NN))


def message(weights, loss, others):
    row = lax.broadcasted_iota(jnp.int32, (8, 128), 0)
    high = loss.astype(BF16).astype(F32)
    terms = jnp.where(row == 0, high, jnp.where(row == 1, loss - high, 0.0))
    pieces = [piece for other in others for piece in (weights, terms, other)]
    return jnp.concatenate(pieces, axis=0).astype(BF16)


def add_sums(values, peers):
    sums = jnp.sum(values.reshape(peers, values.shape[0] // peers, 128), axis=0)
    return sums[:64], sums[64:65, 0:1] + sums[65:66, 0:1]


def head_kernel(
    got, base, gate, back_base, back_gate, marks, place, heavy,
    updated, grad, total, hidden, slopes,
):
    hidden[...] = got[...].astype(F32)
    columns = jnp.transpose(marks[16:24, :])
    gain, bias, dist_bias = columns[:, 0:1], columns[:, 1:2], columns[:64, 2:3]
    q = []
    kept = []
    lanes = lax.broadcasted_iota(jnp.int32, (128, 128), 1) * 2
    chosen = (lanes[:16] == place[0]).astype(F32).astype(BF16)
    heres = [hidden[pl.ds(block, 128, stride=6), :] for block in range(6)]
    labels = [dot(chosen, heres[4 + group].astype(BF16), NT)[0:1] for group in range(2)]
    for group in range(2):
        heres[4 + group] = jnp.where(lanes == place[0], heres[group], heres[4 + group])
    normeds = []
    for here in heres:
        center = jnp.mean(here, axis=0, keepdims=True)
        spread = jnp.mean(jnp.square(here - center), axis=0, keepdims=True)
        normed = (here - center) * lax.rsqrt(spread + 1e-05)
        normeds.append((normed * gain + bias).astype(BF16))
    update = dot(jnp.concatenate(normeds, axis=1), heavy[128:256, :], TN)
    sums = (base[...] + gate[...] * update[:512]).astype(BF16)
    back_sums = (back_base[...] + back_gate[...] * update[512:]).astype(BF16)
    updated[...] = sums
    sums = jnp.concatenate([sums, back_sums], axis=0)
    logit = dot(heavy[256:320, :], sums, NT)
    for block in range(6):
        at = slice(block * 128, (block + 1) * 128)
        q.append(logit[:, at])
        kept.append(sums[at])
    lanes = lanes[:64]
    higher = lanes >= place[0]
    pairs = (
        jnp.where(higher, q[0], q[2]) + q[4],
        jnp.where(higher, q[2], q[3]) + q[5],
        q[3] + q[3],
    )
    bins = lax.broadcasted_iota(jnp.int32, (64, 128), 0).astype(F32)
    row = lambda at: marks[at : at + 1, :]
    mirrored = [jnp.where(labels[group] < 63.5, row(3 + group), 0.0) for group in range(2)]
    counted = [jnp.where(lanes[:1] == place[0], 0.0, mirrored[0]), mirrored[1]]
    mirrored.append(row(5))
    labels.append(row(8))
    losses = jnp.zeros((1, 128), F32)
    slope = []
    for group in range(3):
        logits = pairs[group] + dist_bias
        shifted = logits - jnp.max(logits, axis=0, keepdims=True)
        powers = jnp.exp(shifted)
        norms = jnp.sum(powers, axis=0, keepdims=True)
        log_probs = shifted - jnp.log(norms)
        probs = powers / norms
        onehot = (bins == row(6 + group)).astype(F32)
        onehot_back = (bins == labels[group]).astype(F32)
        losses = losses - row(group) * jnp.sum(onehot * log_probs, axis=0, keepdims=True)
        if group < 2:
            losses = losses - counted[group] * jnp.sum(onehot_back * log_probs, axis=0, keepdims=True)
        slope.append(row(group) * (probs - onehot) + mirrored[group] * (probs - onehot_back))
    blocks = (
        (0, jnp.where(higher, slope[0], 0.0)),
        (2, jnp.where(higher, slope[1], slope[0])),
        (3, jnp.where(higher, 0.0, slope[1]) + slope[2]),
        (4, jnp.where(lanes == place[0], 0.0, slope[0])),
        (5, slope[1]),
    )
    weights = jnp.zeros((64, 128), F32)
    for block, values in blocks:
        high = values.astype(BF16)
        low = (values - high.astype(F32)).astype(BF16)
        weights = weights + dot(high, kept[block], NN) + dot(low, kept[block], NN)
    for n in range(3):
        grad[n * 64 : (n + 1) * 64, :] = blocks[n][1]
    slopes[...] = jnp.transpose(jnp.concatenate(slope[:2], axis=0))
    others = [slopes[pl.ds(y * 32 + x, 8, stride=4), :] for y in range(4) for x in range(4)]
    total[...] = message(weights, jnp.sum(losses, axis=1, keepdims=True), others)


def middle_kernel(got, send, slopes):
    values = got[...].astype(F32)
    slopes[...] = values.reshape(16, 80, 128)[:, 72:80].reshape(128, 128)
    weights, loss = add_sums(values, 16)
    send[...] = message(weights, loss, [slopes[pl.ds(z, 16, stride=8), :] for z in range(8)])


def last_kernel(
    got, updated, grad, place, heavy, grad_weight, loss, grad_pair, pair_out, slopes, rows
):
    for block in range(4):
        rows[pl.ds(block // 2 * 256 + block % 2, 128, stride=2), :] = updated[
            block * 128 : (block + 1) * 128, :
        ].astype(F32)
    pair_out[...] = rows[...].astype(BF16)
    dist_weight = heavy[256:320, :]
    part = {}
    for n, block in enumerate((0, 2, 3)):
        slope = grad[n * 64 : (n + 1) * 64, :]
        high = slope.astype(BF16)
        low = (slope - high.astype(F32)).astype(BF16)
        part[block] = dot(high, dist_weight, TN) + dot(low, dist_weight, TN)
    values = got[...].astype(F32)
    for z in range(8):
        for y in range(4):
            at = z * 88 + 72 + y * 4
            slopes[y * 32 + z * 4 : y * 32 + z * 4 + 4, :] = values[at : at + 4]
    there = slopes[...].astype(BF16)
    none = jnp.zeros((64, 128), BF16)
    first = dot(there, jnp.concatenate([dist_weight, none], axis=0), NN)
    second = dot(there, jnp.concatenate([none, dist_weight], axis=0), NN)
    device = lax.broadcasted_iota(jnp.int32, (128, 128), 0) * 2
    results = (
        part[0] + jnp.where(device < place[0], first, 0.0),
        jnp.where(device <= place[0], second, first),
        part[2],
        part[3] + jnp.where(device > place[0], second, 0.0),
    )
    for block in range(4):
        grad_pair[pl.ds(block // 2 * 256 + block % 2, 128, stride=2), :] = results[block]
    weights, total = add_sums(values, 8)
    grad_weight[...] = weights * (1.0 / 256)
    loss[0] = total[0, 0] * (1.0 / 65536)


def run(kernel, outs, scratch, args, **specs):
    shapes = [jax.ShapeDtypeStruct(s, d) for s, d in outs]
    moved = sum(x.size * x.dtype.itemsize for x in args)
    scratch = [pltpu.VMEM(*s) if isinstance(s, tuple) else s for s in scratch]
    return pl.pallas_call(
        kernel,
        out_shape=shapes,
        scratch_shapes=scratch,
        compiler_params=pltpu.CompilerParams(vmem_limit_bytes=24 * 1024 * 1024),
        cost_estimate=pl.CostEstimate(flops=10_000_000, bytes_accessed=moved, transcendentals=0),
        **specs,
    )(*args)


VMEM, FAR = pl.BlockSpec(memory_space=pltpu.VMEM), pl.BlockSpec(memory_space=pl.ANY)
SMEM = pl.BlockSpec(memory_space=pltpu.SMEM)


def pack(place, *args):
    scratch = [(arg.shape, arg.dtype) for arg in args]
    scratch += [((512, 128), F32), ((1280, 128), F32), ((16, 256), F32)]
    scratch += [pltpu.SemaphoreType.DMA((13,))]
    outs = [
        ((1280, 128), BF16),
        ((256, 128), F32),
        ((512, 128), F32),
        ((512, 128), F32),
        ((24, 128), F32),
        ((320, 128), BF16),
    ]
    args = [pltpu.with_memory_space_constraint(arg, pltpu.HBM) for arg in args]
    return run(pack_kernel, outs, scratch, (place, *args), in_specs=[SMEM] + [FAR] * 13)


def triangle(*args):
    outs = [((768, 128), BF16), ((256, 128), F32), ((256, 128), F32)]
    return run(triangle_kernel, outs, [((1280, 128), F32), ((768, 128), F32)], args)


def head(*args):
    outs = [((512, 128), BF16), ((192, 128), F32), ((1280, 128), BF16)]
    scratch = [((768, 128), F32), ((128, 128), F32)]
    return run(head_kernel, outs, scratch, args, in_specs=[VMEM] * 6 + [SMEM] + [VMEM])


def middle(got):
    return run(middle_kernel, [((704, 128), BF16)], [((128, 128), F32)], (got,))[0]


def last(*args):
    outs = [((64, 128), F32), ((1,), F32), ((512, 128), F32), ((512, 128), BF16)]
    scratch = [((128, 128), F32), ((512, 128), F32)]
    specs = {"in_specs": [VMEM] * 3 + [SMEM, VMEM], "out_specs": [VMEM, SMEM, VMEM, VMEM]}
    return run(last_kernel, outs, scratch, args, **specs)


def exchange(values, axes):
    return lax.all_to_all(values, axes, 0, 0, tiled=True)


def on_device(
    pair,
    chain,
    targets,
    pair_mask,
    ln_in_gain,
    ln_in_bias,
    in_weight,
    out_gate_weight,
    ln_out_gain,
    ln_out_bias,
    out_weight,
    dist_weight,
    dist_bias,
):
    place = (lax.axis_index(GROUP) * 2).reshape(1)
    row = lambda values: values.reshape(1, values.shape[0])
    send, labels, base, gate, marks, heavy = pack(
        place,
        targets,
        pair_mask,
        row(chain),
        pair.reshape(512, 128),
        row(ln_in_gain),
        row(ln_in_bias),
        row(ln_out_gain),
        row(ln_out_bias),
        row(dist_bias),
        in_weight,
        out_gate_weight,
        out_weight,
        jnp.swapaxes(dist_weight, 0, 1),
    )
    got = exchange(send.reshape(128, 5, 2, 128), GROUP).reshape(1280, 128)
    products, back_base, back_gate = triangle(got, labels, marks, heavy)
    hidden = exchange(products.reshape(128, 3, 2, 128), GROUP).reshape(768, 128)
    updated, grad, total = head(hidden, base, gate, back_base, back_gate, marks, place, heavy)
    total = middle(exchange(total.reshape(16, 80, 128), PLANE).reshape(1280, 128))
    total = exchange(total.reshape(8, 88, 128), "zlo").reshape(704, 128)
    grad_weight, loss, grad_pair, pair_out = last(total, updated, grad, place, heavy)
    return (
        pair_out.reshape(2, 256, 128),
        grad_pair.reshape(2, 256, 128),
        jnp.swapaxes(grad_weight, 0, 1),
        loss,
    )


def solution(mesh):
    fine = Mesh(mesh.devices.reshape(2, 2, 4, 8, 4), EVERY)
    part = ("zhi", "core")
    in_specs = (
        P(EVERY, None, None),
        P(part),
        P(EVERY, None),
        P(EVERY, None),
        P(),
        P(),
        P(),
        P(),
        P(),
        P(),
        P(),
        P(part, None),
        P(),
    )
    out_specs = (
        P(EVERY, None, None),
        P(EVERY, None, None),
        P(part, None),
        P(part),
    )
    return jax.shard_map(
        on_device, mesh=fine, in_specs=in_specs, out_specs=out_specs, check_vma=False
    )
```

time: 103 us -> 101 us (0.981)
  blocking collectives: 54.1 us -> 95.8 us
  waiting for transfers between devices: 26.3 us -> 0 us
  starting transfers between devices: 13.9 us -> 0 us
  Pallas kernels: 6.85 us -> 4.32 us
    all_to_all x2 -> x4, blocking collectives: 54.1 us -> 95.8 us  [exchange(): return lax.all_to_all(values, axes, 0, 0, tiled=True)]
    all_to_all x2 -> x0, waiting for transfers between devices: 26.3 us -> none  [exchange(): return lax.all_to_all(values, axes, 0, 0, tiled=True)]
    all_to_all x2 -> x0, starting transfers between devices: 13.9 us -> none  [exchange(): return lax.all_to_all(values, axes, 0, 0, tiled=True)]
    pallas_call x7 -> x5, Pallas kernels: 6.85 us -> 4.32 us  [run(): pl.pallas_call(kernel, out_shape=shapes, scratch_shapes=scratch, compiler...]
  transfers between devices with their start and end apart: 2 -> 0, of which waited for: 2 -> 0; matrix products, arithmetic and copies ran while one was open for 0% -> 0% of each run, Pallas kernels for 1% -> 0%
where the time goes in v7:
time: 101 us
  blocking collectives  95.8 us (95%)
  Pallas kernels  4.32 us (4%)
    all_to_all x4, blocking collectives, exchange(): return lax.all_to_all(values, axes, 0, 0, tiled=True)  95.8 us
    pallas_call x5, Pallas kernels, run(): pl.pallas_call(kernel, out_shape=shapes, scratch_shapes=scratch, compiler...  4.32 us

profile of v7, /device:TPU:32, one launch (start us, length us, event | category | flops | bytes accessed | tf_op | source)
XLA Modules:
  0.0 100.8 jit_solution(16845180673341011513)
XLA Ops:
  0.6 1.8 %shard_map.156 = (bf16[1280,128]{1,0:T(8,128)(2,1)S(1)}, f32[256,128]{1,0:T(8,128)S(1)}, f32[512,128]{1,0:T(8,128)S(1)}, f32[512,128]{1,0:T(8,128)S(1)}, f32[24,...) custom-call(s32[1]{0:T(128)} %bitcast.place, s32[2,256]{1,0:T(2,128)} %refs_0_.1, s32[2,256]{1,0:T(2,128)} %refs_1_.1, ...), custom_call_target="tpu_custom_call" | custom-call | flops 10000000 | bytes 351492 | tf_op jit(solution)/shard_map/pallas_call | solution.py:295
  2.5 41.6 %all_to_all.20 = bf16[128,5,2,128]{3,2,1,0:T(2,128)(2,1)S(1)} all-to-all(bf16[128,5,2,128]{3,2,1,0:T(2,128)(2,1)S(1)} %bitcast.26), channel_id=1, replica_groups=mesh['zhi'=2,'core'=2,'y'=4,'zlo'=8,'x'=4] {'y','zlo','x'}, dimensions={0} | all-to-all | bytes 655360 | tf_op jit(solution)/shard_map/all_to_all | solution.py:348
  44.1 0.4 shard_map.157
  44.5 25.5 %all_to_all.21 = bf16[128,3,2,128]{3,2,1,0:T(2,128)(2,1)S(1)} all-to-all(bf16[128,3,2,128]{3,2,1,0:T(2,128)(2,1)S(1)} %bitcast.27), channel_id=1, replica_groups=mesh['zhi'=2,'core'=2,'y'=4,'zlo'=8,'x'=4] {'y','zlo','x'}, dimensions={0} | all-to-all | bytes 393216 | tf_op jit(solution)/shard_map/all_to_all | solution.py:348
  70.0 1.0 shard_map.158
  71.0 12.4 %all_to_all.22 = bf16[16,80,128]{2,1,0:T(8,128)(2,1)S(1)} all-to-all(bf16[16,80,128]{2,1,0:T(8,128)(2,1)S(1)} %bitcast.25), channel_id=1, replica_groups=mesh['zhi'=2,'core'=2,'y'=4,'zlo'=8,'x'=4] {'y','x'}, dimensions={0} | all-to-all | bytes 655360 | tf_op jit(solution)/shard_map/all_to_all | solution.py:348
  83.4 0.1 shard_map.159
  83.6 16.2 %all_to_all.23 = bf16[8,88,128]{2,1,0:T(8,128)(2,1)S(1)} all-to-all(bf16[8,88,128]{2,1,0:T(8,128)(2,1)S(1)} %bitcast.24), channel_id=1, replica_groups=mesh['zhi'=2,'core'=2,'y'=4,'zlo'=8,'x'=4] {'zlo'}, dimensions={0} | all-to-all | bytes 360448 | tf_op jit(solution)/shard_map/all_to_all | solution.py:348
  99.7 1.0 %shard_map.160 = (f32[64,128]{1,0:T(8,128)}, f32[1]{0:T(128)}, f32[512,128]{1,0:T(8,128)}, bf16[512,128]{1,0:T(8,128)(2,1)}) custom-call(bf16[704,128]{1,0:T(8,128)(2,1)S(1)} %bitcast.23, bf16[512,128]{1,0:T(8,128)(2,1)S(1)} %get-tuple-element.30.updated, f32[192,128]{1,0:T(8,128)S(1)} %get-tuple-element.31.grad, s32[1]{0:T(128)} %bitcast.place, ...), custom_call_target="tpu_custom_call" | custom-call | flops 10000000 | bytes 491524 | tf_op jit(solution)/shard_map/pallas_call | solution.py:295

commit v8 on v7

--- a/solution.py
+++ b/solution.py
@@ -80,7 +80,7 @@
     for group in range(3):
         marks[6 + group : 7 + group, :] = target[group]
     copies[3].wait()
-    flat[...] = pair[...].astype(F32)
+    flat[0:512, :] = pair[...].astype(F32)
     for block in range(4):
         base[block * 128 : (block + 1) * 128, :] = flat[
             pl.ds(block // 2 * 256 + block % 2, 128, stride=2), :
@@ -100,7 +100,7 @@
     heavy[0:128, :] = gate_weight[...]
     heavy[128:256, :] = out_weight[...]
     heavy[256:320, :] = dist_weight[...]
-    normed = norm_lanes(flat[...], gain[...], bias[...]).astype(BF16)
+    normed = norm_lanes(flat[0:512, :], gain[...], bias[...]).astype(BF16)
     proj = dot(in_weight[...], normed, TT)
     for n in range(4):
         r, half = n // 2, n % 2
@@ -109,8 +109,8 @@
         here = proj[:256, at] * here
         for side in range(2):
             rows[pl.ds(side * 4 + n, 128, stride=10), :] = here[side * 128 : (side + 1) * 128]
-    send[...] = rows[...].astype(BF16)
-    flat[...] = jax.nn.sigmoid(dot(normed, gate_weight[...], NN))
+    send[...] = rows[0:1280, :].astype(BF16)
+    flat[0:512, :] = jax.nn.sigmoid(dot(normed, gate_weight[...], NN))
     for block in range(4):
         gate[block * 128 : (block + 1) * 128, :] = flat[
             pl.ds(block // 2 * 256 + block % 2, 128, stride=2), :
@@ -118,7 +118,7 @@
 
 
 def triangle_kernel(got, labels, marks, heavy, send, base, gate, rows, products):
-    rows[...] = got[...].astype(F32)
+    rows[0:1280, :] = got[...].astype(F32)
     sides = []
     for side in range(2):
         halves = []
@@ -145,7 +145,7 @@
     products[pl.ds(5, 128, stride=6), :] = jnp.where(
         lane == device, labels[128:256, :], jnp.where(lane > device, second, third)
     )
-    send[...] = products[...].astype(BF16)
+    send[...] = products[0:768, :].astype(BF16)
     base[0:128, :] = rows[pl.ds(8, 128, stride=10), :]
     base[128:256, :] = rows[pl.ds(9, 128, stride=10), :]
     normed = norm_lanes(base[...], marks[19:20, :], marks[20:21, :]).astype(BF16)
@@ -169,7 +169,7 @@
     got, base, gate, back_base, back_gate, marks, place, heavy,
     updated, grad, total, hidden, slopes,
 ):
-    hidden[...] = got[...].astype(F32)
+    hidden[0:768, :] = got[...].astype(F32)
     columns = jnp.transpose(marks[16:24, :])
     gain, bias, dist_bias = columns[:, 0:1], columns[:, 1:2], columns[:64, 2:3]
     q = []
@@ -238,26 +238,29 @@
         weights = weights + dot(high, kept[block], NN) + dot(low, kept[block], NN)
     for n in range(3):
         grad[n * 64 : (n + 1) * 64, :] = blocks[n][1]
-    slopes[...] = jnp.transpose(jnp.concatenate(slope[:2], axis=0))
+    slopes[0:128, :] = jnp.transpose(jnp.concatenate(slope[:2], axis=0))
     others = [slopes[pl.ds(y * 32 + x, 8, stride=4), :] for y in range(4) for x in range(4)]
     total[...] = message(weights, jnp.sum(losses, axis=1, keepdims=True), others)
 
 
 def middle_kernel(got, send, slopes):
     values = got[...].astype(F32)
-    slopes[...] = values.reshape(16, 80, 128)[:, 72:80].reshape(128, 128)
+    slopes[0:128, :] = values.reshape(16, 80, 128)[:, 72:80].reshape(128, 128)
     weights, loss = add_sums(values, 16)
     send[...] = message(weights, loss, [slopes[pl.ds(z, 16, stride=8), :] for z in range(8)])
 
 
 def last_kernel(
-    got, updated, grad, place, heavy, grad_weight, loss, grad_pair, pair_out, slopes, rows
+    got, updated, grad, place, heavy, grad_weight, loss, grad_far, pair_far,
+    slopes, rows, grad_pair, pair_out, sems,
 ):
     for block in range(4):
         rows[pl.ds(block // 2 * 256 + block % 2, 128, stride=2), :] = updated[
             block * 128 : (block + 1) * 128, :
         ].astype(F32)
-    pair_out[...] = rows[...].astype(BF16)
+    pair_out[...] = rows[0:512, :].astype(BF16)
+    copies = [pltpu.make_async_copy(pair_out, pair_far, sems.at[0])]
+    copies[0].start()
     dist_weight = heavy[256:320, :]
     part = {}
     for n, block in enumerate((0, 2, 3)):
@@ -283,9 +286,19 @@
     )
     for block in range(4):
         grad_pair[pl.ds(block // 2 * 256 + block % 2, 128, stride=2), :] = results[block]
+        if block % 2:
+            half = pl.ds(block // 2 * 256, 256)
+            copies.append(
+                pltpu.make_async_copy(
+                    grad_pair.at[half], grad_far.at[half], sems.at[1 + block // 2]
+                )
+            )
+            copies[-1].start()
     weights, total = add_sums(values, 8)
     grad_weight[...] = weights * (1.0 / 256)
     loss[0] = total[0, 0] * (1.0 / 65536)
+    for copy in copies:
+        copy.wait()
 
 
 def run(kernel, outs, scratch, args, **specs):
@@ -308,7 +321,7 @@
 
 def pack(place, *args):
     scratch = [(arg.shape, arg.dtype) for arg in args]
-    scratch += [((512, 128), F32), ((1280, 128), F32), ((16, 256), F32)]
+    scratch += [((520, 128), F32), ((1296, 128), F32), ((16, 256), F32)]
     scratch += [pltpu.SemaphoreType.DMA((13,))]
     outs = [
         ((1280, 128), BF16),
@@ -324,23 +337,24 @@
 
 def triangle(*args):
     outs = [((768, 128), BF16), ((256, 128), F32), ((256, 128), F32)]
-    return run(triangle_kernel, outs, [((1280, 128), F32), ((768, 128), F32)], args)
+    return run(triangle_kernel, outs, [((1296, 128), F32), ((784, 128), F32)], args)
 
 
 def head(*args):
     outs = [((512, 128), BF16), ((192, 128), F32), ((1280, 128), BF16)]
-    scratch = [((768, 128), F32), ((128, 128), F32)]
+    scratch = [((784, 128), F32), ((136, 128), F32)]
     return run(head_kernel, outs, scratch, args, in_specs=[VMEM] * 6 + [SMEM] + [VMEM])
 
 
 def middle(got):
-    return run(middle_kernel, [((704, 128), BF16)], [((128, 128), F32)], (got,))[0]
+    return run(middle_kernel, [((704, 128), BF16)], [((136, 128), F32)], (got,))[0]
 
 
 def last(*args):
     outs = [((64, 128), F32), ((1,), F32), ((512, 128), F32), ((512, 128), BF16)]
-    scratch = [((128, 128), F32), ((512, 128), F32)]
-    specs = {"in_specs": [VMEM] * 3 + [SMEM, VMEM], "out_specs": [VMEM, SMEM, VMEM, VMEM]}
+    scratch = [((128, 128), F32), ((520, 128), F32), ((520, 128), F32), ((512, 128), BF16)]
+    scratch += [pltpu.SemaphoreType.DMA((3,))]
+    specs = {"in_specs": [VMEM] * 3 + [SMEM, VMEM], "out_specs": [VMEM, SMEM, FAR, FAR]}
     return run(last_kernel, outs, scratch, args, **specs)
 
 

time: 101 us -> 102 us (level)
  no operation moved by 1% of the time
where the time goes in v8:
time: 102 us; the launch traced here: 101 us
  blocking collectives  95.8 us (94%)
  Pallas kernels  4.92 us (5%)
    all_to_all x4, blocking collectives, exchange(): return lax.all_to_all(values, axes, 0, 0, tiled=True)  95.8 us
    pallas_call x5, Pallas kernels, run(): pl.pallas_call(kernel, out_shape=shapes, scratch_shapes=scratch, compiler...  4.92 us

profile of v8, /device:TPU:32, one launch (start us, length us, event | category | flops | bytes accessed | tf_op | source)
XLA Modules:
  0.0 101.4 jit_solution(7324728907123100175)
XLA Ops:
  0.6 1.8 %shard_map.156 = (bf16[1280,128]{1,0:T(8,128)(2,1)S(1)}, f32[256,128]{1,0:T(8,128)S(1)}, f32[512,128]{1,0:T(8,128)S(1)}, f32[512,128]{1,0:T(8,128)S(1)}, f32[24,...) custom-call(s32[1]{0:T(128)} %bitcast.place, s32[2,256]{1,0:T(2,128)} %refs_0_.1, s32[2,256]{1,0:T(2,128)} %refs_1_.1, ...), custom_call_target="tpu_custom_call" | custom-call | flops 10000000 | bytes 351492 | tf_op jit(solution)/shard_map/pallas_call | solution.py:308
  2.5 41.6 %all_to_all.20 = bf16[128,5,2,128]{3,2,1,0:T(2,128)(2,1)S(1)} all-to-all(bf16[128,5,2,128]{3,2,1,0:T(2,128)(2,1)S(1)} %bitcast.26), channel_id=1, replica_groups=mesh['zhi'=2,'core'=2,'y'=4,'zlo'=8,'x'=4] {'y','zlo','x'}, dimensions={0} | all-to-all | bytes 655360 | tf_op jit(solution)/shard_map/all_to_all | solution.py:362
  44.1 0.4 shard_map.157
  44.5 25.5 %all_to_all.21 = bf16[128,3,2,128]{3,2,1,0:T(2,128)(2,1)S(1)} all-to-all(bf16[128,3,2,128]{3,2,1,0:T(2,128)(2,1)S(1)} %bitcast.27), channel_id=1, replica_groups=mesh['zhi'=2,'core'=2,'y'=4,'zlo'=8,'x'=4] {'y','zlo','x'}, dimensions={0} | all-to-all | bytes 393216 | tf_op jit(solution)/shard_map/all_to_all | solution.py:362
  70.0 1.0 shard_map.158
  71.0 12.4 %all_to_all.22 = bf16[16,80,128]{2,1,0:T(8,128)(2,1)S(1)} all-to-all(bf16[16,80,128]{2,1,0:T(8,128)(2,1)S(1)} %bitcast.25), channel_id=1, replica_groups=mesh['zhi'=2,'core'=2,'y'=4,'zlo'=8,'x'=4] {'y','x'}, dimensions={0} | all-to-all | bytes 655360 | tf_op jit(solution)/shard_map/all_to_all | solution.py:362
  83.4 0.1 shard_map.159
  83.6 16.2 %all_to_all.23 = bf16[8,88,128]{2,1,0:T(8,128)(2,1)S(1)} all-to-all(bf16[8,88,128]{2,1,0:T(8,128)(2,1)S(1)} %bitcast.24), channel_id=1, replica_groups=mesh['zhi'=2,'core'=2,'y'=4,'zlo'=8,'x'=4] {'zlo'}, dimensions={0} | all-to-all | bytes 360448 | tf_op jit(solution)/shard_map/all_to_all | solution.py:362
  99.7 1.6 %shard_map.160 = (f32[64,128]{1,0:T(8,128)}, f32[1]{0:T(128)}, f32[512,128]{1,0:T(8,128)}, bf16[512,128]{1,0:T(8,128)(2,1)}) custom-call(bf16[704,128]{1,0:T(8,128)(2,1)S(1)} %bitcast.23, bf16[512,128]{1,0:T(8,128)(2,1)S(1)} %get-tuple-element.30.updated, f32[192,128]{1,0:T(8,128)S(1)} %get-tuple-element.31.grad, s32[1]{0:T(128)} %bitcast.place, ...), custom_call_target="tpu_custom_call" | custom-call | flops 10000000 | bytes 491524 | tf_op jit(solution)/shard_map/pallas_call | solution.py:308

commit v9 on v8

--- a/solution.py
+++ b/solution.py
@@ -251,16 +251,14 @@
 
 
 def last_kernel(
-    got, updated, grad, place, heavy, grad_weight, loss, grad_far, pair_far,
-    slopes, rows, grad_pair, pair_out, sems,
+    got, updated, grad, place, heavy, grad_weight, loss, grad_pair, pair_out,
+    slopes, rows, order,
 ):
     for block in range(4):
         rows[pl.ds(block // 2 * 256 + block % 2, 128, stride=2), :] = updated[
             block * 128 : (block + 1) * 128, :
         ].astype(F32)
     pair_out[...] = rows[0:512, :].astype(BF16)
-    copies = [pltpu.make_async_copy(pair_out, pair_far, sems.at[0])]
-    copies[0].start()
     dist_weight = heavy[256:320, :]
     part = {}
     for n, block in enumerate((0, 2, 3)):
@@ -285,20 +283,11 @@
         part[3] + jnp.where(device > place[0], second, 0.0),
     )
     for block in range(4):
-        grad_pair[pl.ds(block // 2 * 256 + block % 2, 128, stride=2), :] = results[block]
-        if block % 2:
-            half = pl.ds(block // 2 * 256, 256)
-            copies.append(
-                pltpu.make_async_copy(
-                    grad_pair.at[half], grad_far.at[half], sems.at[1 + block // 2]
-                )
-            )
-            copies[-1].start()
+        order[pl.ds(block // 2 * 256 + block % 2, 128, stride=2), :] = results[block]
+    grad_pair[...] = order[0:512, :]
     weights, total = add_sums(values, 8)
     grad_weight[...] = weights * (1.0 / 256)
     loss[0] = total[0, 0] * (1.0 / 65536)
-    for copy in copies:
-        copy.wait()
 
 
 def run(kernel, outs, scratch, args, **specs):
@@ -352,9 +341,8 @@
 
 def last(*args):
     outs = [((64, 128), F32), ((1,), F32), ((512, 128), F32), ((512, 128), BF16)]
-    scratch = [((128, 128), F32), ((520, 128), F32), ((520, 128), F32), ((512, 128), BF16)]
-    scratch += [pltpu.SemaphoreType.DMA((3,))]
-    specs = {"in_specs": [VMEM] * 3 + [SMEM, VMEM], "out_specs": [VMEM, SMEM, FAR, FAR]}
+    scratch = [((128, 128), F32), ((520, 128), F32), ((520, 128), F32)]
+    specs = {"in_specs": [VMEM] * 3 + [SMEM, VMEM], "out_specs": [VMEM, SMEM, VMEM, VMEM]}
     return run(last_kernel, outs, scratch, args, **specs)
 
 

time: 102 us -> 101 us (level)
  no operation moved by 1% of the time
where the time goes in v9:
time: 101 us
  blocking collectives  95.8 us (95%)
  Pallas kernels  4.35 us (4%)
    all_to_all x4, blocking collectives, exchange(): return lax.all_to_all(values, axes, 0, 0, tiled=True)  95.8 us
    pallas_call x5, Pallas kernels, run(): pl.pallas_call(kernel, out_shape=shapes, scratch_shapes=scratch, compiler...  4.35 us

profile of v9, /device:TPU:32, one launch (start us, length us, event | category | flops | bytes accessed | tf_op | source)
XLA Modules:
  0.0 100.8 jit_solution(7643993869396138562)
XLA Ops:
  0.6 1.8 %shard_map.156 = (bf16[1280,128]{1,0:T(8,128)(2,1)S(1)}, f32[256,128]{1,0:T(8,128)S(1)}, f32[512,128]{1,0:T(8,128)S(1)}, f32[512,128]{1,0:T(8,128)S(1)}, f32[24,...) custom-call(s32[1]{0:T(128)} %bitcast.place, s32[2,256]{1,0:T(2,128)} %refs_0_.1, s32[2,256]{1,0:T(2,128)} %refs_1_.1, ...), custom_call_target="tpu_custom_call" | custom-call | flops 10000000 | bytes 351492 | tf_op jit(solution)/shard_map/pallas_call | solution.py:297
  2.5 41.6 %all_to_all.20 = bf16[128,5,2,128]{3,2,1,0:T(2,128)(2,1)S(1)} all-to-all(bf16[128,5,2,128]{3,2,1,0:T(2,128)(2,1)S(1)} %bitcast.26), channel_id=1, replica_groups=mesh['zhi'=2,'core'=2,'y'=4,'zlo'=8,'x'=4] {'y','zlo','x'}, dimensions={0} | all-to-all | bytes 655360 | tf_op jit(solution)/shard_map/all_to_all | solution.py:350
  44.1 0.4 shard_map.157
  44.5 25.5 %all_to_all.21 = bf16[128,3,2,128]{3,2,1,0:T(2,128)(2,1)S(1)} all-to-all(bf16[128,3,2,128]{3,2,1,0:T(2,128)(2,1)S(1)} %bitcast.27), channel_id=1, replica_groups=mesh['zhi'=2,'core'=2,'y'=4,'zlo'=8,'x'=4] {'y','zlo','x'}, dimensions={0} | all-to-all | bytes 393216 | tf_op jit(solution)/shard_map/all_to_all | solution.py:350
  70.0 1.0 shard_map.158
  71.0 12.4 %all_to_all.22 = bf16[16,80,128]{2,1,0:T(8,128)(2,1)S(1)} all-to-all(bf16[16,80,128]{2,1,0:T(8,128)(2,1)S(1)} %bitcast.25), channel_id=1, replica_groups=mesh['zhi'=2,'core'=2,'y'=4,'zlo'=8,'x'=4] {'y','x'}, dimensions={0} | all-to-all | bytes 655360 | tf_op jit(solution)/shard_map/all_to_all | solution.py:350
  83.4 0.1 shard_map.159
  83.6 16.2 %all_to_all.23 = bf16[8,88,128]{2,1,0:T(8,128)(2,1)S(1)} all-to-all(bf16[8,88,128]{2,1,0:T(8,128)(2,1)S(1)} %bitcast.24), channel_id=1, replica_groups=mesh['zhi'=2,'core'=2,'y'=4,'zlo'=8,'x'=4] {'zlo'}, dimensions={0} | all-to-all | bytes 360448 | tf_op jit(solution)/shard_map/all_to_all | solution.py:350
  99.7 1.0 %shard_map.160 = (f32[64,128]{1,0:T(8,128)}, f32[1]{0:T(128)}, f32[512,128]{1,0:T(8,128)}, bf16[512,128]{1,0:T(8,128)(2,1)}) custom-call(bf16[704,128]{1,0:T(8,128)(2,1)S(1)} %bitcast.23, bf16[512,128]{1,0:T(8,128)(2,1)S(1)} %get-tuple-element.30.updated, f32[192,128]{1,0:T(8,128)S(1)} %get-tuple-element.31.grad, s32[1]{0:T(128)} %bitcast.place, ...), custom_call_target="tpu_custom_call" | custom-call | flops 10000000 | bytes 491524 | tf_op jit(solution)/shard_map/pallas_call | solution.py:297

commit v10 on v9

--- a/solution.py
+++ b/solution.py
@@ -26,6 +26,10 @@
     return (values - center) * lax.rsqrt(spread + 1e-05) * gain + bias
 
 
+def sigmoid(values):
+    return 0.5 * jnp.tanh(0.5 * values) + 0.5
+
+
 def picker(parity):
     rows = lax.broadcasted_iota(jnp.int32, (128, 256), 0)
     columns = lax.broadcasted_iota(jnp.int32, (128, 256), 1)
@@ -38,8 +42,8 @@
     targets, mask, chain, pair, gain, bias, out_gain, out_bias, dist_bias = near[:9]
     in_weight, gate_weight, out_weight, dist_weight = near[9:]
     copies = [pltpu.make_async_copy(far[n], near[n], sems.at[n]) for n in range(13)]
-    for copy in copies:
-        copy.start()
+    for n in (3, 9, 0, 1, 2, 4, 5, 6, 7, 8, 10, 11, 12):
+        copies[n].start()
     lower = lax.broadcasted_iota(jnp.int32, (128, 128), 0) * 2 <= place[0]
     pickers = picker(0), picker(1)
     for copy in copies[:3]:
@@ -90,8 +94,20 @@
     )
     rows[pl.ds(8, 128, stride=10), :] = jnp.where(lower, first, second)
     rows[pl.ds(9, 128, stride=10), :] = jnp.where(lower, second, third)
-    for copy in copies[4:]:
-        copy.wait()
+    for n in (4, 5, 9):
+        copies[n].wait()
+    normed = norm_lanes(flat[0:512, :], gain[...], bias[...]).astype(BF16)
+    proj = dot(in_weight[...], normed, TT)
+    for n in range(4):
+        r, half = n // 2, n % 2
+        at = slice(n * 128, (n + 1) * 128)
+        here = sigmoid(proj[256:, at]) * maskf[r : r + 1, half * 128 : (half + 1) * 128]
+        here = proj[:256, at] * here
+        for side in range(2):
+            rows[pl.ds(side * 4 + n, 128, stride=10), :] = here[side * 128 : (side + 1) * 128]
+    send[...] = rows[0:1280, :].astype(BF16)
+    for n in (6, 7, 8, 10, 11, 12):
+        copies[n].wait()
     marks[16:17, :] = out_gain[...]
     marks[17:18, :] = out_bias[...]
     marks[18:19, :64] = dist_bias[...]
@@ -100,17 +116,7 @@
     heavy[0:128, :] = gate_weight[...]
     heavy[128:256, :] = out_weight[...]
     heavy[256:320, :] = dist_weight[...]
-    normed = norm_lanes(flat[0:512, :], gain[...], bias[...]).astype(BF16)
-    proj = dot(in_weight[...], normed, TT)
-    for n in range(4):
-        r, half = n // 2, n % 2
-        at = slice(n * 128, (n + 1) * 128)
-        here = jax.nn.sigmoid(proj[256:, at]) * maskf[r : r + 1, half * 128 : (half + 1) * 128]
-        here = proj[:256, at] * here
-        for side in range(2):
-            rows[pl.ds(side * 4 + n, 128, stride=10), :] = here[side * 128 : (side + 1) * 128]
-    send[...] = rows[0:1280, :].astype(BF16)
-    flat[0:512, :] = jax.nn.sigmoid(dot(normed, gate_weight[...], NN))
+    flat[0:512, :] = sigmoid(dot(normed, gate_weight[...], NN))
     for block in range(4):
         gate[block * 128 : (block + 1) * 128, :] = flat[
             pl.ds(block // 2 * 256 + block % 2, 128, stride=2), :
@@ -149,7 +155,7 @@
     base[0:128, :] = rows[pl.ds(8, 128, stride=10), :]
     base[128:256, :] = rows[pl.ds(9, 128, stride=10), :]
     normed = norm_lanes(base[...], marks[19:20, :], marks[20:21, :]).astype(BF16)
-    gate[...] = jax.nn.sigmoid(dot(normed, heavy[0:128, :], NN))
+    gate[...] = sigmoid(dot(normed, heavy[0:128, :], NN))
 
 
 def message(weights, loss, others):
@@ -217,7 +223,7 @@
         powers = jnp.exp(shifted)
         norms = jnp.sum(powers, axis=0, keepdims=True)
         log_probs = shifted - jnp.log(norms)
-        probs = powers / norms
+        probs = powers * (1.0 / norms)
         onehot = (bins == row(6 + group)).astype(F32)
         onehot_back = (bins == labels[group]).astype(F32)
         losses = losses - row(group) * jnp.sum(onehot * log_probs, axis=0, keepdims=True)

time: 101 us -> 101 us (level)
  no operation moved by 1% of the time
where the time goes in v10:
time: 101 us
  blocking collectives  95.8 us (95%)
  Pallas kernels  4.6 us (5%)
    all_to_all x4, blocking collectives, exchange(): return lax.all_to_all(values, axes, 0, 0, tiled=True)  95.8 us
    pallas_call x5, Pallas kernels, run(): pl.pallas_call(kernel, out_shape=shapes, scratch_shapes=scratch, compiler...  4.6 us

profile of v10, /device:TPU:32, one launch (start us, length us, event | category | flops | bytes accessed | tf_op | source)
XLA Modules:
  0.0 101.0 jit_solution(8608012722645221385)
XLA Ops:
  0.6 2.1 %shard_map.156 = (bf16[1280,128]{1,0:T(8,128)(2,1)S(1)}, f32[256,128]{1,0:T(8,128)S(1)}, f32[512,128]{1,0:T(8,128)S(1)}, f32[512,128]{1,0:T(8,128)S(1)}, f32[24,...) custom-call(s32[1]{0:T(128)} %bitcast.place, s32[2,256]{1,0:T(2,128)} %refs_0_.1, s32[2,256]{1,0:T(2,128)} %refs_1_.1, ...), custom_call_target="tpu_custom_call" | custom-call | flops 10000000 | bytes 351492 | tf_op jit(solution)/shard_map/pallas_call | solution.py:303
  2.7 41.6 %all_to_all.20 = bf16[128,5,2,128]{3,2,1,0:T(2,128)(2,1)S(1)} all-to-all(bf16[128,5,2,128]{3,2,1,0:T(2,128)(2,1)S(1)} %bitcast.26), channel_id=1, replica_groups=mesh['zhi'=2,'core'=2,'y'=4,'zlo'=8,'x'=4] {'y','zlo','x'}, dimensions={0} | all-to-all | bytes 655360 | tf_op jit(solution)/shard_map/all_to_all | solution.py:356
  44.4 0.4 shard_map.157
  44.8 25.5 %all_to_all.21 = bf16[128,3,2,128]{3,2,1,0:T(2,128)(2,1)S(1)} all-to-all(bf16[128,3,2,128]{3,2,1,0:T(2,128)(2,1)S(1)} %bitcast.27), channel_id=1, replica_groups=mesh['zhi'=2,'core'=2,'y'=4,'zlo'=8,'x'=4] {'y','zlo','x'}, dimensions={0} | all-to-all | bytes 393216 | tf_op jit(solution)/shard_map/all_to_all | solution.py:356
  70.3 1.0 shard_map.158
  71.3 12.4 %all_to_all.22 = bf16[16,80,128]{2,1,0:T(8,128)(2,1)S(1)} all-to-all(bf16[16,80,128]{2,1,0:T(8,128)(2,1)S(1)} %bitcast.25), channel_id=1, replica_groups=mesh['zhi'=2,'core'=2,'y'=4,'zlo'=8,'x'=4] {'y','x'}, dimensions={0} | all-to-all | bytes 655360 | tf_op jit(solution)/shard_map/all_to_all | solution.py:356
  83.7 0.1 shard_map.159
  83.8 16.2 %all_to_all.23 = bf16[8,88,128]{2,1,0:T(8,128)(2,1)S(1)} all-to-all(bf16[8,88,128]{2,1,0:T(8,128)(2,1)S(1)} %bitcast.24), channel_id=1, replica_groups=mesh['zhi'=2,'core'=2,'y'=4,'zlo'=8,'x'=4] {'zlo'}, dimensions={0} | all-to-all | bytes 360448 | tf_op jit(solution)/shard_map/all_to_all | solution.py:356
  100.0 1.0 %shard_map.160 = (f32[64,128]{1,0:T(8,128)}, f32[1]{0:T(128)}, f32[512,128]{1,0:T(8,128)}, bf16[512,128]{1,0:T(8,128)(2,1)}) custom-call(bf16[704,128]{1,0:T(8,128)(2,1)S(1)} %bitcast.23, bf16[512,128]{1,0:T(8,128)(2,1)S(1)} %get-tuple-element.30.updated, f32[192,128]{1,0:T(8,128)S(1)} %get-tuple-element.31.grad, s32[1]{0:T(128)} %bitcast.place, ...), custom_call_target="tpu_custom_call" | custom-call | flops 10000000 | bytes 491524 | tf_op jit(solution)/shard_map/pallas_call | solution.py:303

commit v11 on v9

--- a/solution.py
+++ b/solution.py
@@ -153,16 +153,18 @@
 
 
 def message(weights, loss, others):
-    row = lax.broadcasted_iota(jnp.int32, (8, 128), 0)
+    row = lax.broadcasted_iota(jnp.int32, (64, 128), 0)
+    lane = lax.broadcasted_iota(jnp.int32, (1, 128), 1)
     high = loss.astype(BF16).astype(F32)
-    terms = jnp.where(row == 0, high, jnp.where(row == 1, loss - high, 0.0))
-    pieces = [piece for other in others for piece in (weights, terms, other)]
+    terms = jnp.where(lane == 0, high, jnp.where(lane == 1, loss - high, 0.0))
+    sums = jnp.where(row == 63, terms, weights)
+    pieces = [piece for other in others for piece in (sums, other)]
     return jnp.concatenate(pieces, axis=0).astype(BF16)
 
 
 def add_sums(values, peers):
-    sums = jnp.sum(values.reshape(peers, values.shape[0] // peers, 128), axis=0)
-    return sums[:64], sums[64:65, 0:1] + sums[65:66, 0:1]
+    sums = jnp.sum(values.reshape(peers, values.shape[0] // peers, 128)[:, :64], axis=0)
+    return sums, sums[63:64, 0:1] + sums[63:64, 1:2]
 
 
 def head_kernel(
@@ -245,7 +247,7 @@
 
 def middle_kernel(got, send, slopes):
     values = got[...].astype(F32)
-    slopes[0:128, :] = values.reshape(16, 80, 128)[:, 72:80].reshape(128, 128)
+    slopes[0:128, :] = values.reshape(16, 72, 128)[:, 64:72].reshape(128, 128)
     weights, loss = add_sums(values, 16)
     send[...] = message(weights, loss, [slopes[pl.ds(z, 16, stride=8), :] for z in range(8)])
 
@@ -269,7 +271,7 @@
     values = got[...].astype(F32)
     for z in range(8):
         for y in range(4):
-            at = z * 88 + 72 + y * 4
+            at = z * 80 + 64 + y * 4
             slopes[y * 32 + z * 4 : y * 32 + z * 4 + 4, :] = values[at : at + 4]
     there = slopes[...].astype(BF16)
     none = jnp.zeros((64, 128), BF16)
@@ -286,7 +288,10 @@
         order[pl.ds(block // 2 * 256 + block % 2, 128, stride=2), :] = results[block]
     grad_pair[...] = order[0:512, :]
     weights, total = add_sums(values, 8)
-    grad_weight[...] = weights * (1.0 / 256)
+    row = lax.broadcasted_iota(jnp.int32, (64, 128), 0)
+    weights = jnp.where(row == 63, 0.0, weights)
+    rest = jnp.sum(weights, axis=0, keepdims=True)
+    grad_weight[...] = jnp.where(row == 63, -rest, weights) * (1.0 / 256)
     loss[0] = total[0, 0] * (1.0 / 65536)
 
 
@@ -330,13 +335,13 @@
 
 
 def head(*args):
-    outs = [((512, 128), BF16), ((192, 128), F32), ((1280, 128), BF16)]
+    outs = [((512, 128), BF16), ((192, 128), F32), ((1152, 128), BF16)]
     scratch = [((784, 128), F32), ((136, 128), F32)]
     return run(head_kernel, outs, scratch, args, in_specs=[VMEM] * 6 + [SMEM] + [VMEM])
 
 
 def middle(got):
-    return run(middle_kernel, [((704, 128), BF16)], [((136, 128), F32)], (got,))[0]
+    return run(middle_kernel, [((640, 128), BF16)], [((136, 128), F32)], (got,))[0]
 
 
 def last(*args):
@@ -387,8 +392,8 @@
     products, back_base, back_gate = triangle(got, labels, marks, heavy)
     hidden = exchange(products.reshape(128, 3, 2, 128), GROUP).reshape(768, 128)
     updated, grad, total = head(hidden, base, gate, back_base, back_gate, marks, place, heavy)
-    total = middle(exchange(total.reshape(16, 80, 128), PLANE).reshape(1280, 128))
-    total = exchange(total.reshape(8, 88, 128), "zlo").reshape(704, 128)
+    total = middle(exchange(total.reshape(16, 72, 128), PLANE).reshape(1152, 128))
+    total = exchange(total.reshape(8, 80, 128), "zlo").reshape(640, 128)
     grad_weight, loss, grad_pair, pair_out = last(total, updated, grad, place, heavy)
     return (
         pair_out.reshape(2, 256, 128),

time: 101 us -> 101 us (level)
  the two profiles are of different devices: /device:TPU:32 before, /device:TPU:2 now
where the time goes in v11:
time: 101 us; the launch traced here: 100 us
  blocking collectives  95.2 us (94%)
  Pallas kernels  4.41 us (4%)
    all_to_all x4, blocking collectives, exchange(): return lax.all_to_all(values, axes, 0, 0, tiled=True)  95.2 us
    pallas_call x5, Pallas kernels, run(): pl.pallas_call(kernel, out_shape=shapes, scratch_shapes=scratch, compiler...  4.41 us

profile of v11, /device:TPU:2, one launch (start us, length us, event | category | flops | bytes accessed | tf_op | source)
XLA Modules:
  0.0 100.3 jit_solution(15733012057036638129)
XLA Ops:
  0.6 1.8 %shard_map.156 = (bf16[1280,128]{1,0:T(8,128)(2,1)S(1)}, f32[256,128]{1,0:T(8,128)S(1)}, f32[512,128]{1,0:T(8,128)S(1)}, f32[512,128]{1,0:T(8,128)S(1)}, f32[24,...) custom-call(s32[1]{0:T(128)} %bitcast.place, s32[2,256]{1,0:T(2,128)} %refs_0_.1, s32[2,256]{1,0:T(2,128)} %refs_1_.1, ...), custom_call_target="tpu_custom_call" | custom-call | flops 10000000 | bytes 351492 | tf_op jit(solution)/shard_map/pallas_call | solution.py:302
  2.5 42.6 %all_to_all.20 = bf16[128,5,2,128]{3,2,1,0:T(2,128)(2,1)S(1)} all-to-all(bf16[128,5,2,128]{3,2,1,0:T(2,128)(2,1)S(1)} %bitcast.25), channel_id=1, replica_groups=mesh['zhi'=2,'core'=2,'y'=4,'zlo'=8,'x'=4] {'y','zlo','x'}, dimensions={0} | all-to-all | bytes 655360 | tf_op jit(solution)/shard_map/all_to_all | solution.py:355
  45.1 0.4 shard_map.157
  45.4 25.3 %all_to_all.21 = bf16[128,3,2,128]{3,2,1,0:T(2,128)(2,1)S(1)} all-to-all(bf16[128,3,2,128]{3,2,1,0:T(2,128)(2,1)S(1)} %bitcast.27), channel_id=1, replica_groups=mesh['zhi'=2,'core'=2,'y'=4,'zlo'=8,'x'=4] {'y','zlo','x'}, dimensions={0} | all-to-all | bytes 393216 | tf_op jit(solution)/shard_map/all_to_all | solution.py:355
  70.8 1.0 shard_map.158
  71.8 11.8 %all_to_all.22 = bf16[16,72,128]{2,1,0:T(8,128)(2,1)S(1)} all-to-all(bf16[16,72,128]{2,1,0:T(8,128)(2,1)S(1)} %bitcast.26), channel_id=1, replica_groups=mesh['zhi'=2,'core'=2,'y'=4,'zlo'=8,'x'=4] {'y','x'}, dimensions={0} | all-to-all | bytes 589824 | tf_op jit(solution)/shard_map/all_to_all | solution.py:355
  83.6 0.2 shard_map.159
  83.8 15.5 %all_to_all.23 = bf16[8,80,128]{2,1,0:T(8,128)(2,1)S(1)} all-to-all(bf16[8,80,128]{2,1,0:T(8,128)(2,1)S(1)} %bitcast.23), channel_id=1, replica_groups=mesh['zhi'=2,'core'=2,'y'=4,'zlo'=8,'x'=4] {'zlo'}, dimensions={0} | all-to-all | bytes 327680 | tf_op jit(solution)/shard_map/all_to_all | solution.py:355
  99.3 1.0 %shard_map.160 = (f32[64,128]{1,0:T(8,128)}, f32[1]{0:T(128)}, f32[512,128]{1,0:T(8,128)}, bf16[512,128]{1,0:T(8,128)(2,1)}) custom-call(bf16[640,128]{1,0:T(8,128)(2,1)S(1)} %bitcast.24, bf16[512,128]{1,0:T(8,128)(2,1)S(1)} %get-tuple-element.30.updated, f32[192,128]{1,0:T(8,128)S(1)} %get-tuple-element.31.grad, s32[1]{0:T(128)} %bitcast.place, ...), custom_call_target="tpu_custom_call" | custom-call | flops 10000000 | bytes 475140 | tf_op jit(solution)/shard_map/pallas_call | solution.py:302

commit v12 on v11

--- a/solution.py
+++ b/solution.py
@@ -219,7 +219,7 @@
         powers = jnp.exp(shifted)
         norms = jnp.sum(powers, axis=0, keepdims=True)
         log_probs = shifted - jnp.log(norms)
-        probs = powers / norms
+        probs = powers * (1.0 / norms)
         onehot = (bins == row(6 + group)).astype(F32)
         onehot_back = (bins == labels[group]).astype(F32)
         losses = losses - row(group) * jnp.sum(onehot * log_probs, axis=0, keepdims=True)

time: 101 us -> 101 us (level)
  no operation moved by 1% of the time
where the time goes in v12:
time: 101 us; the launch traced here: 100 us
  blocking collectives  95.2 us (94%)
  Pallas kernels  4.41 us (4%)
    all_to_all x4, blocking collectives, exchange(): return lax.all_to_all(values, axes, 0, 0, tiled=True)  95.2 us
    pallas_call x5, Pallas kernels, run(): pl.pallas_call(kernel, out_shape=shapes, scratch_shapes=scratch, compiler...  4.41 us

profile of v12, /device:TPU:2, one launch (start us, length us, event | category | flops | bytes accessed | tf_op | source)
XLA Modules:
  0.0 100.3 jit_solution(15733012057036638129)
XLA Ops:
  0.6 1.8 %shard_map.156 = (bf16[1280,128]{1,0:T(8,128)(2,1)S(1)}, f32[256,128]{1,0:T(8,128)S(1)}, f32[512,128]{1,0:T(8,128)S(1)}, f32[512,128]{1,0:T(8,128)S(1)}, f32[24,...) custom-call(s32[1]{0:T(128)} %bitcast.place, s32[2,256]{1,0:T(2,128)} %refs_0_.1, s32[2,256]{1,0:T(2,128)} %refs_1_.1, ...), custom_call_target="tpu_custom_call" | custom-call | flops 10000000 | bytes 351492 | tf_op jit(solution)/shard_map/pallas_call | solution.py:302
  2.5 42.6 %all_to_all.20 = bf16[128,5,2,128]{3,2,1,0:T(2,128)(2,1)S(1)} all-to-all(bf16[128,5,2,128]{3,2,1,0:T(2,128)(2,1)S(1)} %bitcast.25), channel_id=1, replica_groups=mesh['zhi'=2,'core'=2,'y'=4,'zlo'=8,'x'=4] {'y','zlo','x'}, dimensions={0} | all-to-all | bytes 655360 | tf_op jit(solution)/shard_map/all_to_all | solution.py:355
  45.1 0.4 shard_map.157
  45.4 25.3 %all_to_all.21 = bf16[128,3,2,128]{3,2,1,0:T(2,128)(2,1)S(1)} all-to-all(bf16[128,3,2,128]{3,2,1,0:T(2,128)(2,1)S(1)} %bitcast.27), channel_id=1, replica_groups=mesh['zhi'=2,'core'=2,'y'=4,'zlo'=8,'x'=4] {'y','zlo','x'}, dimensions={0} | all-to-all | bytes 393216 | tf_op jit(solution)/shard_map/all_to_all | solution.py:355
  70.8 1.0 shard_map.158
  71.8 11.8 %all_to_all.22 = bf16[16,72,128]{2,1,0:T(8,128)(2,1)S(1)} all-to-all(bf16[16,72,128]{2,1,0:T(8,128)(2,1)S(1)} %bitcast.26), channel_id=1, replica_groups=mesh['zhi'=2,'core'=2,'y'=4,'zlo'=8,'x'=4] {'y','x'}, dimensions={0} | all-to-all | bytes 589824 | tf_op jit(solution)/shard_map/all_to_all | solution.py:355
  83.6 0.2 shard_map.159
  83.8 15.5 %all_to_all.23 = bf16[8,80,128]{2,1,0:T(8,128)(2,1)S(1)} all-to-all(bf16[8,80,128]{2,1,0:T(8,128)(2,1)S(1)} %bitcast.23), channel_id=1, replica_groups=mesh['zhi'=2,'core'=2,'y'=4,'zlo'=8,'x'=4] {'zlo'}, dimensions={0} | all-to-all | bytes 327680 | tf_op jit(solution)/shard_map/all_to_all | solution.py:355
  99.3 1.0 %shard_map.160 = (f32[64,128]{1,0:T(8,128)}, f32[1]{0:T(128)}, f32[512,128]{1,0:T(8,128)}, bf16[512,128]{1,0:T(8,128)(2,1)}) custom-call(bf16[640,128]{1,0:T(8,128)(2,1)S(1)} %bitcast.24, bf16[512,128]{1,0:T(8,128)(2,1)S(1)} %get-tuple-element.30.updated, f32[192,128]{1,0:T(8,128)S(1)} %get-tuple-element.31.grad, s32[1]{0:T(128)} %bitcast.place, ...), custom_call_target="tpu_custom_call" | custom-call | flops 10000000 | bytes 475140 | tf_op jit(solution)/shard_map/pallas_call | solution.py:302
